TPU v7x, 128 devices: a whole 4x4x4 slice. The times are simulated.
128 devices in a mesh: replica: 8 (over z_hi, x), fsdp: 16 (over z_lo, y, core).
Axes of the slice: x: 4, y: 4, z: 4 (z_hi: 2, z_lo: 2; z = z_hi * 2 + z_lo), core: 2. Of those that a mesh axis runs over, the one named last changes fastest.
Arguments:
- step: int32 [1], replicated, may hold values from 0 to 999
- hidden_in: bfloat16 [8, 2048, 3072], P('replica', 'fsdp'), may hold values from -6 to 6
- cotangent: bfloat16 [8, 2048, 3072], P('replica', 'fsdp'), may hold values from -6 to 6
- norm_gain: bfloat16 [3072], replicated, may hold values from 0.5 to 1.5
- weights: bfloat16 [8, 3, 3072, 4096], P('replica', None, None, 'fsdp'), may hold values from -0.109375 to 0.109375
- adam_m: float32 [8, 3072, 4096], P('replica', None, 'fsdp'), may hold values from -0.046875 to 0.046875
- adam_v: float32 [8, 3072, 4096], P('replica', None, 'fsdp'), may hold values from 1e-06 to 0.0001
- global_frag: float32 [3072, 4096], P(None, 'fsdp'), may hold values from -0.109375 to 0.109375
- outer_mom: float32 [3072, 4096], P(None, 'fsdp'), may hold values from -0.15625 to 0.15625
Outputs:
- global_new: float32 [3072, 4096], P(None, 'fsdp')
- momentum_new: float32 [3072, 4096], P(None, 'fsdp')
- merged: bfloat16 [8, 3072, 4096], P('replica', None, 'fsdp')
All inputs are finite; a program needn't handle non-finite values.
Results may differ from a plain program's by a relative error of at most 0.0047.
Values may be sent and summed in bfloat16 or wider, within the bound.
No kernel may reach another device: no remote copies, remote signals or barrier semaphores. Data moves between devices by JAX's collectives and lax.ppermute only.
A program may use at most 128 MiB of HBM per device.

v0:
```python
import jax
import jax.numpy as jnp
from jax import lax
from jax.sharding import PartitionSpec as P

beta_one = 0.9
beta_two = 0.95
adam_eps = 1e-08
inner_lr = 0.02
outer_lr = 0.7
nesterov_mu = 0.9
mix_alpha = 0.5
norm_eps = 1e-05


def nesterov(delta, global_part, mom_part):
    mom_next = nesterov_mu * mom_part + delta
    return (global_part - outer_lr * (delta + nesterov_mu * mom_next), mom_next)


def outer_update(local_delta, global_frag, outer_mom):
    replicas = lax.axis_size("replica")
    total = lax.psum(local_delta, "replica")
    return nesterov(total / replicas, global_frag, outer_mom)


def per_device(
    step, hidden_in, cotangent, norm_gain, weights, adam_m, adam_v, global_frag, outer_mom
):
    fragment = step[0] % 3
    w_all = weights[0]
    w_plain = lax.dynamic_index_in_dim(w_all, fragment, 0, keepdims=False)
    w_frag = w_plain.astype(jnp.float32)
    local_delta = global_frag - w_frag
    x_float = hidden_in[0].astype(jnp.float32)
    scale_rows = lax.rsqrt(jnp.mean(x_float * x_float, axis=1, keepdims=True) + norm_eps)
    normed = (x_float * scale_rows * norm_gain.astype(jnp.float32)).astype(jnp.bfloat16)
    tokens_total = hidden_in.shape[1] * lax.axis_size("fsdp")
    normed_rows = lax.all_gather(normed, "fsdp", axis=0, tiled=True)
    cotan_rows = lax.all_gather(cotangent[0], "fsdp", axis=0, tiled=True)
    gate = jnp.dot(normed_rows, w_all[0], preferred_element_type=jnp.float32)
    up_val = jnp.dot(normed_rows, w_all[1], preferred_element_type=jnp.float32)
    gate_sig = jax.nn.sigmoid(gate)
    activated = gate * gate_sig
    hidden = (activated * up_val).astype(jnp.bfloat16)
    d_hidden = jnp.dot(cotan_rows, w_all[2], preferred_element_type=jnp.float32)
    d_gate = (d_hidden * up_val * gate_sig * (1.0 + gate * (1.0 - gate_sig))).astype(jnp.bfloat16)
    d_up = (d_hidden * activated).astype(jnp.bfloat16)
    left = jnp.where(fragment == 2, cotan_rows, normed_rows)
    right = jnp.where(fragment == 0, d_gate, jnp.where(fragment == 1, d_up, hidden))
    summed = lax.dot_general(
        left, right, (((0,), (0,)), ((), ())), preferred_element_type=jnp.float32
    )
    grad = summed / tokens_total
    global_new, momentum_new = outer_update(local_delta, global_frag, outer_mom)
    moment_one = beta_one * adam_m[0] + (1.0 - beta_one) * grad
    moment_two = beta_two * adam_v[0] + (1.0 - beta_two) * grad * grad
    w_inner = w_frag - inner_lr * moment_one / (jnp.sqrt(moment_two) + adam_eps)
    merged = (mix_alpha * w_inner + (1.0 - mix_alpha) * global_new).astype(jnp.bfloat16)
    return (global_new, momentum_new, merged[None])


def solution(mesh):
    placed = (
        P(),
        P("replica", "fsdp", None),
        P("replica", "fsdp", None),
        P(),
        P("replica", None, None, "fsdp"),
        P("replica", None, "fsdp"),
        P("replica", None, "fsdp"),
        P(None, "fsdp"),
        P(None, "fsdp"),
    )
    return jax.shard_map(
        per_device,
        mesh=mesh,
        in_specs=placed,
        out_specs=(P(None, "fsdp"), P(None, "fsdp"), P("replica", None, "fsdp")),
        check_vma=False,
    )
```

profile of v0, /device:TPU:1, one launch (start us, length us, event | category | flops | bytes accessed | tf_op | source)
XLA Modules:
  0.0 265.2 jit_solution(944280981521393416)
XLA Ops:
  8.0 0.0 all-reduce.2.cloned.1.call-start
  8.7 4.3 %convert_subtract_fusion.1 = f32[3072,256]{1,0:T(8,128)} fusion(f32[3072,256]{1,0:T(8,128)} %param.16, bf16[1,3,3072,256]{3,2,1,0:T(8,128)(2,1)} %param.13, s32[]{:T(128)S(6)} %select_n.34), kind=kLoop, calls=%fused_computation.6 | loop fusion | flops 1572864 | bytes 7864324 | tf_op jit(solution)/shard_map/sub | solution.py:34
  13.0 0.0 copy-start.2
  13.0 0.0 copy-start
  13.0 0.0 all-reduce.2.cloned.1.call-update
  13.1 0.0 all-gather.6.cloned.1.call-start
  13.1 0.5 all-gather.6.cloned.1.call-update
  13.6 0.0 all-gather.4.cloned.1.call-start
  13.7 0.0 copy-done.2
  13.7 1.6 fusion.12
  15.4 2.3 fusion.14
  17.7 0.0 all-gather.4.cloned.1.call-update
  17.7 94.8 %all-reduce.2.cloned.1.call-done = f32[3072,256]{1,0:T(8,128)} async-done(((f32[3072,256]{1,0:T(8,128)}), f32[3072,256]{1,0:T(8,128)}) %all-reduce.2.cloned.1.call-update) | async-done | bytes 3145744 | tf_op jit(solution)/shard_map/psum | solution.py:23
  112.5 0.0 copy-done
  112.5 6.5 %multiply_subtract_fusion = (f32[3072,256]{1,0:T(8,128)}, f32[3072,256]{1,0:T(8,128)}) fusion(f32[3072,256]{1,0:T(8,128)S(1)} %copy-done, f32[3072,256]{1,0:T(8,128)} %all-reduce.2.cloned.1.call-done, f32[3072,256]{1,0:T(8,128)} %param.17), kind=kLoop, calls=%fused_computation.16 | loop fusion | flops 5505024 | bytes 15728640 | tf_op jit(solution)/shard_map/sub | solution.py:18
  119.0 30.2 %all-gather.6.cloned.1.call-done = bf16[1,2048,3072]{2,1,0:T(8,128)(2,1)} async-done(((bf16[1,128,3072]{2,1,0:T(8,128)(2,1)}), bf16[1,2048,3072]{2,1,0:T(8,128)(2,1)}) %all-gather.6.cloned.1.call-update) | async-done | bytes 12582928 | tf_op jit(solution)/shard_map/all_gather | solution.py:40
  149.3 9.8 %fusion = f32[2048,256]{1,0:T(8,128)} fusion(bf16[1,2048,3072]{2,1,0:T(8,128)(2,1)} %all-gather.6.cloned.1.call-done, bf16[1,3,3072,256]{3,2,1,0:T(8,128)(2,1)} %param.13), kind=kOutput, calls=%fused_computation | convolution fusion | flops 3221225472 | bytes 16252928 | tf_op jit(solution)/shard_map/dot_general | solution.py:46
  159.1 0.0 copy-start.1
  159.1 62.4 %all-gather.4.cloned.1.call-done = bf16[2048,3072]{1,0:T(8,128)(2,1)} async-done(((bf16[128,3072]{1,0:T(8,128)(2,1)}), bf16[2048,3072]{1,0:T(8,128)(2,1)}) %all-gather.4.cloned.1.call-update) | async-done | bytes 12582928 | tf_op jit(solution)/shard_map/all_gather | solution.py:39
  221.5 9.8 %fusion.15 = f32[2048,256]{1,0:T(8,128)} fusion(bf16[2048,3072]{1,0:T(8,128)(2,1)} %all-gather.4.cloned.1.call-done, bf16[1,3,3072,256]{3,2,1,0:T(8,128)(2,1)} %param.13), kind=kOutput, calls=%fused_computation.28 | convolution fusion | flops 3221225472 | bytes 16252928 | tf_op jit(solution)/shard_map/dot_general | solution.py:41
  231.2 0.0 copy-done.1
  231.2 26.5 %fusion.23 = bf16[1,3072,256]{2,1,0:T(8,128)(2,1)} fusion(f32[3072,256]{1,0:T(8,128)S(1)} %copy-done.1, f32[1,3072,256]{2,1,0:T(8,128)} %param.15, f32[1,3072,256]{2,1,0:T(8,128)} %param.14, bf16[1,3,3072,256]{3,2,1,0:T(8,128)(2,1)} %param.13, s32[]{:T(128)S(6)} %select_n.34, f32[2048,256]{1,0:T(8,128)} %fusion, ...), kind=kOutput, calls=%fused_computation.36 | convolution fusion | flops 6470238208 | bytes 56098824 | tf_op jit(solution)/shard_map/dot_general | solution.py:51
  (2 shorter events, 0.0 us)
Async XLA Ops:
  8.0 104.5 %all-reduce.2.cloned.1.call-start = ((), (), s32[]{:S(2)}) async-start(), calls=%async_computation | async-start | bytes 6291456 | tf_op jit(solution)/shard_map/psum | solution.py:23
  13.0 0.7 copy-start.2
  13.0 99.5 %copy-start = (f32[3072,256]{1,0:T(8,128)S(1)}, f32[3072,256]{1,0:T(8,128)}, u32[]{:S(2)}) copy-start(f32[3072,256]{1,0:T(8,128)} %param.16) | copy-start | bytes 9437188
  13.1 136.2 %all-gather.6.cloned.1.call-start = ((), (), s32[]{:S(2)}) async-start(), calls=%async_computation.2 | async-start | bytes 13369344 | tf_op jit(solution)/shard_map/all_gather | solution.py:40
  13.6 207.8 %all-gather.4.cloned.1.call-start = ((), (), s32[]{:S(2)}) async-start(), calls=%async_computation.1 | async-start | bytes 13369344 | tf_op jit(solution)/shard_map/all_gather | solution.py:39
  159.1 72.2 %copy-start.1 = (f32[3072,256]{1,0:T(8,128)S(1)}, f32[3072,256]{1,0:T(8,128)}, u32[]{:S(2)}) copy-start(f32[3072,256]{1,0:T(8,128)} %get-tuple-element.3) | copy-start | bytes 9437188
Sparse Core Ops, SparseCore 0:
  13.2 99.2 all-reduce.1
Sparse Core Ops, SparseCore 1:
  15.2 134.0 all-gather.5
  151.4 70.0 all-gather.3
where the time goes:
time: 267 us; the launch traced here: 265 us
  waiting for transfers between devices  188 us (70%)
  matrix products  46.1 us (17%)
  between operations  16.2 us (6%)
  other arithmetic  14.7 us (6%)
    psum x1, waiting for transfers between devices, outer_update(): total = lax.psum(local_delta, 'replica')  94.8 us
    all_gather x1, waiting for transfers between devices, per_device(): normed_rows = lax.all_gather(normed, 'fsdp', axis=0, tiled=True)  62.4 us
    all_gather x1, waiting for transfers between devices, per_device(): cotan_rows = lax.all_gather(cotangent[0], 'fsdp', axis=0, tiled=True)  30.2 us
    dot_general x1, matrix products, per_device(): lax.dot_general(left, right, (((0,), (0,)), ((), ())), preferred_element_...  26.5 us
    dot_general x1, matrix products, per_device(): d_hidden = jnp.dot(cotan_rows, w_all[2], preferred_element_type=jnp.float32)  9.8 us
    dot_general x1, matrix products, per_device(): gate = jnp.dot(normed_rows, w_all[0], preferred_element_type=jnp.float32)  9.78 us
    sub x1, other arithmetic, nesterov(): return (global_part - outer_lr * (delta + nesterov_mu * mom_next), mom_next)  6.48 us
  transfers between devices with their start and end apart: 3, of which 3 were waited for; matrix products, arithmetic and copies ran while one was open for 8% of the time, Pallas kernels for 0%

commit v1 on v0

v1 whole, which is shorter than its diff:
```python
import functools

import jax
import jax.numpy as jnp
from jax import lax
from jax.experimental import pallas as pl
from jax.experimental.pallas import tpu as pltpu
from jax.sharding import PartitionSpec as P

beta_one = 0.9
beta_two = 0.95
adam_eps = 1e-08
inner_lr = 0.02
outer_lr = 0.7
nesterov_mu = 0.9
mix_alpha = 0.5
norm_eps = 1e-05

WIRE_SCALE = float(2**18)

ANY = pl.BlockSpec(memory_space=pl.ANY)
VMEM = pl.BlockSpec(memory_space=pltpu.VMEM)
SMEM = pl.BlockSpec(memory_space=pltpu.SMEM)
MIB = 1024 * 1024


def fsdp_id(z, y, c):
    return (z % 2) * 8 + (y % 4) * 2 + c


def permutation(to):
    return [(fsdp_id(z, y, c), fsdp_id(*to(z, y, c))) for z in range(2) for y in range(4) for c in range(2)]


STRAIGHT = permutation(lambda z, y, c: (z, y + 1 - 2 * c, c))
CROSSED = permutation(lambda z, y, c: (z, y + 2 * c - 1, 1 - c))
OTHER_Z = permutation(lambda z, y, c: (z + 1, y, c))
SIBLING = permutation(lambda z, y, c: (z, y, 1 - c))


def replica_shift(k):
    return [(h * 4 + x, h * 4 + (x + k) % 4) for h in range(2) for x in range(4)]


OTHER_H = [(r, (r + 4) % 8) for r in range(8)]


def norm_kernel(x_ref, c_ref, g_ref, u_ref):
    rows = x_ref.shape[0]
    x = x_ref[...].astype(jnp.float32)
    scale = lax.rsqrt(jnp.mean(x * x, axis=1, keepdims=True) + norm_eps)
    u_ref[pl.ds(0, rows), :] = (x * scale * g_ref[...].astype(jnp.float32)).astype(jnp.bfloat16)
    u_ref[pl.ds(rows, rows), :] = c_ref[...]


def normed_and_cotangent(x, c, gain):
    rows, d = x.shape
    return pl.pallas_call(
        norm_kernel,
        out_shape=jax.ShapeDtypeStruct((2 * rows, d), jnp.bfloat16),
        in_specs=[VMEM, VMEM, VMEM],
        out_specs=VMEM,
        compiler_params=pltpu.CompilerParams(vmem_limit_bytes=16 * MIB),
        name="norm",
    )(x, c, gain.reshape(1, d))


def forward_kernel(count, frag_ref, *refs):
    blocks = refs[:count]
    w_own, w_sib, right_ref = refs[count : count + 3]
    n_s, c_s, w_s, gate_s, up_s, dh_s, sems = refs[count + 3 :]
    rows = blocks[0].shape[0] // 2
    cols = w_own.shape[2]
    frag = frag_ref[0]
    copies = []
    for k, block in enumerate(blocks):
        copies.append(pltpu.make_async_copy(block.at[pl.ds(0, rows)], n_s.at[pl.ds(k * rows, rows)], sems.at[2 * k]))
        copies.append(pltpu.make_async_copy(block.at[pl.ds(rows, rows)], c_s.at[pl.ds(k * rows, rows)], sems.at[2 * k + 1]))
    weights = [
        pltpu.make_async_copy(w.at[m], w_s.at[3 * h + m], sems.at[2 * count + 3 * h + m])
        for h, w in enumerate((w_own, w_sib))
        for m in range(3)
    ]
    for copy in copies + weights:
        copy.start()
    for copy in copies:
        copy.wait()
    for h in range(2):
        for m, (left, out) in enumerate(((n_s, gate_s), (n_s, up_s), (c_s, dh_s))):
            weights[3 * h + m].wait()
            out[...] = jnp.dot(left[...], w_s[3 * h + m], preferred_element_type=jnp.float32)
        gate = gate_s[...]
        sig = jax.nn.sigmoid(gate)
        at = right_ref.at[:, pl.ds(h * cols, cols)]

        @pl.when(frag == 0)
        def _():
            at[...] = (dh_s[...] * up_s[...] * sig * (1.0 + gate * (1.0 - sig))).astype(jnp.bfloat16)

        @pl.when(frag == 1)
        def _():
            at[...] = (dh_s[...] * (gate * sig)).astype(jnp.bfloat16)

        @pl.when(frag == 2)
        def _():
            at[...] = (gate * sig * up_s[...]).astype(jnp.bfloat16)


def forward(frag, blocks, w_own, w_sib):
    count = len(blocks)
    rows = count * blocks[0].shape[0] // 2
    _, d, cols = w_own.shape
    return pl.pallas_call(
        functools.partial(forward_kernel, count),
        out_shape=jax.ShapeDtypeStruct((rows, 2 * cols), jnp.bfloat16),
        in_specs=[SMEM] + [ANY] * (count + 2),
        out_specs=VMEM,
        scratch_shapes=[
            pltpu.VMEM((rows, d), jnp.bfloat16),
            pltpu.VMEM((rows, d), jnp.bfloat16),
            pltpu.VMEM((6, d, cols), jnp.bfloat16),
            pltpu.VMEM((rows, cols), jnp.float32),
            pltpu.VMEM((rows, cols), jnp.float32),
            pltpu.VMEM((rows, cols), jnp.float32),
            pltpu.SemaphoreType.DMA((2 * count + 6,)),
        ],
        compiler_params=pltpu.CompilerParams(vmem_limit_bytes=32 * MIB),
        cost_estimate=pl.CostEstimate(flops=12 * rows * d * cols, bytes_accessed=12 * d * cols + 4 * rows * d, transcendentals=0),
        name="forward",
    )(frag, *blocks, w_own, w_sib)


def grad_kernel(count, spans, chunk, frag_ref, *refs):
    blocks = refs[:count]
    rights = refs[count : count + len(spans)]
    sib_ref, own_ref, left_s, right_s, sems = refs[count + len(spans) :]
    rows = blocks[0].shape[0] // 2
    cols = own_ref.shape[1]
    start = jnp.where(frag_ref[0] == 2, rows, 0)
    start = pl.multiple_of(start, rows)
    copies = [
        pltpu.make_async_copy(block.at[pl.ds(start, rows)], left_s.at[pl.ds(k * rows, rows)], sems.at[k])
        for k, block in enumerate(blocks)
    ]
    copies += [
        pltpu.make_async_copy(r, right_s.at[pl.ds(at, size)], sems.at[count + j])
        for j, (r, (at, size)) in enumerate(zip(rights, spans))
    ]
    for copy in copies:
        copy.start()
    for copy in copies:
        copy.wait()
    for out, at in ((sib_ref, cols), (own_ref, 0)):

        @pl.loop(0, left_s.shape[1] // chunk)
        def _(j):
            span = pl.ds(pl.multiple_of(j * chunk, chunk), chunk)
            out[span, :] = lax.dot_general(
                left_s[:, span], right_s[:, pl.ds(at, cols)], (((0,), (0,)), ((), ())), preferred_element_type=jnp.float32
            ).astype(out.dtype)


def partial_grads(frag, blocks, rights):
    count = len(blocks)
    rows, d = blocks[0].shape
    rows //= 2
    cols = rights[0].shape[1] // 2
    spans, at = [], 0
    for r in rights:
        spans.append((at, r.shape[0]))
        at += r.shape[0]
    return pl.pallas_call(
        functools.partial(grad_kernel, count, tuple(spans), 256),
        out_shape=(jax.ShapeDtypeStruct((d, cols), jnp.bfloat16), jax.ShapeDtypeStruct((d, cols), jnp.float32)),
        in_specs=[SMEM] + [ANY] * (count + len(rights)),
        out_specs=(VMEM, VMEM),
        scratch_shapes=[
            pltpu.VMEM((at, d), jnp.bfloat16),
            pltpu.VMEM((at, 2 * cols), jnp.bfloat16),
            pltpu.SemaphoreType.DMA((count + len(rights),)),
        ],
        compiler_params=pltpu.CompilerParams(vmem_limit_bytes=32 * MIB),
        cost_estimate=pl.CostEstimate(flops=4 * at * d * cols, bytes_accessed=2 * at * d + 6 * d * cols, transcendentals=0),
        name="grad",
    )(frag, *blocks, *rights)


def replica_delta(w_frag, global_frag):
    x = lax.rem(lax.axis_index("replica"), 4)
    d, cols = w_frag.shape
    quarters = w_frag.reshape(4, d // 4, cols)

    def quarter(k):
        return lax.dynamic_index_in_dim(quarters, lax.rem(x + k, 4), 0, keepdims=False)

    got = [quarter(0)] + [lax.ppermute(quarter(k), "replica", replica_shift(k)) for k in (1, 2, 3)]
    base = lax.dynamic_index_in_dim(global_frag.reshape(4, d // 4, cols), x, 0, keepdims=False)
    part = sum(base - w.astype(jnp.float32) for w in got)
    part = (part * (WIRE_SCALE / 8)).astype(jnp.float16)
    other = lax.ppermute(part, "replica", OTHER_H)
    mine = (part.astype(jnp.float32) + other.astype(jnp.float32)).astype(jnp.float16)
    slots = [mine] + [lax.ppermute(mine, "replica", replica_shift(k)) for k in (1, 2, 3)]
    twice = jnp.stack([slots[(-j) % 4] for j in range(8)])
    return lax.dynamic_slice_in_dim(twice, lax.rem(4 - x, 4), 4, 0).reshape(d, cols)


def per_device(step, hidden_in, cotangent, norm_gain, weights, adam_m, adam_v, global_frag, outer_mom):
    fragment = step[0] % 3
    frag = fragment.reshape(1)
    w_own = weights[0]
    w_sib = lax.ppermute(w_own, "fsdp", SIBLING)
    own = normed_and_cotangent(hidden_in[0], cotangent[0], norm_gain)

    straight = functools.partial(lax.ppermute, axis_name="fsdp", perm=STRAIGHT)
    crossed = functools.partial(lax.ppermute, axis_name="fsdp", perm=CROSSED)
    other_z = functools.partial(lax.ppermute, axis_name="fsdp", perm=OTHER_Z)
    near = straight(own)
    cross = crossed(own)
    z_own = other_z(own)
    z_near = straight(z_own)
    far = straight(near)
    z_cross = other_z(cross)
    z_far = straight(z_near)

    w_frag = lax.dynamic_index_in_dim(w_own, fragment, 0, keepdims=False)
    delta = replica_delta(w_frag, global_frag).astype(jnp.float32) * (1 / WIRE_SCALE)
    momentum_new = nesterov_mu * outer_mom + delta
    global_new = global_frag - outer_lr * (delta + nesterov_mu * momentum_new)

    groups = ((own, near), (cross, z_own), (z_near, far), (z_cross, z_far))
    rights = [forward(frag, group, w_own, w_sib) for group in groups]
    grad_sib, grad_own = partial_grads(frag, sum(groups, ()), rights)
    tokens_total = hidden_in.shape[1] * lax.axis_size("fsdp")
    grad = (grad_own + lax.ppermute(grad_sib, "fsdp", SIBLING).astype(jnp.float32)) / tokens_total

    moment_one = beta_one * adam_m[0] + (1.0 - beta_one) * grad
    moment_two = beta_two * adam_v[0] + (1.0 - beta_two) * grad * grad
    w_inner = w_frag.astype(jnp.float32) - inner_lr * moment_one / (jnp.sqrt(moment_two) + adam_eps)
    merged = (mix_alpha * w_inner + (1.0 - mix_alpha) * global_new).astype(jnp.bfloat16)
    return (global_new, momentum_new, merged[None])


def solution(mesh):
    placed = (
        P(),
        P("replica", "fsdp", None),
        P("replica", "fsdp", None),
        P(),
        P("replica", None, None, "fsdp"),
        P("replica", None, "fsdp"),
        P("replica", None, "fsdp"),
        P(None, "fsdp"),
        P(None, "fsdp"),
    )
    return jax.shard_map(
        per_device,
        mesh=mesh,
        in_specs=placed,
        out_specs=(P(None, "fsdp"), P(None, "fsdp"), P("replica", None, "fsdp")),
        check_vma=False,
    )
```

time: 267 us -> 156 us (0.58)
  waiting for transfers between devices: 188 us -> 61.2 us
  matrix products: 46.1 us -> 0 us
  Pallas kernels: 0 us -> 42.7 us
  starting transfers between devices: 0.12 us -> 29.8 us
  between operations: 16.2 us -> 1.55 us
  local copies, waits for them, and re-layouts: 0.04 us -> 11.5 us
  other arithmetic: 14.7 us -> 8.87 us
    psum x1 -> x0, waiting for transfers between devices: 94.8 us -> none  [outer_update(): total = lax.psum(local_delta, 'replica')]
    all_gather x2 -> x0, waiting for transfers between devices: 92.6 us -> none  [the longest x1 62.4 us: per_device(): normed_rows = lax.all_gather(normed, 'fsdp', axis=0, tiled=True)]
    ppermute x0 -> x16, waiting for transfers between devices: none -> 61.2 us  [the longest x1 26.6 us: per_device(): z_own = other_z(own)]
    dot_general x3 -> x0, matrix products: 46.1 us -> none  [the longest x1 26.5 us: per_device(): lax.dot_general(left, right, (((0,), (0,)), ((), ())), preferred_element_...]
    pallas_call x0 -> x6, Pallas kernels: none -> 42.7 us  [the longest x4 30.4 us: forward(): pl.pallas_call(functools.partial(forward_kernel, count), out_shape=jax.Sh...]
    ppermute x0 -> x16, starting transfers between devices: none -> 29.8 us  [the longest x3 6.72 us: replica_delta(): lax.ppermute(quarter(k), 'replica', replica_shift(k))]
    sub x2 -> x0, other arithmetic: 10.8 us -> none  [the longest x1 6.48 us: nesterov(): return (global_part - outer_lr * (delta + nesterov_mu * mom_next), mom_next)]
    unnamed x6 -> x28, local copies, waits for them, and re-layouts: 0.04 us -> 9.11 us
  transfers between devices with their start and end apart: 3 -> 16, of which waited for: 3 -> 6; matrix products, arithmetic and copies ran while one was open for 8% -> 5% of each run, Pallas kernels for 0% -> 27%
where the time goes in v1:
time: 156 us
  waiting for transfers between devices  61.2 us (39%)
  Pallas kernels  42.7 us (27%)
  starting transfers between devices  29.8 us (19%)
  local copies, waits for them, and re-layouts  11.5 us (7%)
  other arithmetic  8.87 us (6%)
    pallas_call x4, Pallas kernels, forward(): pl.pallas_call(functools.partial(forward_kernel, count), out_shape=jax.Sh...  30.4 us
    ppermute x1, waiting for transfers between devices, per_device(): z_own = other_z(own)  26.6 us
    ppermute x3, waiting for transfers between devices, replica_delta(): lax.ppermute(quarter(k), 'replica', replica_shift(k))  19.9 us
    pallas_call x1, Pallas kernels, partial_grads(): pl.pallas_call(functools.partial(grad_kernel, count, tuple(spans), 256),...  11.8 us
    unnamed x28, local copies, waits for them, and re-layouts  9.11 us
    ppermute x1, waiting for transfers between devices, replica_delta(): other = lax.ppermute(part, 'replica', OTHER_H)  7.37 us
    ppermute x3, starting transfers between devices, replica_delta(): lax.ppermute(quarter(k), 'replica', replica_shift(k))  6.72 us
    ppermute x3, waiting for transfers between devices, replica_delta(): lax.ppermute(mine, 'replica', replica_shift(k))  6.34 us
  transfers between devices with their start and end apart: 16, of which 6 were waited for; matrix products, arithmetic and copies ran while one was open for 5% of the time, Pallas kernels for 27%

profile of v1, /device:TPU:1, one launch (start us, length us, event | category | flops | bytes accessed | tf_op | source)
XLA Modules:
  0.0 155.6 jit_solution(12972183927887498142)
XLA Ops:
  0.6 1.5 collective-permute-start.14
  2.1 0.7 reshape.38.g_ref
  2.8 1.1 copy-done.1
  4.0 1.1 copy-done.2
  5.1 0.5 norm.1.refs_0_
  5.6 1.8 %collective-permute-start.9 = (bf16[256,3072]{1,0:T(8,128)(2,1)S(1)}, bf16[256,3072]{1,0:T(8,128)(2,1)S(1)}, u32[]{:S(2)}, u32[]{:S(2)}) collective-permute-start(bf16[256,3072]{1,0:T(8,128)(2,1)S(1)} %norm.1.refs_0_), channel_id=1, source_target_pairs={{0,8},{1,9},{2,10},{3,11},{4,12},{5,13},{6,14},{7,15},{8,0},{9,1},... | collective-permute-start | bytes 4718600 | tf_op jit(solution)/shard_map/ppermute | solution.py:219
  8.1 1.5 constant_dynamic-slice_fusion
  9.6 0.0 copy-start.3
  9.6 0.1 dynamic-slice_bitcast_fusion.2
  9.7 2.5 %collective-permute-start.2 = (bf16[768,256]{1,0:T(8,128)(2,1)S(1)}, bf16[768,256]{1,0:T(8,128)(2,1)S(1)}, u32[]{:S(2)}, u32[]{:S(2)}) collective-permute-start(bf16[768,256]{1,0:T(8,128)(2,1)S(1)} %get-tuple-element.13), channel_id=1, source_target_pairs={{0,48},{16,0},{32,16},{48,32},{64,112},{80,64},{96,80},{112,96},{1... | collective-permute-start | bytes 1179656 | tf_op jit(solution)/shard_map/ppermute | solution.py:196
  12.3 2.7 %collective-permute-start.7 = (bf16[256,3072]{1,0:T(8,128)(2,1)S(1)}, bf16[256,3072]{1,0:T(8,128)(2,1)}, u32[]{:S(2)}, u32[]{:S(2)}) collective-permute-start(bf16[256,3072]{1,0:T(8,128)(2,1)S(1)} %norm.1.refs_0_), channel_id=1, source_target_pairs={{0,2},{1,7},{2,4},{3,1},{4,6},{5,3},{6,0},{7,5},{8,10},{9,15},{10,... | collective-permute-start | bytes 4718600 | tf_op jit(solution)/shard_map/ppermute | solution.py:217
  15.0 0.6 collective-permute-start.8
  15.6 26.6 %collective-permute-done.9.refs_1_.refs_3_ = bf16[256,3072]{1,0:T(8,128)(2,1)S(1)} collective-permute-done((bf16[256,3072]{1,0:T(8,128)(2,1)S(1)}, bf16[256,3072]{1,0:T(8,128)(2,1)S(1)}, u32[]{:S(2)}, u32[]{:S(2)}) %collective-permute-start.9) | collective-permute-done | bytes 1572896 | tf_op jit(solution)/shard_map/ppermute | solution.py:219
  42.2 2.7 %collective-permute-start.10 = (bf16[256,3072]{1,0:T(8,128)(2,1)S(1)}, bf16[256,3072]{1,0:T(8,128)(2,1)}, u32[]{:S(2)}, u32[]{:S(2)}) collective-permute-start(bf16[256,3072]{1,0:T(8,128)(2,1)S(1)} %collective-permute-done.9.refs_1_.refs_3_), channel_id=1, source_target_pairs={{0,2},{1,7},{2,4},{3,1},{4,6},{5,3},{6,0},{7,5},{8,10},{9,15},{10,... | collective-permute-start | bytes 4718600 | tf_op jit(solution)/shard_map/ppermute | solution.py:220
  44.9 2.7 %collective-permute-start.1 = (bf16[768,256]{1,0:T(8,128)(2,1)S(1)}, bf16[768,256]{1,0:T(8,128)(2,1)S(1)}, u32[]{:S(2)}, u32[]{:S(2)}) collective-permute-start(bf16[768,256]{1,0:T(8,128)(2,1)S(1)} %get-tuple-element.14), channel_id=1, source_target_pairs={{0,32},{16,48},{32,0},{48,16},{64,96},{80,112},{96,64},{112,80},{1... | collective-permute-start | bytes 1179656 | tf_op jit(solution)/shard_map/ppermute | solution.py:196
  47.6 9.7 %collective-permute-done.1 = bf16[768,256]{1,0:T(8,128)(2,1)S(1)} collective-permute-done((bf16[768,256]{1,0:T(8,128)(2,1)S(1)}, bf16[768,256]{1,0:T(8,128)(2,1)S(1)}, u32[]{:S(2)}, u32[]{:S(2)}) %collective-permute-start.1) | collective-permute-done | bytes 393248 | tf_op jit(solution)/shard_map/ppermute | solution.py:196
  57.3 0.7 copy-done.10
  58.1 1.4 collective-permute-start
  59.5 10.2 %collective-permute-done = bf16[768,256]{1,0:T(8,128)(2,1)} collective-permute-done((bf16[768,256]{1,0:T(8,128)(2,1)S(1)}, bf16[768,256]{1,0:T(8,128)(2,1)}, u32[]{:S(2)}, u32[]{:S(2)}) %collective-permute-start) | collective-permute-done | bytes 393248 | tf_op jit(solution)/shard_map/ppermute | solution.py:196
  69.7 1.9 %fusion.14 = f16[768,256]{1,0:T(8,128)(2,1)S(1)} fusion(bf16[768,256]{1,0:T(8,128)(2,1)} %copy-done.9, bf16[768,256]{1,0:T(8,128)(2,1)} %copy-done.10, bf16[768,256]{1,0:T(8,128)(2,1)} %collective-permute-done, f32[4,768,256]{2,1,0:T(8,128)} %bitcast.84, s32[]{:T(128)S(6)} %select_n.31, bf16[4,768,256]{2,1,0:T(8,128)(2,1)} %bitcast.83, s32[]{:T(128)S(6)} %select_n.34), kind=kLoop, calls=%fused_computation.21 | loop fusion | flops 2555904 | bytes 2752520 | tf_op jit(solution)/shard_map/convert_element_type | solution.py:199
  71.6 3.6 %collective-permute-start.3 = (f16[768,256]{1,0:T(8,128)(2,1)S(1)}, f16[768,256]{1,0:T(8,128)(2,1)S(1)}, u32[]{:S(2)}, u32[]{:S(2)}) collective-permute-start(f16[768,256]{1,0:T(8,128)(2,1)S(1)} %fusion.14), channel_id=1, source_target_pairs={{0,64},{16,80},{32,96},{48,112},{64,0},{80,16},{96,32},{112,48},{1... | collective-permute-start | bytes 1179656 | tf_op jit(solution)/shard_map/ppermute | solution.py:200
  75.2 0.8 collective-permute-start.12
  76.0 7.4 %collective-permute-done.3 = f16[768,256]{1,0:T(8,128)(2,1)S(1)} collective-permute-done((f16[768,256]{1,0:T(8,128)(2,1)S(1)}, f16[768,256]{1,0:T(8,128)(2,1)S(1)}, u32[]{:S(2)}, u32[]{:S(2)}) %collective-permute-start.3) | collective-permute-done | bytes 393248 | tf_op jit(solution)/shard_map/ppermute | solution.py:200
  83.4 1.0 bitcast_dynamic-update-slice_fusion.6
  84.4 1.3 collective-permute-start.4
  85.7 6.3 %collective-permute-done.4 = f16[768,256]{1,0:T(8,128)(2,1)S(1)} collective-permute-done((f16[768,256]{1,0:T(8,128)(2,1)}, f16[768,256]{1,0:T(8,128)(2,1)S(1)}, u32[]{:S(2)}, u32[]{:S(2)}) %collective-permute-start.4) | collective-permute-done | bytes 393248 | tf_op jit(solution)/shard_map/ppermute | solution.py:202
  92.0 2.2 %collective-permute-start.5 = (f16[768,256]{1,0:T(8,128)(2,1)}, f16[768,256]{1,0:T(8,128)(2,1)S(1)}, u32[]{:S(2)}, u32[]{:S(2)}) collective-permute-start(f16[768,256]{1,0:T(8,128)(2,1)} %get-tuple-element.11), channel_id=1, source_target_pairs={{0,32},{16,48},{32,0},{48,16},{64,96},{80,112},{96,64},{112,80},{1... | collective-permute-start | bytes 1179656 | tf_op jit(solution)/shard_map/ppermute | solution.py:202
  94.2 0.8 bitcast_dynamic-update-slice_fusion.4
  95.0 0.9 collective-permute-start.6
  95.9 2.3 %copy-done = bf16[1,3,3072,256]{3,2,1,0:T(8,128)(2,1)S(1)} copy-done((bf16[1,3,3072,256]{3,2,1,0:T(8,128)(2,1)S(1)}, bf16[1,3,3072,256]{3,2,1,0:T(8,128)(2,1)}, u32[]{:S(2)}) %copy-start) | copy-done | bytes 4718616
  98.2 7.4 %forward.4.refs_8_ = bf16[256,512]{1,0:T(8,128)(2,1)S(1)} custom-call(s32[1]{0:T(128)} %bitcast.15.frag_ref, bf16[256,3072]{1,0:T(8,128)(2,1)S(1)} %norm.1.refs_0_, bf16[256,3072]{1,0:T(8,128)(2,1)} %collective-permute-done.7.refs_1_, bf16[3,3072,256]{2,1,0:T(8,128)(2,1)S(1)} %bitcast.76, bf16[3,3072,256]{2,1,0:T(8,128)(2,1)} %collective-permute-done.14.refs_3_), custom_call_target="tpu_custom_call" | custom-call | flops 2415919104 | bytes 12582912 | tf_op jit(solution)/shard_map/forward/pallas_call | solution.py:113
  105.7 7.5 %forward.5.refs_9_ = bf16[256,512]{1,0:T(8,128)(2,1)S(1)} custom-call(s32[1]{0:T(128)} %bitcast.15.frag_ref, bf16[256,3072]{1,0:T(8,128)(2,1)} %collective-permute-done.8.refs_0_.refs_2_, bf16[256,3072]{1,0:T(8,128)(2,1)S(1)} %collective-permute-done.9.refs_1_.refs_3_, bf16[3,3072,256]{2,1,0:T(8,128)(2,1)S(1)} %bitcast.77, ...), custom_call_target="tpu_custom_call" | custom-call | flops 2415919104 | bytes 12582912 | tf_op jit(solution)/shard_map/forward/pallas_call | solution.py:113
  113.2 7.8 %forward.6.refs_10_ = bf16[256,512]{1,0:T(8,128)(2,1)S(1)} custom-call(s32[1]{0:T(128)} %bitcast.15.frag_ref, bf16[256,3072]{1,0:T(8,128)(2,1)} %collective-permute-done.10.refs_0_.refs_4_, bf16[256,3072]{1,0:T(8,128)(2,1)} %collective-permute-done.11.refs_1_.refs_5_, bf16[3,3072,256]{2,1,0:T(8,128)(2,1)S(1)} %bitcast.78, ...), custom_call_target="tpu_custom_call" | custom-call | flops 2415919104 | bytes 12582912 | tf_op jit(solution)/shard_map/forward/pallas_call | solution.py:113
  121.0 7.8 %forward.7.refs_11_ = bf16[256,512]{1,0:T(8,128)(2,1)S(1)} custom-call(s32[1]{0:T(128)} %bitcast.15.frag_ref, bf16[256,3072]{1,0:T(8,128)(2,1)} %collective-permute-done.12.refs_0_.refs_6_, bf16[256,3072]{1,0:T(8,128)(2,1)} %collective-permute-done.13.refs_1_.refs_7_, bf16[3,3072,256]{2,1,0:T(8,128)(2,1)S(1)} %bitcast.79, ...), custom_call_target="tpu_custom_call" | custom-call | flops 2415919104 | bytes 12582912 | tf_op jit(solution)/shard_map/forward/pallas_call | solution.py:113
  128.8 0.0 copy-start.8
  128.8 11.8 %grad.1 = (bf16[3072,256]{1,0:T(8,128)(2,1)S(1)}, f32[3072,256]{1,0:T(8,128)S(1)}) custom-call(s32[1]{0:T(128)} %bitcast.15.frag_ref, bf16[256,3072]{1,0:T(8,128)(2,1)S(1)} %norm.1.refs_0_, bf16[256,3072]{1,0:T(8,128)(2,1)} %collective-permute-done.7.refs_1_, bf16[256,3072]{1,0:T(8,128)(2,1)} %collective-permute-done.8.refs_0_.refs_2_, ...), custom_call_target="tpu_custom_call" | custom-call | flops 3221225472 | bytes 11010048 | tf_op jit(solution)/shard_map/grad/pallas_call | solution.py:172
  140.6 5.0 %collective-permute-start.15 = (bf16[3072,256]{1,0:T(8,128)(2,1)S(1)}, bf16[3072,256]{1,0:T(8,128)(2,1)S(1)}, u32[]{:S(2)}, u32[]{:S(2)}) collective-permute-start(bf16[3072,256]{1,0:T(8,128)(2,1)S(1)} %get-tuple-element.6), channel_id=1, source_target_pairs={{0,1},{1,0},{2,3},{3,2},{4,5},{5,4},{6,7},{7,6},{8,9},{9,8},{10,11... | collective-permute-start | bytes 4718600 | tf_op jit(solution)/shard_map/ppermute | solution.py:234
  145.6 0.1 bitcast_dynamic-update-slice_fusion.2
  145.7 0.1 bitcast_dynamic-update-slice_fusion
  145.7 1.2 bitcast_dynamic-update-slice_fusion.7
  147.0 0.1 bitcast_dynamic-update-slice_fusion.5
  147.1 0.1 bitcast_dynamic-update-slice_fusion.3
  147.2 0.1 bitcast_dynamic-update-slice_fusion.1
  147.3 0.3 convert_multiply_fusion
  147.6 1.0 collective-permute-done.15
  148.6 0.5 copy-done.4
  149.1 0.9 copy-done.5
  150.0 5.6 %fusion.9 = (bf16[1,3072,256]{2,1,0:T(8,128)(2,1)}, f32[3072,256]{1,0:T(8,128)}, f32[3072,256]{1,0:T(8,128)}) fusion(f32[1,3072,256]{2,1,0:T(8,128)S(1)} %copy-done.5, f32[3072,256]{1,0:T(8,128)S(1)} %get-tuple-element.5, bf16[3072,256]{1,0:T(8,128)(2,1)S(1)} %collective-permute-done.15, f32[1,3072,256]{2,1,0:T(8,128)S(1)} %copy-done.6, ...), kind=kLoop, calls=%fused_computation.15 | loop fusion | flops 18874368 | bytes 29884420 | tf_op jit(solution)/shard_map/broadcast_in_dim | solution.py:240
  (26 shorter events, 0.1 us)
Async XLA Ops:
  0.6 94.4 %collective-permute-start.14 = (bf16[3,3072,256]{2,1,0:T(8,128)(2,1)}, bf16[3,3072,256]{2,1,0:T(8,128)(2,1)}, u32[]{:S(2)}, u32[]{:S(2)}) collective-permute-start(bf16[3,3072,256]{2,1,0:T(8,128)(2,1)} %bitcast.75), channel_id=1, source_target_pairs={{0,1},{1,0},{2,3},{3,2},{4,5},{5,4},{6,7},{7,6},{8,9},{9,8},{10,11... | collective-permute-start | bytes 14155784 | tf_op jit(solution)/shard_map/ppermute | solution.py:211
  2.8 1.1 copy-start.1
  4.0 1.1 copy-start.2
  5.6 36.6 %collective-permute-start.9 = (bf16[256,3072]{1,0:T(8,128)(2,1)S(1)}, bf16[256,3072]{1,0:T(8,128)(2,1)S(1)}, u32[]{:S(2)}, u32[]{:S(2)}) collective-permute-start(bf16[256,3072]{1,0:T(8,128)(2,1)S(1)} %norm.1.refs_0_), channel_id=1, source_target_pairs={{0,8},{1,9},{2,10},{3,11},{4,12},{5,13},{6,14},{7,15},{8,0},{9,1},... | collective-permute-start | bytes 4718600 | tf_op jit(solution)/shard_map/ppermute | solution.py:219
  9.6 32.6 %copy-start.3 = (bf16[1,1,3072,256]{3,2,1,0:T(8,128)(2,1)}, bf16[1,1,3072,256]{3,2,1,0:T(8,128)(2,1)S(1)}, u32[]{:S(2)}) copy-start(bf16[1,1,3072,256]{3,2,1,0:T(8,128)(2,1)S(1)} %constant_dynamic-slice_fusion) | copy-start | bytes 4718596
  9.7 35.2 %collective-permute-start.2 = (bf16[768,256]{1,0:T(8,128)(2,1)S(1)}, bf16[768,256]{1,0:T(8,128)(2,1)S(1)}, u32[]{:S(2)}, u32[]{:S(2)}) collective-permute-start(bf16[768,256]{1,0:T(8,128)(2,1)S(1)} %get-tuple-element.13), channel_id=1, source_target_pairs={{0,48},{16,0},{32,16},{48,32},{64,112},{80,64},{96,80},{112,96},{1... | collective-permute-start | bytes 1179656 | tf_op jit(solution)/shard_map/ppermute | solution.py:196
  12.3 63.0 %collective-permute-start.7 = (bf16[256,3072]{1,0:T(8,128)(2,1)S(1)}, bf16[256,3072]{1,0:T(8,128)(2,1)}, u32[]{:S(2)}, u32[]{:S(2)}) collective-permute-start(bf16[256,3072]{1,0:T(8,128)(2,1)S(1)} %norm.1.refs_0_), channel_id=1, source_target_pairs={{0,2},{1,7},{2,4},{3,1},{4,6},{5,3},{6,0},{7,5},{8,10},{9,15},{10,... | collective-permute-start | bytes 4718600 | tf_op jit(solution)/shard_map/ppermute | solution.py:217
  15.0 60.2 %collective-permute-start.8 = (bf16[256,3072]{1,0:T(8,128)(2,1)S(1)}, bf16[256,3072]{1,0:T(8,128)(2,1)}, u32[]{:S(2)}, u32[]{:S(2)}) collective-permute-start(bf16[256,3072]{1,0:T(8,128)(2,1)S(1)} %norm.1.refs_0_), channel_id=1, source_target_pairs={{0,7},{1,2},{2,1},{3,4},{4,3},{5,6},{6,5},{7,0},{8,15},{9,10},{10,... | collective-permute-start | bytes 4718600 | tf_op jit(solution)/shard_map/ppermute | solution.py:218
  42.2 33.8 %collective-permute-start.10 = (bf16[256,3072]{1,0:T(8,128)(2,1)S(1)}, bf16[256,3072]{1,0:T(8,128)(2,1)}, u32[]{:S(2)}, u32[]{:S(2)}) collective-permute-start(bf16[256,3072]{1,0:T(8,128)(2,1)S(1)} %collective-permute-done.9.refs_1_.refs_3_), channel_id=1, source_target_pairs={{0,2},{1,7},{2,4},{3,1},{4,6},{5,3},{6,0},{7,5},{8,10},{9,15},{10,... | collective-permute-start | bytes 4718600 | tf_op jit(solution)/shard_map/ppermute | solution.py:220
  44.9 12.4 %copy-start.9 = (bf16[768,256]{1,0:T(8,128)(2,1)}, bf16[768,256]{1,0:T(8,128)(2,1)S(1)}, u32[]{:S(2)}) copy-start(bf16[768,256]{1,0:T(8,128)(2,1)S(1)} %collective-permute-done.2) | copy-start | bytes 1179652
  44.9 12.4 %collective-permute-start.1 = (bf16[768,256]{1,0:T(8,128)(2,1)S(1)}, bf16[768,256]{1,0:T(8,128)(2,1)S(1)}, u32[]{:S(2)}, u32[]{:S(2)}) collective-permute-start(bf16[768,256]{1,0:T(8,128)(2,1)S(1)} %get-tuple-element.14), channel_id=1, source_target_pairs={{0,32},{16,48},{32,0},{48,16},{64,96},{80,112},{96,64},{112,80},{1... | collective-permute-start | bytes 1179656 | tf_op jit(solution)/shard_map/ppermute | solution.py:196
  57.3 0.7 copy-start.10
  58.1 11.6 %collective-permute-start = (bf16[768,256]{1,0:T(8,128)(2,1)S(1)}, bf16[768,256]{1,0:T(8,128)(2,1)}, u32[]{:S(2)}, u32[]{:S(2)}) collective-permute-start(bf16[768,256]{1,0:T(8,128)(2,1)S(1)} %get-tuple-element.12), channel_id=1, source_target_pairs={{0,16},{16,32},{32,48},{48,0},{64,80},{80,96},{96,112},{112,64},{1... | collective-permute-start | bytes 1179656 | tf_op jit(solution)/shard_map/ppermute | solution.py:196
  71.6 11.8 %collective-permute-start.3 = (f16[768,256]{1,0:T(8,128)(2,1)S(1)}, f16[768,256]{1,0:T(8,128)(2,1)S(1)}, u32[]{:S(2)}, u32[]{:S(2)}) collective-permute-start(f16[768,256]{1,0:T(8,128)(2,1)S(1)} %fusion.14), channel_id=1, source_target_pairs={{0,64},{16,80},{32,96},{48,112},{64,0},{80,16},{96,32},{112,48},{1... | collective-permute-start | bytes 1179656 | tf_op jit(solution)/shard_map/ppermute | solution.py:200
  75.2 37.9 %collective-permute-start.11 = (bf16[256,3072]{1,0:T(8,128)(2,1)}, bf16[256,3072]{1,0:T(8,128)(2,1)}, u32[]{:S(2)}, u32[]{:S(2)}) collective-permute-start(bf16[256,3072]{1,0:T(8,128)(2,1)} %collective-permute-done.7.refs_1_), channel_id=1, source_target_pairs={{0,2},{1,7},{2,4},{3,1},{4,6},{5,3},{6,0},{7,5},{8,10},{9,15},{10,... | collective-permute-start | bytes 4718600 | tf_op jit(solution)/shard_map/ppermute | solution.py:221
  75.2 45.7 %collective-permute-start.12 = (bf16[256,3072]{1,0:T(8,128)(2,1)}, bf16[256,3072]{1,0:T(8,128)(2,1)}, u32[]{:S(2)}, u32[]{:S(2)}) collective-permute-start(bf16[256,3072]{1,0:T(8,128)(2,1)} %collective-permute-done.8.refs_0_.refs_2_), channel_id=1, source_target_pairs={{0,8},{1,9},{2,10},{3,11},{4,12},{5,13},{6,14},{7,15},{8,0},{9,1},... | collective-permute-start | bytes 4718600 | tf_op jit(solution)/shard_map/ppermute | solution.py:222
  76.0 44.9 %collective-permute-start.13 = (bf16[256,3072]{1,0:T(8,128)(2,1)}, bf16[256,3072]{1,0:T(8,128)(2,1)}, u32[]{:S(2)}, u32[]{:S(2)}) collective-permute-start(bf16[256,3072]{1,0:T(8,128)(2,1)} %collective-permute-done.10.refs_0_.refs_4_), channel_id=1, source_target_pairs={{0,2},{1,7},{2,4},{3,1},{4,6},{5,3},{6,0},{7,5},{8,10},{9,15},{10,... | collective-permute-start | bytes 4718600 | tf_op jit(solution)/shard_map/ppermute | solution.py:223
  84.4 7.6 %collective-permute-start.4 = (f16[768,256]{1,0:T(8,128)(2,1)}, f16[768,256]{1,0:T(8,128)(2,1)S(1)}, u32[]{:S(2)}, u32[]{:S(2)}) collective-permute-start(f16[768,256]{1,0:T(8,128)(2,1)} %get-tuple-element.11), channel_id=1, source_target_pairs={{0,48},{16,0},{32,16},{48,32},{64,112},{80,64},{96,80},{112,96},{1... | collective-permute-start | bytes 1179656 | tf_op jit(solution)/shard_map/ppermute | solution.py:202
  92.0 53.5 %collective-permute-start.5 = (f16[768,256]{1,0:T(8,128)(2,1)}, f16[768,256]{1,0:T(8,128)(2,1)S(1)}, u32[]{:S(2)}, u32[]{:S(2)}) collective-permute-start(f16[768,256]{1,0:T(8,128)(2,1)} %get-tuple-element.11), channel_id=1, source_target_pairs={{0,32},{16,48},{32,0},{48,16},{64,96},{80,112},{96,64},{112,80},{1... | collective-permute-start | bytes 1179656 | tf_op jit(solution)/shard_map/ppermute | solution.py:202
  95.0 50.6 %collective-permute-start.6 = (f16[768,256]{1,0:T(8,128)(2,1)}, f16[768,256]{1,0:T(8,128)(2,1)S(1)}, u32[]{:S(2)}, u32[]{:S(2)}) collective-permute-start(f16[768,256]{1,0:T(8,128)(2,1)} %get-tuple-element.11), channel_id=1, source_target_pairs={{0,16},{16,32},{32,48},{48,0},{64,80},{80,96},{96,112},{112,64},{1... | collective-permute-start | bytes 1179656 | tf_op jit(solution)/shard_map/ppermute | solution.py:202
  95.9 2.3 %copy-start = (bf16[1,3,3072,256]{3,2,1,0:T(8,128)(2,1)S(1)}, bf16[1,3,3072,256]{3,2,1,0:T(8,128)(2,1)}, u32[]{:S(2)}) copy-start(bf16[1,3,3072,256]{3,2,1,0:T(8,128)(2,1)} %param.13) | copy-start | bytes 14155780
  128.8 16.8 %copy-start.8 = (f16[8,768,256]{2,1,0:T(8,128)(2,1)S(1)}, f16[8,768,256]{2,1,0:T(8,128)(2,1)}, u32[]{:S(2)}) copy-start(f16[8,768,256]{2,1,0:T(8,128)(2,1)} %bitcast_dynamic-update-slice_fusion.4) | copy-start | bytes 9437188
  128.8 19.8 %copy-start.7 = (f32[3072,256]{1,0:T(8,128)S(1)}, f32[3072,256]{1,0:T(8,128)}, u32[]{:S(2)}) copy-start(f32[3072,256]{1,0:T(8,128)} %param.17) | copy-start | bytes 9437188
  140.6 8.0 %collective-permute-start.15 = (bf16[3072,256]{1,0:T(8,128)(2,1)S(1)}, bf16[3072,256]{1,0:T(8,128)(2,1)S(1)}, u32[]{:S(2)}, u32[]{:S(2)}) collective-permute-start(bf16[3072,256]{1,0:T(8,128)(2,1)S(1)} %get-tuple-element.6), channel_id=1, source_target_pairs={{0,1},{1,0},{2,3},{3,2},{4,5},{5,4},{6,7},{7,6},{8,9},{9,8},{10,11... | collective-permute-start | bytes 4718600 | tf_op jit(solution)/shard_map/ppermute | solution.py:234
  145.6 3.0 %copy-start.6 = (f32[1,3072,256]{2,1,0:T(8,128)S(1)}, f32[1,3072,256]{2,1,0:T(8,128)}, u32[]{:S(2)}) copy-start(f32[1,3072,256]{2,1,0:T(8,128)} %param.14) | copy-start | bytes 9437188
  147.1 2.0 %copy-start.4 = (f32[3072,256]{1,0:T(8,128)S(1)}, f32[3072,256]{1,0:T(8,128)}, u32[]{:S(2)}) copy-start(f32[3072,256]{1,0:T(8,128)} %param.16) | copy-start | bytes 9437188
  147.1 2.9 %copy-start.5 = (f32[1,3072,256]{2,1,0:T(8,128)S(1)}, f32[1,3072,256]{2,1,0:T(8,128)}, u32[]{:S(2)}) copy-start(f32[1,3072,256]{2,1,0:T(8,128)} %param.15) | copy-start | bytes 9437188

commit v2 on v0

v2 whole, which is shorter than its diff:
```python
import functools

import jax
import jax.numpy as jnp
from jax import lax
from jax.experimental import pallas as pl
from jax.experimental.pallas import tpu as pltpu
from jax.sharding import PartitionSpec as P

beta_one = 0.9
beta_two = 0.95
adam_eps = 1e-08
inner_lr = 0.02
outer_lr = 0.7
nesterov_mu = 0.9
mix_alpha = 0.5
norm_eps = 1e-05

WIRE_SCALE = float(2**18)

ANY = pl.BlockSpec(memory_space=pl.ANY)
VMEM = pl.BlockSpec(memory_space=pltpu.VMEM)
SMEM = pl.BlockSpec(memory_space=pltpu.SMEM)
MIB = 1024 * 1024
CHEAP = pl.CostEstimate(flops=1, bytes_accessed=1, transcendentals=0)


def fsdp_id(z, y, c):
    return (z % 2) * 8 + (y % 4) * 2 + c


def permutation(to):
    return [(fsdp_id(z, y, c), fsdp_id(*to(z, y, c))) for z in range(2) for y in range(4) for c in range(2)]


STRAIGHT = permutation(lambda z, y, c: (z, y + 1 - 2 * c, c))
CROSSED = permutation(lambda z, y, c: (z, y + 2 * c - 1, 1 - c))
OTHER_Z = permutation(lambda z, y, c: (z + 1, y, c))
SIBLING = permutation(lambda z, y, c: (z, y, 1 - c))

HALF_PAIR = [(h * 4 + x, h * 4 + (x ^ 1)) for h in range(2) for x in range(4)]
QUARTER_PAIR = [(h * 4 + x, h * 4 + 3 - x) for h in range(2) for x in range(4)]
OTHER_H = [(r, (r + 4) % 8) for r in range(8)]


def norm_kernel(x_ref, c_ref, g_ref, u_ref):
    x = x_ref[...].astype(jnp.float32)
    scale = lax.rsqrt(jnp.mean(x * x, axis=1, keepdims=True) + norm_eps)
    gain = g_ref[...].astype(jnp.float32).reshape(1, -1)
    u_ref[0] = (x * scale * gain).astype(jnp.bfloat16)
    u_ref[1] = c_ref[...]


def normed_and_cotangent(x, c, gain):
    rows, d = x.shape
    tile = 32
    return pl.pallas_call(
        norm_kernel,
        grid=(rows // tile,),
        out_shape=jax.ShapeDtypeStruct((2, rows, d), jnp.bfloat16),
        in_specs=[
            pl.BlockSpec((tile, d), lambda i: (i, 0)),
            pl.BlockSpec((tile, d), lambda i: (i, 0)),
            pl.BlockSpec((d,), lambda i: (0,)),
        ],
        out_specs=pl.BlockSpec((2, tile, d), lambda i: (0, i, 0)),
        compiler_params=pltpu.CompilerParams(vmem_limit_bytes=60 * MIB),
        cost_estimate=CHEAP,
        name="norm",
    )(x, c, gain)


def blocks_kernel(count, past, halves, emit, has_total, frag_ref, *refs):
    def take(n):
        nonlocal refs
        taken, refs = refs[:n], refs[n:]
        return taken

    blocks, old_blocks, weights = take(count), take(past), take(halves)
    old_right = take(1)[0] if past else None
    totals = take(halves) if has_total else None
    outs = take(halves if emit else 1)
    n_s, c_s, w_s, up_s, dh_s, right_s, left_s, past_s, sems = refs
    rows = blocks[0].shape[1]
    cols = weights[0].shape[2]
    frag = frag_ref[0]
    used = 0

    def load(source, target):
        nonlocal used
        copy = pltpu.make_async_copy(source, target, sems.at[used])
        used += 1
        copy.start()
        return copy

    def load_weight(h, m):
        return load(weights[h].at[m], w_s.at[3 * h + m])

    n_in = [load(b.at[0], n_s.at[pl.ds(k * rows, rows)]) for k, b in enumerate(blocks)]
    w_in = [load_weight(0, 0), load_weight(0, 1)]
    c_in = [load(b.at[1], c_s.at[pl.ds(k * rows, rows)]) for k, b in enumerate(blocks)]
    w_in += [load_weight(0, 2)] + [load_weight(h, m) for h in range(1, halves) for m in range(3)]
    side = jnp.where(frag == 2, 1, 0)
    old_in = [load(b.at[side], left_s.at[pl.ds(k * rows, rows)]) for k, b in enumerate(old_blocks)]
    if past:
        old_in.append(load(old_right, past_s))

    def dot(left, i):
        return jnp.dot(left[...], w_s[i], preferred_element_type=jnp.float32)

    def times(left_t, right):
        return jnp.dot(left_t, right, preferred_element_type=jnp.float32)

    for copy in n_in:
        copy.wait()
    for h in range(halves):
        w_in[3 * h].wait()
        gate = dot(n_s, 3 * h)
        w_in[3 * h + 1].wait()

        @pl.when(frag != 1)
        def _():
            up_s[...] = dot(n_s, 3 * h + 1)

        if h == 0:
            for copy in c_in:
                copy.wait()
        w_in[3 * h + 2].wait()

        @pl.when(frag != 2)
        def _():
            dh_s[...] = dot(c_s, 3 * h + 2)

        sig = jax.nn.sigmoid(gate)
        here = slice(h * cols, (h + 1) * cols)
        right = right_s if emit else outs[0].at[:, here]

        @pl.when(frag == 0)
        def _():
            right[...] = (dh_s[...] * up_s[...] * sig * (1.0 + gate * (1.0 - sig))).astype(jnp.bfloat16)

        @pl.when(frag == 1)
        def _():
            right[...] = (dh_s[...] * (gate * sig)).astype(jnp.bfloat16)

        @pl.when(frag == 2)
        def _():
            right[...] = (gate * sig * up_s[...]).astype(jnp.bfloat16)

        if not emit:
            continue
        if h == 0:
            for copy in old_in:
                copy.wait()

        right_t = right_s[...].T
        past_t = past_s[:, here].T if past else None

        def add(left):
            step = 768
            for at in range(0, left.shape[1], step):
                span = slice(at, at + step)
                term = times(right_t, left[:, span])
                if past:
                    term = term + times(past_t, left_s[:, span])
                if has_total:
                    term = term + totals[h][:, span]
                outs[h][:, span] = term.astype(outs[h].dtype)

        pl.when(frag == 2)(lambda: add(c_s))
        pl.when(frag != 2)(lambda: add(n_s))


def blocks_call(frag, blocks, weights, limit, old_blocks=(), old_right=None, totals=(), kind=None):
    count, past, halves = len(blocks), len(old_blocks), len(weights)
    rows = count * blocks[0].shape[1]
    past_rows = max(past * blocks[0].shape[1], 16)
    _, d, cols = weights[0].shape
    aliases = {}
    if totals and kind == jnp.float32:
        aliases = {1 + count + past + halves + bool(past) + h: h for h in range(halves)}
    if kind:
        outs = [jax.ShapeDtypeStruct((cols, d), kind)] * halves
    else:
        outs = [jax.ShapeDtypeStruct((rows, halves * cols), jnp.bfloat16)]
    operands = [frag, *blocks, *old_blocks, *weights] + ([old_right] if past else []) + list(totals)
    return pl.pallas_call(
        functools.partial(blocks_kernel, count, past, halves, bool(kind), bool(totals)),
        out_shape=outs,
        in_specs=[SMEM] + [ANY] * (len(operands) - 1 - len(totals)) + [VMEM] * len(totals),
        out_specs=[VMEM] * len(outs),
        scratch_shapes=[
            pltpu.VMEM((rows, d), jnp.bfloat16),
            pltpu.VMEM((rows, d), jnp.bfloat16),
            pltpu.VMEM((3 * halves, d, cols), jnp.bfloat16),
            pltpu.VMEM((rows, cols), jnp.float32),
            pltpu.VMEM((rows, cols), jnp.float32),
            pltpu.VMEM((rows if kind else 16, cols), jnp.bfloat16),
            pltpu.VMEM((past_rows, d), jnp.bfloat16),
            pltpu.VMEM((past_rows, halves * cols), jnp.bfloat16),
            pltpu.SemaphoreType.DMA((2 * count + 3 * halves + past + 1,)),
        ],
        input_output_aliases=aliases,
        compiler_params=pltpu.CompilerParams(vmem_limit_bytes=limit * MIB),
        cost_estimate=CHEAP,
        name="blocks",
    )(*operands)


def adam_kernel(tokens, own_ref, other_ref, m_ref, v_ref, mixed_ref, out_ref):
    grad = (own_ref[...] + other_ref[...].astype(jnp.float32)).T * (1.0 / tokens)
    moment_one = beta_one * m_ref[...] + (1.0 - beta_one) * grad
    moment_two = beta_two * v_ref[...] + (1.0 - beta_two) * grad * grad
    step_inner = inner_lr * moment_one / (jnp.sqrt(moment_two) + adam_eps)
    out_ref[...] = (mixed_ref[...] - mix_alpha * step_inner).astype(jnp.bfloat16)


def adam(tokens, own, other, m, v, mixed):
    d, cols = m.shape
    tile = 512
    wide = pl.BlockSpec((cols, tile), lambda i: (0, i))
    tall = pl.BlockSpec((tile, cols), lambda i: (i, 0))
    return pl.pallas_call(
        functools.partial(adam_kernel, tokens),
        grid=(d // tile,),
        out_shape=jax.ShapeDtypeStruct((d, cols), jnp.bfloat16),
        in_specs=[wide, wide, tall, tall, tall],
        out_specs=tall,
        compiler_params=pltpu.CompilerParams(vmem_limit_bytes=16 * MIB),
        cost_estimate=CHEAP,
        name="adam",
    )(own, other, m, v, mixed)


def after(value, *others):
    return lax.optimization_barrier((value, *others))[0]


def per_device(step, hidden_in, cotangent, norm_gain, weights, adam_m, adam_v, global_frag, outer_mom):
    fragment = step[0] % 3
    frag = fragment.reshape(1)
    w_own = weights[0]
    w_sib = lax.ppermute(w_own, "fsdp", SIBLING)
    w_both = [w_sib, w_own]
    own = normed_and_cotangent(hidden_in[0], cotangent[0], norm_gain)

    straight = functools.partial(lax.ppermute, axis_name="fsdp", perm=STRAIGHT)
    crossed = functools.partial(lax.ppermute, axis_name="fsdp", perm=CROSSED)
    other_z = functools.partial(lax.ppermute, axis_name="fsdp", perm=OTHER_Z)

    x = lax.rem(lax.axis_index("replica"), 4)
    h = lax.rem((x + 1) // 2, 2)
    q = x // 2
    d, cols = global_frag.shape
    half, quarter = d // 2, d // 4

    def w_rows(at, size):
        return lax.dynamic_slice(w_own, (fragment, at, 0), (1, size, cols))[0]

    def g_rows(at, size):
        return lax.dynamic_slice(global_frag, (at, 0), (size, cols))

    def wire(value):
        return (value * (WIRE_SCALE / 8)).astype(jnp.float16)

    near = straight(own)
    z_own = other_z(own)
    cross = crossed(own)
    w_pair = lax.ppermute(after(w_rows((1 - h) * half, half), own), "replica", HALF_PAIR)

    def pair_delta(at):
        base = g_rows(h * half + at, quarter)
        mine = w_rows(h * half + at, quarter).astype(jnp.float32)
        theirs = lax.dynamic_slice_in_dim(w_pair, at, quarter).astype(jnp.float32)
        return (base - mine) + (base - theirs)

    sent = wire(pair_delta((1 - q) * quarter))
    got = lax.ppermute(sent, "replica", QUARTER_PAIR)
    part = wire(pair_delta(q * quarter) + got.astype(jnp.float32) * (8 / WIRE_SCALE))
    part = after(part, near, cross, z_own)
    other = lax.ppermute(part, "replica", OTHER_H)

    z_near = straight(z_own)
    z_cross = other_z(cross)
    first = [own, near, cross, z_own]
    (right,) = blocks_call(frag, first, w_both, 58)
    far = straight(near)
    mine = (part.astype(jnp.float32) + other.astype(jnp.float32)).astype(jnp.float16)
    mine = after(mine, right)
    got = lax.ppermute(mine, "replica", QUARTER_PAIR)
    mine = jnp.where(q == 0, jnp.concatenate([mine, got]), jnp.concatenate([got, mine]))
    got = lax.ppermute(mine, "replica", HALF_PAIR)
    z_far = straight(after(z_near, right))

    delta = jnp.where(h == 0, jnp.concatenate([mine, got]), jnp.concatenate([got, mine]))
    delta = delta.astype(jnp.float32) * (1 / WIRE_SCALE)
    momentum_new = nesterov_mu * outer_mom + delta
    global_new = global_frag - outer_lr * (delta + nesterov_mu * momentum_new)
    mixed = mix_alpha * w_rows(0, d).astype(jnp.float32) + (1.0 - mix_alpha) * global_new

    second = [far, z_near, z_cross]
    totals = blocks_call(frag, second, w_both, 54, first, right, kind=jnp.float32)
    z_far = after(z_far, mixed, *totals)
    (grad_sib,) = blocks_call(frag, [z_far], [w_sib], 28, totals=totals[:1], kind=jnp.bfloat16)
    grad_sib = lax.ppermute(grad_sib, "fsdp", SIBLING)
    (grad_own,) = blocks_call(frag, [z_far], [w_own], 28, totals=totals[1:], kind=jnp.float32)
    tokens_total = hidden_in.shape[1] * lax.axis_size("fsdp")
    merged = adam(tokens_total, grad_own, grad_sib, adam_m[0], adam_v[0], mixed)
    return (global_new, momentum_new, merged[None])


def solution(mesh):
    placed = (
        P(),
        P("replica", "fsdp", None),
        P("replica", "fsdp", None),
        P(),
        P("replica", None, None, "fsdp"),
        P("replica", None, "fsdp"),
        P("replica", None, "fsdp"),
        P(None, "fsdp"),
        P(None, "fsdp"),
    )
    return jax.shard_map(
        per_device,
        mesh=mesh,
        in_specs=placed,
        out_specs=(P(None, "fsdp"), P(None, "fsdp"), P("replica", None, "fsdp")),
        check_vma=False,
    )
```

time: 267 us -> 126 us (0.47)
  waiting for transfers between devices: 188 us -> 48.4 us
  matrix products: 46.1 us -> 0 us
  Pallas kernels: 0 us -> 36.8 us
  starting transfers between devices: 0.12 us -> 26.9 us
  between operations: 16.2 us -> 1.49 us
  other arithmetic: 14.7 us -> 9.8 us
    psum x1 -> x0, waiting for transfers between devices: 94.8 us -> none  [outer_update(): total = lax.psum(local_delta, 'replica')]
    all_gather x2 -> x0, waiting for transfers between devices: 92.6 us -> none  [the longest x1 62.4 us: per_device(): normed_rows = lax.all_gather(normed, 'fsdp', axis=0, tiled=True)]
    ppermute x0 -> x14, waiting for transfers between devices: none -> 48.4 us  [the longest x1 18 us: per_device(): lax.ppermute(after(w_rows((1 - h) * half, half), own), 'replica', HALF_PAIR)]
    dot_general x3 -> x0, matrix products: 46.1 us -> none  [the longest x1 26.5 us: per_device(): lax.dot_general(left, right, (((0,), (0,)), ((), ())), preferred_element_...]
    pallas_call x0 -> x6, Pallas kernels: none -> 36.8 us  [the longest x4 28.7 us: blocks_call(): pl.pallas_call(functools.partial(blocks_kernel, count, past, halves, bool...]
    ppermute x0 -> x14, starting transfers between devices: none -> 26.9 us  [the longest x1 6.65 us: per_device(): z_far = straight(after(z_near, right))]
    sub x2 -> x0, other arithmetic: 10.8 us -> none  [the longest x1 6.48 us: nesterov(): return (global_part - outer_lr * (delta + nesterov_mu * mom_next), mom_next)]
    add x0 -> x1, other arithmetic: none -> 5.87 us  [per_device(): mix_alpha * w_rows(0, d).astype(jnp.float32)]
  transfers between devices with their start and end apart: 3 -> 14, of which waited for: 3 -> 6; matrix products, arithmetic and copies ran while one was open for 8% -> 9% of each run, Pallas kernels for 0% -> 23%
where the time goes in v2:
time: 126 us; the launch traced here: 125 us
  waiting for transfers between devices  48.4 us (38%)
  Pallas kernels  36.8 us (29%)
  starting transfers between devices  26.9 us (21%)
  other arithmetic  9.8 us (8%)
  local copies, waits for them, and re-layouts  2.1 us (2%)
  between operations  1.49 us (1%)
    pallas_call x4, Pallas kernels, blocks_call(): pl.pallas_call(functools.partial(blocks_kernel, count, past, halves, bool...  28.7 us
    ppermute x1, waiting for transfers between devices, per_device(): lax.ppermute(after(w_rows((1 - h) * half, half), own), 'replica', HALF_PAIR)  18 us
    ppermute x1, waiting for transfers between devices, per_device(): z_cross = other_z(cross)  9.11 us
    ppermute x1, waiting for transfers between devices, per_device(): got = lax.ppermute(sent, 'replica', QUARTER_PAIR)  8.55 us
    ppermute x1, starting transfers between devices, per_device(): z_far = straight(after(z_near, right))  6.65 us
    ppermute x1, waiting for transfers between devices, per_device(): other = lax.ppermute(part, 'replica', OTHER_H)  6.12 us
    add x1, other arithmetic, per_device(): mix_alpha * w_rows(0, d).astype(jnp.float32)  5.87 us
    ppermute x1, waiting for transfers between devices, per_device(): got = lax.ppermute(mine, 'replica', QUARTER_PAIR)  5.76 us
  transfers between devices with their start and end apart: 14, of which 6 were waited for; matrix products, arithmetic and copies ran while one was open for 9% of the time, Pallas kernels for 23%

profile of v2, /device:TPU:1, one launch (start us, length us, event | category | flops | bytes accessed | tf_op | source)
XLA Modules:
  0.0 125.5 jit_solution(13358779159678072493)
XLA Ops:
  0.6 0.0 copy-start.4
  0.6 1.5 %collective-permute-start.6 = (bf16[3,3072,256]{2,1,0:T(8,128)(2,1)}, bf16[3,3072,256]{2,1,0:T(8,128)(2,1)}, u32[]{:S(2)}, u32[]{:S(2)}) collective-permute-start(bf16[3,3072,256]{2,1,0:T(8,128)(2,1)} %bitcast.19), channel_id=1, source_target_pairs={{0,1},{1,0},{2,3},{3,2},{4,5},{5,4},{6,7},{7,6},{8,9},{9,8},{10,11... | collective-permute-start | bytes 14155784 | tf_op jit(solution)/shard_map/ppermute | solution.py:243
  2.1 3.9 %norm.1.refs_0_.refs_3_ = bf16[2,128,3072]{2,1,0:T(8,128)(2,1)} custom-call(bf16[128,3072]{1,0:T(8,128)(2,1)} %bitcast.28, bf16[128,3072]{1,0:T(8,128)(2,1)} %bitcast.29, bf16[3072]{0:T(1024)(128)(2,1)} %g_ref.1), custom_call_target="tpu_custom_call" | custom-call | flops 1 | bytes 1 | tf_op jit(solution)/shard_map/norm/pallas_call | solution.py:57
  6.0 1.9 %collective-permute-start.4 = (bf16[2,128,3072]{2,1,0:T(8,128)(2,1)}, bf16[2,128,3072]{2,1,0:T(8,128)(2,1)}, u32[]{:S(2)}, u32[]{:S(2)}) collective-permute-start(bf16[2,128,3072]{2,1,0:T(8,128)(2,1)} %norm.1.refs_0_.refs_3_), channel_id=1, source_target_pairs={{0,8},{1,9},{2,10},{3,11},{4,12},{5,13},{6,14},{7,15},{8,0},{9,1},... | collective-permute-start | bytes 4718600 | tf_op jit(solution)/shard_map/ppermute | solution.py:267
  7.9 1.5 %collective-permute-start.3 = (bf16[2,128,3072]{2,1,0:T(8,128)(2,1)}, bf16[2,128,3072]{2,1,0:T(8,128)(2,1)}, u32[]{:S(2)}, u32[]{:S(2)}) collective-permute-start(bf16[2,128,3072]{2,1,0:T(8,128)(2,1)} %norm.1.refs_0_.refs_3_), channel_id=1, source_target_pairs={{0,7},{1,2},{2,1},{3,4},{4,3},{5,6},{6,5},{7,0},{8,15},{9,10},{10,... | collective-permute-start | bytes 4718600 | tf_op jit(solution)/shard_map/ppermute | solution.py:268
  9.4 1.4 %collective-permute-start.2 = (bf16[2,128,3072]{2,1,0:T(8,128)(2,1)}, bf16[2,128,3072]{2,1,0:T(8,128)(2,1)}, u32[]{:S(2)}, u32[]{:S(2)}) collective-permute-start(bf16[2,128,3072]{2,1,0:T(8,128)(2,1)} %norm.1.refs_0_.refs_3_), channel_id=1, source_target_pairs={{0,2},{1,7},{2,4},{3,1},{4,6},{5,3},{6,0},{7,5},{8,10},{9,15},{10,... | collective-permute-start | bytes 4718600 | tf_op jit(solution)/shard_map/ppermute | solution.py:266
  11.4 2.1 %dynamic-slice_bitcast_fusion = bf16[1536,256]{1,0:T(8,128)(2,1)} fusion(bf16[1,3,3072,256]{3,2,1,0:T(8,128)(2,1)} %param.13, s32[]{:T(128)S(6)} %select_n.59, s32[]{:T(128)S(6)} %select_n.60), kind=kLoop, calls=%fused_computation.17 | loop fusion | bytes 1572872 | tf_op jit(solution)/shard_map/squeeze | solution.py:258
  13.5 1.2 collective-permute-start
  14.7 18.0 %collective-permute-done = bf16[1536,256]{1,0:T(8,128)(2,1)} collective-permute-done((bf16[1536,256]{1,0:T(8,128)(2,1)}, bf16[1536,256]{1,0:T(8,128)(2,1)}, u32[]{:S(2)}, u32[]{:S(2)}) %collective-permute-start) | collective-permute-done | bytes 786464 | tf_op jit(solution)/shard_map/ppermute | solution.py:269
  32.7 0.0 copy-done.4
  32.7 2.1 %fusion.3 = f16[768,256]{1,0:T(8,128)(2,1)} fusion(f32[3072,256]{1,0:T(8,128)S(1)} %copy-done.4, s32[]{:T(128)S(6)} %select_n.62, bf16[1536,256]{1,0:T(8,128)(2,1)} %collective-permute-done, s32[]{:T(128)S(6)} %select_n.63, bf16[1,3,3072,256]{3,2,1,0:T(8,128)(2,1)} %param.13, s32[]{:T(128)S(6)} %select_n.59), kind=kLoop, calls=%fused_computation.10 | loop fusion | flops 1376256 | bytes 1966092 | tf_op jit(solution)/shard_map/convert_element_type | solution.py:264
  34.7 2.5 %collective-permute-start.1 = (f16[768,256]{1,0:T(8,128)(2,1)}, f16[768,256]{1,0:T(8,128)(2,1)S(1)}, u32[]{:S(2)}, u32[]{:S(2)}) collective-permute-start(f16[768,256]{1,0:T(8,128)(2,1)} %fusion.3), channel_id=1, source_target_pairs={{0,48},{16,32},{32,16},{48,0},{64,112},{80,96},{96,80},{112,64},{1... | collective-permute-start | bytes 1179656 | tf_op jit(solution)/shard_map/ppermute | solution.py:278
  37.2 8.5 %collective-permute-done.1 = f16[768,256]{1,0:T(8,128)(2,1)S(1)} collective-permute-done((f16[768,256]{1,0:T(8,128)(2,1)}, f16[768,256]{1,0:T(8,128)(2,1)S(1)}, u32[]{:S(2)}, u32[]{:S(2)}) %collective-permute-start.1) | collective-permute-done | bytes 393248 | tf_op jit(solution)/shard_map/ppermute | solution.py:278
  45.8 1.4 %fusion.7 = f16[768,256]{1,0:T(8,128)(2,1)S(1)} fusion(f16[768,256]{1,0:T(8,128)(2,1)S(1)} %collective-permute-done.1, f32[3072,256]{1,0:T(8,128)S(1)} %copy-done.4, s32[]{:T(128)S(6)} %select_n.57, bf16[1536,256]{1,0:T(8,128)(2,1)} %collective-permute-done, s32[]{:T(128)S(6)} %select_n.61, bf16[1,3,3072,256]{3,2,1,0:T(8,128)(2,1)} %param.13, s32[]{:T(128)S(6)} %select_n.59), kind=kLoop, calls=%fused_computation.15 | loop fusion | flops 1966080 | bytes 2359308 | tf_op jit(solution)/shard_map/convert_element_type | solution.py:264
  47.1 0.0 collective-permute-done.4.refs_3_.refs_6_
  47.2 0.0 collective-permute-done.3.refs_2_.refs_5_
  47.2 0.0 collective-permute-done.2.refs_1_.refs_4_
  47.2 3.4 %collective-permute-start.5 = (f16[768,256]{1,0:T(8,128)(2,1)S(1)}, f16[768,256]{1,0:T(8,128)(2,1)S(1)}, u32[]{:S(2)}, u32[]{:S(2)}) collective-permute-start(f16[768,256]{1,0:T(8,128)(2,1)S(1)} %fusion.7), channel_id=1, source_target_pairs={{0,64},{16,80},{32,96},{48,112},{64,0},{80,16},{96,32},{112,48},{1... | collective-permute-start | bytes 1179656 | tf_op jit(solution)/shard_map/ppermute | solution.py:281
  50.6 1.2 collective-permute-start.9
  51.7 0.0 collective-permute-start.12
  51.7 0.2 collective-permute-start.11
  51.9 6.1 %collective-permute-done.5 = f16[768,256]{1,0:T(8,128)(2,1)S(1)} collective-permute-done((f16[768,256]{1,0:T(8,128)(2,1)S(1)}, f16[768,256]{1,0:T(8,128)(2,1)S(1)}, u32[]{:S(2)}, u32[]{:S(2)}) %collective-permute-start.5) | collective-permute-done | bytes 393248 | tf_op jit(solution)/shard_map/ppermute | solution.py:281
  58.1 0.2 add_convert_fusion
  58.2 0.0 collective-permute-done.6.refs_4_.refs_7_.refs_1_
  58.2 8.3 %blocks.4.refs_9_ = bf16[512,512]{1,0:T(8,128)(2,1)} custom-call(s32[1]{0:T(128)} %bitcast.6.frag_ref, bf16[2,128,3072]{2,1,0:T(8,128)(2,1)} %norm.1.refs_0_.refs_3_, bf16[2,128,3072]{2,1,0:T(8,128)(2,1)} %collective-permute-done.2.refs_1_.refs_4_, bf16[2,128,3072]{2,1,0:T(8,128)(2,1)} %collective-permute-done.3.refs_2_.refs_5_, ...), custom_call_target="tpu_custom_call" | custom-call | flops 1 | bytes 1 | tf_op jit(solution)/shard_map/blocks/pallas_call | solution.py:187
  66.6 2.6 %collective-permute-start.7 = (f16[768,256]{1,0:T(8,128)(2,1)S(1)}, f16[768,256]{1,0:T(8,128)(2,1)S(1)}, u32[]{:S(2)}, u32[]{:S(2)}) collective-permute-start(f16[768,256]{1,0:T(8,128)(2,1)S(1)} %add_convert_fusion), channel_id=1, source_target_pairs={{0,48},{16,32},{32,16},{48,0},{64,112},{80,96},{96,80},{112,64},{1... | collective-permute-start | bytes 1179656 | tf_op jit(solution)/shard_map/ppermute | solution.py:290
  69.1 5.8 %collective-permute-done.7 = f16[768,256]{1,0:T(8,128)(2,1)S(1)} collective-permute-done((f16[768,256]{1,0:T(8,128)(2,1)S(1)}, f16[768,256]{1,0:T(8,128)(2,1)S(1)}, u32[]{:S(2)}, u32[]{:S(2)}) %collective-permute-start.7) | collective-permute-done | bytes 393248 | tf_op jit(solution)/shard_map/ppermute | solution.py:290
  74.9 0.3 maximum_select_fusion.1
  75.2 0.1 collective-permute-start.8
  75.3 0.0 collective-permute-done.9.refs_1_
  75.3 6.7 %collective-permute-start.10 = (bf16[2,128,3072]{2,1,0:T(8,128)(2,1)}, bf16[2,128,3072]{2,1,0:T(8,128)(2,1)S(1)}, u32[]{:S(2)}, u32[]{:S(2)}) collective-permute-start(bf16[2,128,3072]{2,1,0:T(8,128)(2,1)} %collective-permute-done.9.refs_1_), channel_id=1, source_target_pairs={{0,2},{1,7},{2,4},{3,1},{4,6},{5,3},{6,0},{7,5},{8,10},{9,15},{10,... | collective-permute-start | bytes 4718600 | tf_op jit(solution)/shard_map/ppermute | solution.py:293
  82.0 9.1 %collective-permute-done.12.refs_2_ = bf16[2,128,3072]{2,1,0:T(8,128)(2,1)} collective-permute-done((bf16[2,128,3072]{2,1,0:T(8,128)(2,1)}, bf16[2,128,3072]{2,1,0:T(8,128)(2,1)}, u32[]{:S(2)}, u32[]{:S(2)}) %collective-permute-start.12) | collective-permute-done | bytes 1572896 | tf_op jit(solution)/shard_map/ppermute | solution.py:284
  91.1 0.0 collective-permute-done.11.refs_0_
  91.1 14.5 %blocks.5 = (f32[256,3072]{1,0:T(8,128)}, f32[256,3072]{1,0:T(8,128)}) custom-call(s32[1]{0:T(128)} %bitcast.6.frag_ref, bf16[2,128,3072]{2,1,0:T(8,128)(2,1)} %collective-permute-done.11.refs_0_, bf16[2,128,3072]{2,1,0:T(8,128)(2,1)} %collective-permute-done.9.refs_1_, bf16[2,128,3072]{2,1,0:T(8,128)(2,1)} %collective-permute-done.12.refs_2_, ...), custom_call_target="tpu_custom_call" | custom-call | flops 1 | bytes 1 | tf_op jit(solution)/shard_map/blocks/pallas_call | solution.py:187
  105.6 0.0 copy-start.1
  105.6 0.0 collective-permute-done.8
  105.7 0.0 slice-done
  105.7 0.0 slice-done.1
  105.7 5.9 %fusion = (f32[3072,256]{1,0:T(8,128)S(1)}, f32[3072,256]{1,0:T(8,128)}, f32[3072,256]{1,0:T(8,128)}) fusion(bf16[1,3,3072,256]{3,2,1,0:T(8,128)(2,1)S(1)} %bitcast.23, s32[]{:T(128)S(6)} %select_n.59, f32[3072,256]{1,0:T(8,128)} %param.16, f16[1536,256]{1,0:T(8,128)(2,1)S(1)} %maximum_select_fusion.1, f16[1536,256]{1,0:T(8,128)(2,1)} %collective-permute-done.8, ...), kind=kLoop, calls=%fused_computation.1 | loop fusion | flops 11010048 | bytes 18874372 | tf_op jit(solution)/shard_map/add | solution.py:299
  111.6 0.0 collective-permute-done.10.refs_0_
  111.6 0.0 copy-done.1
  111.6 3.7 %blocks.7 = bf16[256,3072]{1,0:T(8,128)(2,1)S(1)} custom-call(s32[1]{0:T(128)} %bitcast.6.frag_ref, bf16[2,128,3072]{2,1,0:T(8,128)(2,1)S(1)} %collective-permute-done.10.refs_0_, bf16[3,3072,256]{2,1,0:T(8,128)(2,1)} %collective-permute-done.6.refs_4_.refs_7_.refs_1_, f32[256,3072]{1,0:T(8,128)S(1)} %copy-done.1), custom_call_target="tpu_custom_call" | custom-call | flops 1 | bytes 1 | tf_op jit(solution)/shard_map/blocks/pallas_call | solution.py:187
  115.2 0.0 copy-start.2
  115.3 0.0 copy-start.3
  115.3 2.9 %collective-permute-start.13 = (bf16[256,3072]{1,0:T(8,128)(2,1)S(1)}, bf16[256,3072]{1,0:T(8,128)(2,1)S(1)}, u32[]{:S(2)}, u32[]{:S(2)}) collective-permute-start(bf16[256,3072]{1,0:T(8,128)(2,1)S(1)} %blocks.7), channel_id=1, source_target_pairs={{0,1},{1,0},{2,3},{3,2},{4,5},{5,4},{6,7},{7,6},{8,9},{9,8},{10,11... | collective-permute-start | bytes 4718600 | tf_op jit(solution)/shard_map/ppermute | solution.py:305
  118.2 2.2 %blocks.6.own_ref = f32[256,3072]{1,0:T(8,128)S(1)} custom-call(s32[1]{0:T(128)} %bitcast.6.frag_ref, bf16[2,128,3072]{2,1,0:T(8,128)(2,1)S(1)} %collective-permute-done.10.refs_0_, bf16[3,3072,256]{2,1,0:T(8,128)(2,1)S(1)} %bitcast.24, f32[256,3072]{1,0:T(8,128)S(1)} %copy-done), custom_call_target="tpu_custom_call", output_to_operand_aliasing={{}: (3, {})} | custom-call | flops 1 | bytes 1 | tf_op jit(solution)/shard_map/blocks/pallas_call | solution.py:187
  120.4 0.8 collective-permute-done.13.other_ref
  121.2 4.2 %adam.1 = bf16[3072,256]{1,0:T(8,128)(2,1)} custom-call(f32[256,3072]{1,0:T(8,128)S(1)} %blocks.6.own_ref, bf16[256,3072]{1,0:T(8,128)(2,1)S(1)} %collective-permute-done.13.other_ref, f32[3072,256]{1,0:T(8,128)S(1)} %bitcast.25, f32[3072,256]{1,0:T(8,128)S(1)} %bitcast.26, f32[3072,256]{1,0:T(8,128)S(1)} %get-tuple-element.17.mixed_ref), custom_call_target="tpu_custom_call" | custom-call | flops 1 | bytes 1 | tf_op jit(solution)/shard_map/adam/pallas_call | solution.py:223
  (7 shorter events, 0.0 us)
Async XLA Ops:
  0.6 32.0 %copy-start.4 = (f32[3072,256]{1,0:T(8,128)S(1)}, f32[3072,256]{1,0:T(8,128)}, u32[]{:S(2)}) copy-start(f32[3072,256]{1,0:T(8,128)} %param.16) | copy-start | bytes 9437188
  0.6 57.6 %collective-permute-start.6 = (bf16[3,3072,256]{2,1,0:T(8,128)(2,1)}, bf16[3,3072,256]{2,1,0:T(8,128)(2,1)}, u32[]{:S(2)}, u32[]{:S(2)}) collective-permute-start(bf16[3,3072,256]{2,1,0:T(8,128)(2,1)} %bitcast.19), channel_id=1, source_target_pairs={{0,1},{1,0},{2,3},{3,2},{4,5},{5,4},{6,7},{7,6},{8,9},{9,8},{10,11... | collective-permute-start | bytes 14155784 | tf_op jit(solution)/shard_map/ppermute | solution.py:243
  6.0 41.1 %collective-permute-start.4 = (bf16[2,128,3072]{2,1,0:T(8,128)(2,1)}, bf16[2,128,3072]{2,1,0:T(8,128)(2,1)}, u32[]{:S(2)}, u32[]{:S(2)}) collective-permute-start(bf16[2,128,3072]{2,1,0:T(8,128)(2,1)} %norm.1.refs_0_.refs_3_), channel_id=1, source_target_pairs={{0,8},{1,9},{2,10},{3,11},{4,12},{5,13},{6,14},{7,15},{8,0},{9,1},... | collective-permute-start | bytes 4718600 | tf_op jit(solution)/shard_map/ppermute | solution.py:267
  7.9 39.2 %collective-permute-start.3 = (bf16[2,128,3072]{2,1,0:T(8,128)(2,1)}, bf16[2,128,3072]{2,1,0:T(8,128)(2,1)}, u32[]{:S(2)}, u32[]{:S(2)}) collective-permute-start(bf16[2,128,3072]{2,1,0:T(8,128)(2,1)} %norm.1.refs_0_.refs_3_), channel_id=1, source_target_pairs={{0,7},{1,2},{2,1},{3,4},{4,3},{5,6},{6,5},{7,0},{8,15},{9,10},{10,... | collective-permute-start | bytes 4718600 | tf_op jit(solution)/shard_map/ppermute | solution.py:268
  9.4 37.8 %collective-permute-start.2 = (bf16[2,128,3072]{2,1,0:T(8,128)(2,1)}, bf16[2,128,3072]{2,1,0:T(8,128)(2,1)}, u32[]{:S(2)}, u32[]{:S(2)}) collective-permute-start(bf16[2,128,3072]{2,1,0:T(8,128)(2,1)} %norm.1.refs_0_.refs_3_), channel_id=1, source_target_pairs={{0,2},{1,7},{2,4},{3,1},{4,6},{5,3},{6,0},{7,5},{8,10},{9,15},{10,... | collective-permute-start | bytes 4718600 | tf_op jit(solution)/shard_map/ppermute | solution.py:266
  13.5 19.2 %collective-permute-start = (bf16[1536,256]{1,0:T(8,128)(2,1)}, bf16[1536,256]{1,0:T(8,128)(2,1)}, u32[]{:S(2)}, u32[]{:S(2)}) collective-permute-start(bf16[1536,256]{1,0:T(8,128)(2,1)} %dynamic-slice_bitcast_fusion), channel_id=1, source_target_pairs={{0,16},{16,0},{32,48},{48,32},{64,80},{80,64},{96,112},{112,96},{1... | collective-permute-start | bytes 2359304 | tf_op jit(solution)/shard_map/ppermute | solution.py:269
  34.7 11.0 %collective-permute-start.1 = (f16[768,256]{1,0:T(8,128)(2,1)}, f16[768,256]{1,0:T(8,128)(2,1)S(1)}, u32[]{:S(2)}, u32[]{:S(2)}) collective-permute-start(f16[768,256]{1,0:T(8,128)(2,1)} %fusion.3), channel_id=1, source_target_pairs={{0,48},{16,32},{32,16},{48,0},{64,112},{80,96},{96,80},{112,64},{1... | collective-permute-start | bytes 1179656 | tf_op jit(solution)/shard_map/ppermute | solution.py:278
  47.2 10.9 %collective-permute-start.5 = (f16[768,256]{1,0:T(8,128)(2,1)S(1)}, f16[768,256]{1,0:T(8,128)(2,1)S(1)}, u32[]{:S(2)}, u32[]{:S(2)}) collective-permute-start(f16[768,256]{1,0:T(8,128)(2,1)S(1)} %fusion.7), channel_id=1, source_target_pairs={{0,64},{16,80},{32,96},{48,112},{64,0},{80,16},{96,32},{112,48},{1... | collective-permute-start | bytes 1179656 | tf_op jit(solution)/shard_map/ppermute | solution.py:281
  50.6 24.8 %collective-permute-start.9 = (bf16[2,128,3072]{2,1,0:T(8,128)(2,1)}, bf16[2,128,3072]{2,1,0:T(8,128)(2,1)}, u32[]{:S(2)}, u32[]{:S(2)}) collective-permute-start(bf16[2,128,3072]{2,1,0:T(8,128)(2,1)} %collective-permute-done.4.refs_3_.refs_6_), channel_id=1, source_target_pairs={{0,2},{1,7},{2,4},{3,1},{4,6},{5,3},{6,0},{7,5},{8,10},{9,15},{10,... | collective-permute-start | bytes 4718600 | tf_op jit(solution)/shard_map/ppermute | solution.py:283
  51.7 39.4 %collective-permute-start.12 = (bf16[2,128,3072]{2,1,0:T(8,128)(2,1)}, bf16[2,128,3072]{2,1,0:T(8,128)(2,1)}, u32[]{:S(2)}, u32[]{:S(2)}) collective-permute-start(bf16[2,128,3072]{2,1,0:T(8,128)(2,1)} %collective-permute-done.3.refs_2_.refs_5_), channel_id=1, source_target_pairs={{0,8},{1,9},{2,10},{3,11},{4,12},{5,13},{6,14},{7,15},{8,0},{9,1},... | collective-permute-start | bytes 4718600 | tf_op jit(solution)/shard_map/ppermute | solution.py:284
  51.7 39.4 %collective-permute-start.11 = (bf16[2,128,3072]{2,1,0:T(8,128)(2,1)}, bf16[2,128,3072]{2,1,0:T(8,128)(2,1)}, u32[]{:S(2)}, u32[]{:S(2)}) collective-permute-start(bf16[2,128,3072]{2,1,0:T(8,128)(2,1)} %collective-permute-done.2.refs_1_.refs_4_), channel_id=1, source_target_pairs={{0,2},{1,7},{2,4},{3,1},{4,6},{5,3},{6,0},{7,5},{8,10},{9,15},{10,... | collective-permute-start | bytes 4718600 | tf_op jit(solution)/shard_map/ppermute | solution.py:287
  66.6 8.3 %collective-permute-start.7 = (f16[768,256]{1,0:T(8,128)(2,1)S(1)}, f16[768,256]{1,0:T(8,128)(2,1)S(1)}, u32[]{:S(2)}, u32[]{:S(2)}) collective-permute-start(f16[768,256]{1,0:T(8,128)(2,1)S(1)} %add_convert_fusion), channel_id=1, source_target_pairs={{0,48},{16,32},{32,16},{48,0},{64,112},{80,96},{96,80},{112,64},{1... | collective-permute-start | bytes 1179656 | tf_op jit(solution)/shard_map/ppermute | solution.py:290
  75.2 30.4 %collective-permute-start.8 = (f16[1536,256]{1,0:T(8,128)(2,1)S(1)}, f16[1536,256]{1,0:T(8,128)(2,1)}, u32[]{:S(2)}, u32[]{:S(2)}) collective-permute-start(f16[1536,256]{1,0:T(8,128)(2,1)S(1)} %maximum_select_fusion.1), channel_id=1, source_target_pairs={{0,16},{16,0},{32,48},{48,32},{64,80},{80,64},{96,112},{112,96},{1... | collective-permute-start | bytes 2359304 | tf_op jit(solution)/shard_map/ppermute | solution.py:292
  75.3 36.2 %collective-permute-start.10 = (bf16[2,128,3072]{2,1,0:T(8,128)(2,1)}, bf16[2,128,3072]{2,1,0:T(8,128)(2,1)S(1)}, u32[]{:S(2)}, u32[]{:S(2)}) collective-permute-start(bf16[2,128,3072]{2,1,0:T(8,128)(2,1)} %collective-permute-done.9.refs_1_), channel_id=1, source_target_pairs={{0,2},{1,7},{2,4},{3,1},{4,6},{5,3},{6,0},{7,5},{8,10},{9,15},{10,... | collective-permute-start | bytes 4718600 | tf_op jit(solution)/shard_map/ppermute | solution.py:293
  82.0 23.7 %slice-start = ((s8[4718592]{0:T(1024)(128)(4,1)}), s8[524288]{0:T(1024)(128)(4,1)S(1)}, s32[]{:S(2)}) async-start(s8[4718592]{0:T(1024)(128)(4,1)} %bitcast.22), calls=%async_computation | async-start | bytes 1048576
  82.0 23.7 %slice-start.1 = ((s8[4718592]{0:T(1024)(128)(4,1)}), s8[4194304]{0:T(1024)(128)(4,1)S(1)}, s32[]{:S(2)}) async-start(s8[4718592]{0:T(1024)(128)(4,1)} %bitcast.22), calls=%async_computation.1 | async-start | bytes 8388608
  105.6 5.9 %copy-start.1 = (f32[256,3072]{1,0:T(8,128)S(1)}, f32[256,3072]{1,0:T(8,128)}, u32[]{:S(2)}) copy-start(f32[256,3072]{1,0:T(8,128)} %get-tuple-element.14.refs_2_) | copy-start | bytes 9437188
  111.6 6.6 %copy-start = (f32[256,3072]{1,0:T(8,128)S(1)}, f32[256,3072]{1,0:T(8,128)}, u32[]{:S(2)}) copy-start(f32[256,3072]{1,0:T(8,128)} %get-tuple-element.15.refs_2_) | copy-start | bytes 9437188
  115.2 6.0 %copy-start.2 = (f32[1,3072,256]{2,1,0:T(8,128)S(1)}, f32[1,3072,256]{2,1,0:T(8,128)}, u32[]{:S(2)}) copy-start(f32[1,3072,256]{2,1,0:T(8,128)} %param.14) | copy-start | bytes 9437188
  115.3 6.0 %copy-start.3 = (f32[1,3072,256]{2,1,0:T(8,128)S(1)}, f32[1,3072,256]{2,1,0:T(8,128)}, u32[]{:S(2)}) copy-start(f32[1,3072,256]{2,1,0:T(8,128)} %param.15) | copy-start | bytes 9437188
  115.3 6.0 %collective-permute-start.13 = (bf16[256,3072]{1,0:T(8,128)(2,1)S(1)}, bf16[256,3072]{1,0:T(8,128)(2,1)S(1)}, u32[]{:S(2)}, u32[]{:S(2)}) collective-permute-start(bf16[256,3072]{1,0:T(8,128)(2,1)S(1)} %blocks.7), channel_id=1, source_target_pairs={{0,1},{1,0},{2,3},{3,2},{4,5},{5,4},{6,7},{7,6},{8,9},{9,8},{10,11... | collective-permute-start | bytes 4718600 | tf_op jit(solution)/shard_map/ppermute | solution.py:305

commit v3 on v0

v3 whole, which is shorter than its diff:
```python
import functools

import jax
import jax.numpy as jnp
from jax import lax
from jax.experimental import pallas as pl
from jax.experimental.pallas import tpu as pltpu
from jax.sharding import PartitionSpec as P

beta_one = 0.9
beta_two = 0.95
adam_eps = 1e-08
inner_lr = 0.02
outer_lr = 0.7
nesterov_mu = 0.9
mix_alpha = 0.5
norm_eps = 1e-05

WIRE_SCALE = float(2**18)

ANY = pl.BlockSpec(memory_space=pl.ANY)
VMEM = pl.BlockSpec(memory_space=pltpu.VMEM)
SMEM = pl.BlockSpec(memory_space=pltpu.SMEM)
MIB = 1024 * 1024
CHEAP = pl.CostEstimate(flops=1, bytes_accessed=1, transcendentals=0)


def fsdp_id(z, y, c):
    return (z % 2) * 8 + (y % 4) * 2 + c


def permutation(to):
    return [(fsdp_id(z, y, c), fsdp_id(*to(z, y, c))) for z in range(2) for y in range(4) for c in range(2)]


STRAIGHT = permutation(lambda z, y, c: (z, y + 1 - 2 * c, c))
CROSSED = permutation(lambda z, y, c: (z, y + 2 * c - 1, 1 - c))
OTHER_Z = permutation(lambda z, y, c: (z + 1, y, c))
SIBLING = permutation(lambda z, y, c: (z, y, 1 - c))


def replica_pairs(first):
    pairs = []
    for r in range(8):
        for i in range(16):
            beside = (r % 4) ^ 1 if (i % 2 == 0) == first else 3 - r % 4
            pairs.append((r * 16 + i, (r // 4 * 4 + beside) * 16 + i))
    return pairs


HALF_PAIR = replica_pairs(True)
QUARTER_PAIR = replica_pairs(False)
OPPOSITE = [(r, r // 4 * 4 + (r + 2) % 4) for r in range(8)]
OTHER_H = [(r, (r + 4) % 8) for r in range(8)]


def norm_kernel(x_ref, c_ref, g_ref, u_ref, x_s, g_s, sems):
    g_in = pltpu.make_async_copy(g_ref, g_s, sems.at[0])
    x_in = pltpu.make_async_copy(x_ref, x_s, sems.at[1])
    c_in = pltpu.make_async_copy(c_ref, u_ref.at[1], sems.at[2])
    for copy in (g_in, x_in, c_in):
        copy.start()
    g_in.wait()
    gain = g_s[...].astype(jnp.float32).reshape(1, -1)
    x_in.wait()
    x = x_s[...].astype(jnp.float32)
    scale = lax.rsqrt(jnp.mean(x * x, axis=1, keepdims=True) + norm_eps)
    u_ref[0] = (x * scale * gain).astype(jnp.bfloat16)
    c_in.wait()


def normed_and_cotangent(x, c, gain):
    return pl.pallas_call(
        norm_kernel,
        out_shape=jax.ShapeDtypeStruct((2, *x.shape), jnp.bfloat16),
        in_specs=[ANY, ANY, ANY],
        out_specs=VMEM,
        scratch_shapes=[
            pltpu.VMEM(x.shape, jnp.bfloat16),
            pltpu.VMEM(gain.shape, jnp.bfloat16),
            pltpu.SemaphoreType.DMA((3,)),
        ],
        compiler_params=pltpu.CompilerParams(vmem_limit_bytes=60 * MIB),
        cost_estimate=CHEAP,
        name="norm",
    )(x, c, gain)


class Loads:
    def __init__(self, frag, sems, ahead):
        self.frag, self.sems, self.ahead = frag, sems, ahead
        self.entries, self.started, self.waited = [], 0, 0

    def add(self, name, source, target, without=None):
        copy = pltpu.make_async_copy(source, target, self.sems.at[len(self.entries)])
        self.entries.append((name, copy, without))

    def unless(self, without, act):
        if without is None:
            act()
        else:
            pl.when(self.frag != without)(act)

    def start(self):
        while self.started < min(self.waited + self.ahead, len(self.entries)):
            _, copy, without = self.entries[self.started]
            self.unless(without, copy.start)
            self.started += 1

    def wait(self, name):
        while self.waited < len(self.entries) and self.entries[self.waited][0] == name:
            _, copy, without = self.entries[self.waited]
            self.unless(without, copy.wait)
            self.waited += 1
            self.start()


def right_side(frag, loads, tag, n_s, c_s, w_s, up_s, dh_s, right):
    def dot(left, i):
        return jnp.dot(left[...], w_s[i], preferred_element_type=jnp.float32)

    loads.wait(("n", tag))
    loads.wait(("gate", tag))
    gate = dot(n_s, 0)
    loads.wait(("up", tag))

    @pl.when(frag != 1)
    def _():
        up_s[...] = dot(n_s, 1)

    loads.wait(("c", tag))
    loads.wait(("down", tag))

    @pl.when(frag != 2)
    def _():
        dh_s[...] = dot(c_s, 2)

    sig = jax.nn.sigmoid(gate)

    @pl.when(frag == 0)
    def _():
        right[...] = (dh_s[...] * up_s[...] * sig * (1.0 + gate * (1.0 - sig))).astype(jnp.bfloat16)

    @pl.when(frag == 1)
    def _():
        right[...] = (dh_s[...] * (gate * sig)).astype(jnp.bfloat16)

    @pl.when(frag == 2)
    def _():
        right[...] = (gate * sig * up_s[...]).astype(jnp.bfloat16)


def forward_kernel(count, frag_ref, *refs):
    blocks, weights, out_ref = refs[:count], refs[count : count + 2], refs[count + 2]
    n_s, c_s, w_s, up_s, dh_s, sems = refs[count + 3 :]
    rows, cols = blocks[0].shape[1], weights[0].shape[2]
    frag = frag_ref[0]
    loads = Loads(frag, sems, count + 4)
    for h, weight in enumerate(weights):
        if h == 0:
            for k, b in enumerate(blocks):
                loads.add(("n", h), b.at[0], n_s.at[pl.ds(k * rows, rows)])
        loads.add(("gate", h), weight.at[0], w_s.at[h, 0])
        loads.add(("up", h), weight.at[1], w_s.at[h, 1], 1)
        if h == 0:
            for k, b in enumerate(blocks):
                loads.add(("c", h), b.at[1], c_s.at[pl.ds(k * rows, rows)], 2)
        loads.add(("down", h), weight.at[2], w_s.at[h, 2], 2)
    loads.start()
    for h in range(2):
        right = out_ref.at[:, h * cols : (h + 1) * cols]
        right_side(frag, loads, h, n_s, c_s, w_s.at[h], up_s, dh_s, right)


def forward(frag, blocks, weights):
    count, rows = len(blocks), len(blocks) * blocks[0].shape[1]
    _, d, cols = weights[0].shape
    return pl.pallas_call(
        functools.partial(forward_kernel, count),
        out_shape=jax.ShapeDtypeStruct((rows, 2 * cols), jnp.bfloat16),
        in_specs=[SMEM] + [ANY] * (count + 2),
        out_specs=VMEM,
        scratch_shapes=[
            pltpu.VMEM((rows, d), jnp.bfloat16),
            pltpu.VMEM((rows, d), jnp.bfloat16),
            pltpu.VMEM((2, 3, d, cols), jnp.bfloat16),
            pltpu.VMEM((rows, cols), jnp.float32),
            pltpu.VMEM((rows, cols), jnp.float32),
            pltpu.SemaphoreType.DMA((2 * count + 6,)),
        ],
        compiler_params=pltpu.CompilerParams(vmem_limit_bytes=60 * MIB),
        cost_estimate=CHEAP,
        name="forward",
    )(frag, *blocks, *weights)


def add_gradient(right_t, left, out, total=None):
    step = 768
    for at in range(0, out.shape[1], step):
        span = slice(at, at + step)
        term = jnp.dot(right_t, left[:, span], preferred_element_type=jnp.float32)
        if total is not None:
            term = total[:, span] + term
        out[:, span] = term.astype(out.dtype)


def gradient_kernel(past, spans, frag_ref, block, *refs):
    old_blocks, rights, refs = refs[:past], refs[past : past + len(spans)], refs[past + len(spans) :]
    weights, held, outs = refs[:2], refs[2:4], refs[4:6]
    n_s, c_s, up_s, dh_s, left_s, right_s, sems = refs[6:]
    rows, cols = block.shape[1], weights[0].shape[2]
    frag = frag_ref[0]
    side = jnp.where(frag == 2, 1, 0)
    loads = Loads(frag, sems, 8)
    for h in range(2):
        if h == 0:
            loads.add(("n", h), block.at[0], n_s)
        loads.add(("gate", h), weights[h].at[0], held[h].at[0])
        loads.add(("up", h), weights[h].at[1], held[h].at[1], 1)
        if h == 0:
            loads.add(("c", h), block.at[1], c_s)
        loads.add(("down", h), weights[h].at[2], held[h].at[2], 2)
        if h == 0:
            for right, (at, size) in zip(rights, spans):
                loads.add("rest", right, right_s.at[pl.ds(at, size)])
            for k, b in enumerate((*old_blocks, block)):
                loads.add("rest", b.at[side], left_s.at[pl.ds(k * rows, rows)])
    loads.start()
    for h in range(2):
        here = slice(h * cols, (h + 1) * cols)
        right_side(frag, loads, h, n_s, c_s, held[h], up_s, dh_s, right_s.at[past * rows :, here])
        loads.wait("rest")
        add_gradient(right_s[:, here].T, left_s, outs[h])


def gradients(frag, block, weights, old_blocks, rights):
    past, rows = len(old_blocks), block.shape[1]
    _, d, cols = weights[0].shape
    spans, at = [], 0
    for right in rights:
        spans.append((at, right.shape[0]))
        at += right.shape[0]
    total = at + rows
    out = pl.pallas_call(
        functools.partial(gradient_kernel, past, tuple(spans)),
        out_shape=[jax.ShapeDtypeStruct((3, d, cols), jnp.bfloat16)] * 2 + [jax.ShapeDtypeStruct((cols, d), jnp.float32)] * 2,
        in_specs=[SMEM] + [ANY] * (past + len(spans) + 3),
        out_specs=[VMEM] * 4,
        scratch_shapes=[
            pltpu.VMEM((rows, d), jnp.bfloat16),
            pltpu.VMEM((rows, d), jnp.bfloat16),
            pltpu.VMEM((rows, cols), jnp.float32),
            pltpu.VMEM((rows, cols), jnp.float32),
            pltpu.VMEM((total, d), jnp.bfloat16),
            pltpu.VMEM((total, 2 * cols), jnp.bfloat16),
            pltpu.SemaphoreType.DMA((past + len(spans) + 9,)),
        ],
        compiler_params=pltpu.CompilerParams(vmem_limit_bytes=20 * MIB),
        cost_estimate=CHEAP,
        name="gradients",
    )(frag, block, *old_blocks, *rights, *weights)
    return out[:2], out[2:]


def step_kernel(halves, frag_ref, block, *refs):
    weights, totals, outs = refs[:halves], refs[halves : 2 * halves], refs[2 * halves : 3 * halves]
    n_s, c_s, up_s, dh_s, right_s, sems = refs[3 * halves :]
    frag = frag_ref[0]
    loads = Loads(frag, sems, 2)
    loads.add(("n", 0), block.at[0], n_s)
    loads.add(("c", 0), block.at[1], c_s)
    loads.start()
    for h in range(halves):
        right_side(frag, loads, h, n_s, c_s, weights[h], up_s, dh_s, right_s)
        right_t = right_s[...].T
        pl.when(frag == 2)(functools.partial(add_gradient, right_t, c_s, outs[h], totals[h]))
        pl.when(frag != 2)(functools.partial(add_gradient, right_t, n_s, outs[h], totals[h]))


def add_block(frag, block, weights, totals, kind=jnp.float32):
    halves, rows = len(weights), block.shape[1]
    _, d, cols = weights[0].shape
    aliases = {2 + halves + h: h for h in range(halves)} if kind == jnp.float32 else {}
    return pl.pallas_call(
        functools.partial(step_kernel, halves),
        out_shape=[jax.ShapeDtypeStruct((cols, d), kind)] * halves,
        in_specs=[SMEM, ANY] + [VMEM] * (2 * halves),
        out_specs=[VMEM] * halves,
        scratch_shapes=[
            pltpu.VMEM((rows, d), jnp.bfloat16),
            pltpu.VMEM((rows, d), jnp.bfloat16),
            pltpu.VMEM((rows, cols), jnp.float32),
            pltpu.VMEM((rows, cols), jnp.float32),
            pltpu.VMEM((rows, cols), jnp.bfloat16),
            pltpu.SemaphoreType.DMA((2,)),
        ],
        input_output_aliases=aliases,
        compiler_params=pltpu.CompilerParams(vmem_limit_bytes=12 * MIB),
        cost_estimate=CHEAP,
        name="block",
    )(frag, block, *weights, *totals)


def adam_kernel(tokens, tile, own_ref, other_ref, m_ref, v_ref, mixed_ref, out_ref, out_s, sems):
    copies = []
    for i in range(m_ref.shape[0] // tile):
        span = slice(i * tile, (i + 1) * tile)
        grad = (own_ref[:, span] + other_ref[:, span].astype(jnp.float32)).T * (1.0 / tokens)
        moment_one = beta_one * m_ref[span, :] + (1.0 - beta_one) * grad
        moment_two = beta_two * v_ref[span, :] + (1.0 - beta_two) * grad * grad
        step_inner = inner_lr * moment_one / (jnp.sqrt(moment_two) + adam_eps)
        out_s[span, :] = (mixed_ref[span, :] - mix_alpha * step_inner).astype(jnp.bfloat16)
        copy = pltpu.make_async_copy(out_s.at[span, :], out_ref.at[span, :], sems.at[i])
        copy.start()
        copies.append(copy)
    for copy in copies:
        copy.wait()


def adam(tokens, own, other, m, v, mixed):
    d, cols = m.shape
    tile = 512
    return pl.pallas_call(
        functools.partial(adam_kernel, tokens, tile),
        out_shape=jax.ShapeDtypeStruct((d, cols), jnp.bfloat16),
        in_specs=[VMEM] * 5,
        out_specs=ANY,
        scratch_shapes=[pltpu.VMEM((d, cols), jnp.bfloat16), pltpu.SemaphoreType.DMA((d // tile,))],
        compiler_params=pltpu.CompilerParams(vmem_limit_bytes=12 * MIB),
        cost_estimate=CHEAP,
        name="adam",
    )(own, other, m, v, mixed)


def after(value, *others):
    return lax.optimization_barrier((value, *others))[0]


def per_device(step, hidden_in, cotangent, norm_gain, weights, adam_m, adam_v, global_frag, outer_mom):
    fragment = step[0] % 3
    frag = fragment.reshape(1)
    w_own = weights[0]
    w_sib = lax.ppermute(w_own, "fsdp", SIBLING)
    w_both = [w_sib, w_own]
    own = normed_and_cotangent(hidden_in[0], cotangent[0], norm_gain)

    straight = functools.partial(lax.ppermute, axis_name="fsdp", perm=STRAIGHT)
    crossed = functools.partial(lax.ppermute, axis_name="fsdp", perm=CROSSED)
    other_z = functools.partial(lax.ppermute, axis_name="fsdp", perm=OTHER_Z)

    x = lax.rem(lax.axis_index("replica"), 4)
    first_core = lax.rem(lax.axis_index("fsdp"), 2) == 0
    inner, upper = lax.rem((x + 1) // 2, 2), x // 2
    h = jnp.where(first_core, inner, upper)
    q = jnp.where(first_core, upper, inner)
    everyone = ("replica", "fsdp")
    d, cols = global_frag.shape
    half, quarter = d // 2, d // 4

    def w_rows(at, size):
        return lax.dynamic_slice(w_own, (fragment, at, 0), (1, size, cols))[0]

    def g_rows(at, size):
        return lax.dynamic_slice(global_frag, (at, 0), (size, cols))

    def ordered(second, first, other):
        return jnp.where(second == 0, jnp.concatenate([first, other]), jnp.concatenate([other, first]))

    def wire(value):
        return (value * (WIRE_SCALE / 8)).astype(jnp.float16)

    near = straight(own)
    z_own = other_z(own)
    cross = crossed(own)
    w_pair = lax.ppermute(after(w_rows((1 - h) * half, half), own), everyone, HALF_PAIR)

    def pair_delta(at):
        base = g_rows(h * half + at, quarter)
        mine = w_rows(h * half + at, quarter).astype(jnp.float32)
        theirs = lax.dynamic_slice_in_dim(w_pair, at, quarter).astype(jnp.float32)
        return (base - mine) + (base - theirs)

    sent = wire(pair_delta((1 - q) * quarter))
    got = lax.ppermute(sent, everyone, QUARTER_PAIR)
    part = wire(pair_delta(q * quarter) + got.astype(jnp.float32) * (8 / WIRE_SCALE))
    z_own, near, part = lax.optimization_barrier((z_own, near, part))
    other = lax.ppermute(part, "replica", OTHER_H)
    z_near = straight(z_own)
    far = straight(near)
    first = [own, near, cross, z_own]
    right = forward(frag, first, w_both)
    other = after(other, right)
    mine = (part.astype(jnp.float32) + other.astype(jnp.float32)).astype(jnp.float16)
    cross, mine = lax.optimization_barrier((cross, mine))
    z_cross = other_z(cross)
    beside, across = lax.ppermute(mine, everyone, QUARTER_PAIR), lax.ppermute(mine, everyone, HALF_PAIR)
    opposite = lax.ppermute(mine, "replica", OPPOSITE)
    z_near = after(z_near, beside)
    z_far = straight(z_near)
    rights = [right, forward(frag, [z_near], w_both)]

    delta = ordered(h, ordered(q, mine, beside), ordered(q, across, opposite)).astype(jnp.float32) * (1 / WIRE_SCALE)
    momentum_new = nesterov_mu * outer_mom + delta
    global_new = global_frag - outer_lr * (delta + nesterov_mu * momentum_new)
    mixed = mix_alpha * w_rows(0, d).astype(jnp.float32) + (1.0 - mix_alpha) * global_new

    held, totals = gradients(frag, after(far, mixed), w_both, [*first, z_near], rights)
    totals = add_block(frag, z_cross, held, totals)
    (grad_sib,) = add_block(frag, z_far, held[:1], totals[:1], jnp.bfloat16)
    grad_sib = lax.ppermute(grad_sib, "fsdp", SIBLING)
    (grad_own,) = add_block(frag, z_far, held[1:], totals[1:])
    tokens_total = hidden_in.shape[1] * lax.axis_size("fsdp")
    merged = adam(tokens_total, grad_own, grad_sib, adam_m[0], adam_v[0], mixed)
    return (global_new, momentum_new, merged[None])


def solution(mesh):
    placed = (
        P(),
        P("replica", "fsdp", None),
        P("replica", "fsdp", None),
        P(),
        P("replica", None, None, "fsdp"),
        P("replica", None, "fsdp"),
        P("replica", None, "fsdp"),
        P(None, "fsdp"),
        P(None, "fsdp"),
    )
    return jax.shard_map(
        per_device,
        mesh=mesh,
        in_specs=placed,
        out_specs=(P(None, "fsdp"), P(None, "fsdp"), P("replica", None, "fsdp")),
        check_vma=False,
    )
```

time: 267 us -> 114 us (0.43); the launches traced: 265 us -> 115 us
  waiting for transfers between devices: 188 us -> 33.9 us
  matrix products: 46.1 us -> 0 us
  Pallas kernels: 0 us -> 39.7 us
  starting transfers between devices: 0.12 us -> 25.9 us
  between operations: 16.2 us -> 1.73 us
  other arithmetic: 14.7 us -> 10.6 us
  local copies, waits for them, and re-layouts: 0.04 us -> 3.34 us
    psum x1 -> x0, waiting for transfers between devices: 94.8 us -> none  [outer_update(): total = lax.psum(local_delta, 'replica')]
    all_gather x2 -> x0, waiting for transfers between devices: 92.6 us -> none  [the longest x1 62.4 us: per_device(): normed_rows = lax.all_gather(normed, 'fsdp', axis=0, tiled=True)]
    dot_general x3 -> x0, matrix products: 46.1 us -> none  [the longest x1 26.5 us: per_device(): lax.dot_general(left, right, (((0,), (0,)), ((), ())), preferred_element_...]
    pallas_call x0 -> x8, Pallas kernels: none -> 39.7 us  [the longest x2 15.4 us: forward(): pl.pallas_call(functools.partial(forward_kernel, count), out_shape=jax.Sh...]
    ppermute x0 -> x15, waiting for transfers between devices: none -> 33.9 us  [the longest x1 10.2 us: per_device(): lax.ppermute(after(w_rows((1 - h) * half, half), own), everyone, HALF_PAIR)]
    ppermute x0 -> x15, starting transfers between devices: none -> 25.9 us  [the longest x1 5.29 us: per_device(): grad_sib = lax.ppermute(grad_sib, 'fsdp', SIBLING)]
    sub x2 -> x0, other arithmetic: 10.8 us -> none  [the longest x1 6.48 us: nesterov(): return (global_part - outer_lr * (delta + nesterov_mu * mom_next), mom_next)]
    add x0 -> x1, other arithmetic: none -> 5.88 us  [per_device(): mix_alpha * w_rows(0, d).astype(jnp.float32)]
  transfers between devices with their start and end apart: 3 -> 15, of which waited for: 3 -> 8; matrix products, arithmetic and copies ran while one was open for 8% -> 11% of each run, Pallas kernels for 0% -> 30%
where the time goes in v3:
time: 114 us; the launch traced here: 115 us
  Pallas kernels  39.7 us (35%)
  waiting for transfers between devices  33.9 us (30%)
  starting transfers between devices  25.9 us (23%)
  other arithmetic  10.6 us (9%)
  local copies, waits for them, and re-layouts  3.34 us (3%)
  between operations  1.73 us (2%)
    pallas_call x2, Pallas kernels, forward(): pl.pallas_call(functools.partial(forward_kernel, count), out_shape=jax.Sh...  15.4 us
    ppermute x1, waiting for transfers between devices, per_device(): lax.ppermute(after(w_rows((1 - h) * half, half), own), everyone, HALF_PAIR)  10.2 us
    pallas_call x3, Pallas kernels, add_block(): pl.pallas_call(functools.partial(step_kernel, halves), out_shape=[jax.Sha...  9.68 us
    pallas_call x1, Pallas kernels, gradients(): pl.pallas_call(functools.partial(gradient_kernel, past, tuple(spans)), ou...  8.63 us
    ppermute x1, waiting for transfers between devices, per_device(): got = lax.ppermute(sent, everyone, QUARTER_PAIR)  7.23 us
    add x1, other arithmetic, per_device(): mix_alpha * w_rows(0, d).astype(jnp.float32)  5.88 us
    ppermute x1, waiting for transfers between devices, per_device(): z_own = other_z(own)  5.73 us
    ppermute x1, starting transfers between devices, per_device(): grad_sib = lax.ppermute(grad_sib, 'fsdp', SIBLING)  5.29 us
  transfers between devices with their start and end apart: 15, of which 8 were waited for; matrix products, arithmetic and copies ran while one was open for 11% of the time, Pallas kernels for 30%

profile of v3, /device:TPU:1, one launch (start us, length us, event | category | flops | bytes accessed | tf_op | source)
XLA Modules:
  0.0 115.1 jit_solution(3049219430407893337)
XLA Ops:
  0.6 1.5 %collective-permute-start.6 = (bf16[3,3072,256]{2,1,0:T(8,128)(2,1)}, bf16[3,3072,256]{2,1,0:T(8,128)(2,1)}, u32[]{:S(2)}, u32[]{:S(2)}) collective-permute-start(bf16[3,3072,256]{2,1,0:T(8,128)(2,1)} %bitcast.19), channel_id=1, source_target_pairs={{0,1},{1,0},{2,3},{3,2},{4,5},{5,4},{6,7},{7,6},{8,9},{9,8},{10,11... | collective-permute-start | bytes 14155784 | tf_op jit(solution)/shard_map/ppermute | solution.py:343
  2.1 2.7 %norm.1.refs_0_ = bf16[2,128,3072]{2,1,0:T(8,128)(2,1)} custom-call(bf16[128,3072]{1,0:T(8,128)(2,1)} %bitcast.28, bf16[128,3072]{1,0:T(8,128)(2,1)} %bitcast.29, bf16[3072]{0:T(1024)(128)(2,1)} %g_ref.1), custom_call_target="tpu_custom_call" | custom-call | flops 1 | bytes 1 | tf_op jit(solution)/shard_map/norm/pallas_call | solution.py:73
  4.9 1.8 %collective-permute-start.1 = (bf16[2,128,3072]{2,1,0:T(8,128)(2,1)}, bf16[2,128,3072]{2,1,0:T(8,128)(2,1)S(1)}, u32[]{:S(2)}, u32[]{:S(2)}) collective-permute-start(bf16[2,128,3072]{2,1,0:T(8,128)(2,1)} %norm.1.refs_0_), channel_id=1, source_target_pairs={{0,8},{1,9},{2,10},{3,11},{4,12},{5,13},{6,14},{7,15},{8,0},{9,1},... | collective-permute-start | bytes 4718600 | tf_op jit(solution)/shard_map/ppermute | solution.py:373
  6.7 2.7 %collective-permute-start.2 = (bf16[2,128,3072]{2,1,0:T(8,128)(2,1)}, bf16[2,128,3072]{2,1,0:T(8,128)(2,1)S(1)}, u32[]{:S(2)}, u32[]{:S(2)}) collective-permute-start(bf16[2,128,3072]{2,1,0:T(8,128)(2,1)} %norm.1.refs_0_), channel_id=1, source_target_pairs={{0,2},{1,7},{2,4},{3,1},{4,6},{5,3},{6,0},{7,5},{8,10},{9,15},{10,... | collective-permute-start | bytes 4718600 | tf_op jit(solution)/shard_map/ppermute | solution.py:372
  10.1 2.1 %dynamic-slice_bitcast_fusion = bf16[1536,256]{1,0:T(8,128)(2,1)} fusion(bf16[1,3,3072,256]{3,2,1,0:T(8,128)(2,1)} %param.13, s32[]{:T(128)S(6)} %select_n.71, s32[]{:T(128)S(6)} %select_n.72), kind=kLoop, calls=%fused_computation.18 | loop fusion | bytes 1572872 | tf_op jit(solution)/shard_map/squeeze | solution.py:361
  12.2 2.5 %collective-permute-start.3 = (bf16[1536,256]{1,0:T(8,128)(2,1)}, bf16[1536,256]{1,0:T(8,128)(2,1)}, u32[]{:S(2)}, u32[]{:S(2)}) collective-permute-start(bf16[1536,256]{1,0:T(8,128)(2,1)} %dynamic-slice_bitcast_fusion), channel_id=1, source_target_pairs={{0,16},{1,49},{2,18},{3,51},{4,20},{5,53},{6,22},{7,55},{8,24},{9,... | collective-permute-start | bytes 2359304 | tf_op jit(solution)/shard_map/ppermute | solution.py:375
  14.7 0.0 collective-permute-start
  14.7 10.2 %collective-permute-done.3 = bf16[1536,256]{1,0:T(8,128)(2,1)} collective-permute-done((bf16[1536,256]{1,0:T(8,128)(2,1)}, bf16[1536,256]{1,0:T(8,128)(2,1)}, u32[]{:S(2)}, u32[]{:S(2)}) %collective-permute-start.3) | collective-permute-done | bytes 786464 | tf_op jit(solution)/shard_map/ppermute | solution.py:375
  24.9 2.3 %fusion.3 = f16[768,256]{1,0:T(8,128)(2,1)} fusion(f32[3072,256]{1,0:T(8,128)} %param.16, s32[]{:T(128)S(6)} %select_n.74, bf16[1536,256]{1,0:T(8,128)(2,1)} %collective-permute-done.3, s32[]{:T(128)S(6)} %select_n.75, bf16[1,3,3072,256]{3,2,1,0:T(8,128)(2,1)} %param.13, s32[]{:T(128)S(6)} %select_n.71), kind=kLoop, calls=%fused_computation.11 | loop fusion | flops 1376256 | bytes 1966092 | tf_op jit(solution)/shard_map/convert_element_type | solution.py:370
  27.1 0.0 collective-permute-start.4
  27.1 7.2 %collective-permute-done.4 = f16[768,256]{1,0:T(8,128)(2,1)S(1)} collective-permute-done((f16[768,256]{1,0:T(8,128)(2,1)}, f16[768,256]{1,0:T(8,128)(2,1)S(1)}, u32[]{:S(2)}, u32[]{:S(2)}) %collective-permute-start.4) | collective-permute-done | bytes 393248 | tf_op jit(solution)/shard_map/ppermute | solution.py:384
  34.4 1.6 %fusion.7 = f16[768,256]{1,0:T(8,128)(2,1)S(1)} fusion(f16[768,256]{1,0:T(8,128)(2,1)S(1)} %collective-permute-done.4, f32[3072,256]{1,0:T(8,128)} %param.16, s32[]{:T(128)S(6)} %select_n.69, bf16[1536,256]{1,0:T(8,128)(2,1)} %collective-permute-done.3, s32[]{:T(128)S(6)} %select_n.73, bf16[1,3,3072,256]{3,2,1,0:T(8,128)(2,1)} %param.13, s32[]{:T(128)S(6)} %select_n.71), kind=kLoop, calls=%fused_computation.16 | loop fusion | flops 1966080 | bytes 2359308 | tf_op jit(solution)/shard_map/convert_element_type | solution.py:370
  36.0 5.7 %collective-permute-done.1.refs_3_ = bf16[2,128,3072]{2,1,0:T(8,128)(2,1)S(1)} collective-permute-done((bf16[2,128,3072]{2,1,0:T(8,128)(2,1)}, bf16[2,128,3072]{2,1,0:T(8,128)(2,1)S(1)}, u32[]{:S(2)}, u32[]{:S(2)}) %collective-permute-start.1) | collective-permute-done | bytes 1572896 | tf_op jit(solution)/shard_map/ppermute | solution.py:373
  41.7 0.0 collective-permute-done.2.refs_1_
  41.7 2.7 %collective-permute-start.10 = (bf16[2,128,3072]{2,1,0:T(8,128)(2,1)S(1)}, bf16[2,128,3072]{2,1,0:T(8,128)(2,1)}, u32[]{:S(2)}, u32[]{:S(2)}) collective-permute-start(bf16[2,128,3072]{2,1,0:T(8,128)(2,1)S(1)} %collective-permute-done.1.refs_3_), channel_id=1, source_target_pairs={{0,2},{1,7},{2,4},{3,1},{4,6},{5,3},{6,0},{7,5},{8,10},{9,15},{10,... | collective-permute-start | bytes 4718600 | tf_op jit(solution)/shard_map/ppermute | solution.py:388
  44.5 3.3 %collective-permute-start.5 = (f16[768,256]{1,0:T(8,128)(2,1)S(1)}, f16[768,256]{1,0:T(8,128)(2,1)S(1)}, u32[]{:S(2)}, u32[]{:S(2)}) collective-permute-start(f16[768,256]{1,0:T(8,128)(2,1)S(1)} %fusion.7), channel_id=1, source_target_pairs={{0,64},{16,80},{32,96},{48,112},{64,0},{80,16},{96,32},{112,48},{1... | collective-permute-start | bytes 1179656 | tf_op jit(solution)/shard_map/ppermute | solution.py:387
  47.8 0.0 collective-permute-done.refs_2_
  47.8 9.7 %forward.2.refs_5_ = bf16[512,512]{1,0:T(8,128)(2,1)} custom-call(s32[1]{0:T(128)} %bitcast.6.frag_ref, bf16[2,128,3072]{2,1,0:T(8,128)(2,1)} %norm.1.refs_0_, bf16[2,128,3072]{2,1,0:T(8,128)(2,1)} %copy-done.3, bf16[2,128,3072]{2,1,0:T(8,128)(2,1)} %collective-permute-done.refs_2_, bf16[2,128,3072]{2,1,0:T(8,128)(2,1)} %copy-done.1, ...), custom_call_target="tpu_custom_call" | custom-call | flops 1 | bytes 1 | tf_op jit(solution)/shard_map/forward/pallas_call | solution.py:178
  57.5 0.0 collective-permute-done.5
  57.5 0.1 add_convert_fusion
  57.6 1.3 %collective-permute-start.7 = (f16[768,256]{1,0:T(8,128)(2,1)S(1)}, f16[768,256]{1,0:T(8,128)(2,1)S(1)}, u32[]{:S(2)}, u32[]{:S(2)}) collective-permute-start(f16[768,256]{1,0:T(8,128)(2,1)S(1)} %add_convert_fusion), channel_id=1, source_target_pairs={{0,48},{1,17},{2,50},{3,19},{4,52},{5,21},{6,54},{7,23},{8,56},{9,... | collective-permute-start | bytes 1179656 | tf_op jit(solution)/shard_map/ppermute | solution.py:396
  58.9 1.8 %collective-permute-start.8 = (f16[768,256]{1,0:T(8,128)(2,1)S(1)}, f16[768,256]{1,0:T(8,128)(2,1)S(1)}, u32[]{:S(2)}, u32[]{:S(2)}) collective-permute-start(f16[768,256]{1,0:T(8,128)(2,1)S(1)} %add_convert_fusion), channel_id=1, source_target_pairs={{0,16},{1,49},{2,18},{3,51},{4,20},{5,53},{6,22},{7,55},{8,24},{9,... | collective-permute-start | bytes 1179656 | tf_op jit(solution)/shard_map/ppermute | solution.py:396
  60.7 0.6 collective-permute-start.9
  61.4 0.5 collective-permute-start.12
  61.9 1.3 %collective-permute-start.13 = (bf16[2,128,3072]{2,1,0:T(8,128)(2,1)}, bf16[2,128,3072]{2,1,0:T(8,128)(2,1)}, u32[]{:S(2)}, u32[]{:S(2)}) collective-permute-start(bf16[2,128,3072]{2,1,0:T(8,128)(2,1)} %collective-permute-done.refs_2_), channel_id=1, source_target_pairs={{0,8},{1,9},{2,10},{3,11},{4,12},{5,13},{6,14},{7,15},{8,0},{9,1},... | collective-permute-start | bytes 4718600 | tf_op jit(solution)/shard_map/ppermute | solution.py:395
  63.2 2.8 %collective-permute-done.7 = f16[768,256]{1,0:T(8,128)(2,1)S(1)} collective-permute-done((f16[768,256]{1,0:T(8,128)(2,1)S(1)}, f16[768,256]{1,0:T(8,128)(2,1)S(1)}, u32[]{:S(2)}, u32[]{:S(2)}) %collective-permute-start.7) | collective-permute-done | bytes 393248 | tf_op jit(solution)/shard_map/ppermute | solution.py:396
  66.0 0.6 collective-permute-start.11
  66.6 5.7 %forward.3.refs_6_ = bf16[128,512]{1,0:T(8,128)(2,1)} custom-call(s32[1]{0:T(128)} %bitcast.6.frag_ref, bf16[2,128,3072]{2,1,0:T(8,128)(2,1)} %collective-permute-done.10.refs_0_.refs_4_, bf16[3,3072,256]{2,1,0:T(8,128)(2,1)} %collective-permute-done.6.refs_4_.refs_1_.refs_7_, bf16[3,3072,256]{2,1,0:T(8,128)(2,1)} %bitcast.21), custom_call_target="tpu_custom_call" | custom-call | flops 1 | bytes 1 | tf_op jit(solution)/shard_map/forward/pallas_call | solution.py:178
  72.3 0.0 copy-start.9
  72.3 0.3 maximum_select_fusion.1
  72.6 5.2 %collective-permute-done.8 = f16[768,256]{1,0:T(8,128)(2,1)S(1)} collective-permute-done((f16[768,256]{1,0:T(8,128)(2,1)S(1)}, f16[768,256]{1,0:T(8,128)(2,1)S(1)}, u32[]{:S(2)}, u32[]{:S(2)}) %collective-permute-start.8) | collective-permute-done | bytes 393248 | tf_op jit(solution)/shard_map/ppermute | solution.py:396
  77.8 0.9 collective-permute-done.9
  78.8 0.3 maximum_select_fusion.2
  79.1 0.0 slice-start.1
  79.1 0.0 copy-start
  79.2 5.9 %fusion = (f32[3072,256]{1,0:T(8,128)S(1)}, f32[3072,256]{1,0:T(8,128)}, f32[3072,256]{1,0:T(8,128)}) fusion(bf16[1,3,3072,256]{3,2,1,0:T(8,128)(2,1)} %param.13, s32[]{:T(128)S(6)} %select_n.71, f32[3072,256]{1,0:T(8,128)S(1)} %copy-done.9, f16[1536,256]{1,0:T(8,128)(2,1)S(1)} %maximum_select_fusion.1, f16[1536,256]{1,0:T(8,128)(2,1)S(1)} %maximum_select_fusion.2, ...), kind=kLoop, calls=%fused_computation.1 | loop fusion | flops 11010048 | bytes 18874372 | tf_op jit(solution)/shard_map/add | solution.py:405
  85.0 0.0 collective-permute-done.12.block
  85.1 1.1 copy-done.4
  86.2 0.1 copy-done.7
  86.3 0.0 copy-done.8
  86.3 8.6 %gradients.1 = (bf16[3,3072,256]{2,1,0:T(8,128)(2,1)S(1)}, bf16[3,3072,256]{2,1,0:T(8,128)(2,1)S(1)}, f32[256,3072]{1,0:T(8,128)S(1)}, f32[256,3072]{1,0:T(8,128)S(1)}) custom-call(s32[1]{0:T(128)} %bitcast.6.frag_ref, bf16[2,128,3072]{2,1,0:T(8,128)(2,1)} %collective-permute-done.12.block, bf16[2,128,3072]{2,1,0:T(8,128)(2,1)S(1)} %copy-done, ...), custom_call_target="tpu_custom_call" | custom-call | flops 1 | bytes 1 | tf_op jit(solution)/shard_map/gradients/pallas_call | solution.py:244
  94.9 0.9 collective-permute-done.13.block
  95.9 5.3 %block.3 = (f32[256,3072]{1,0:T(8,128)S(1)}, f32[256,3072]{1,0:T(8,128)S(1)}) custom-call(s32[1]{0:T(128)} %bitcast.6.frag_ref, bf16[2,128,3072]{2,1,0:T(8,128)(2,1)} %collective-permute-done.13.block, bf16[3,3072,256]{2,1,0:T(8,128)(2,1)S(1)} %get-tuple-element.28.refs_0_, ...), custom_call_target="tpu_custom_call", output_to_operand_aliasing={{0}: (4, {}), {1}: (5, {})} | custom-call | flops 1 | bytes 1 | tf_op jit(solution)/shard_map/block/pallas_call | solution.py:284
  101.2 2.1 %block.5 = bf16[256,3072]{1,0:T(8,128)(2,1)S(1)} custom-call(s32[1]{0:T(128)} %bitcast.6.frag_ref, bf16[2,128,3072]{2,1,0:T(8,128)(2,1)S(1)} %collective-permute-done.11.block, bf16[3,3072,256]{2,1,0:T(8,128)(2,1)S(1)} %get-tuple-element.28.refs_0_, f32[256,3072]{1,0:T(8,128)S(1)} %get-tuple-element.32.refs_1_), custom_call_target="tpu_custom_call" | custom-call | flops 1 | bytes 1 | tf_op jit(solution)/shard_map/block/pallas_call | solution.py:284
  103.4 5.3 %collective-permute-start.14 = (bf16[256,3072]{1,0:T(8,128)(2,1)S(1)}, bf16[256,3072]{1,0:T(8,128)(2,1)S(1)}, u32[]{:S(2)}, u32[]{:S(2)}) collective-permute-start(bf16[256,3072]{1,0:T(8,128)(2,1)S(1)} %block.5), channel_id=1, source_target_pairs={{0,1},{1,0},{2,3},{3,2},{4,5},{5,4},{6,7},{7,6},{8,9},{9,8},{10,11... | collective-permute-start | bytes 4718600 | tf_op jit(solution)/shard_map/ppermute | solution.py:410
  108.7 2.2 %block.4.own_ref = f32[256,3072]{1,0:T(8,128)S(1)} custom-call(s32[1]{0:T(128)} %bitcast.6.frag_ref, bf16[2,128,3072]{2,1,0:T(8,128)(2,1)S(1)} %collective-permute-done.11.block, bf16[3,3072,256]{2,1,0:T(8,128)(2,1)S(1)} %get-tuple-element.26.refs_1_.refs_0_, f32[256,3072]{1,0:T(8,128)S(1)} %get-tuple-element.31.refs_1_), custom_call_target="tpu_custom_call", output_to_operand_aliasing={{}: (3, {})} | custom-call | flops 1 | bytes 1 | tf_op jit(solution)/shard_map/block/pallas_call | solution.py:284
  110.9 0.8 collective-permute-done.14.other_ref
  111.7 3.2 %adam.1 = bf16[3072,256]{1,0:T(8,128)(2,1)} custom-call(f32[256,3072]{1,0:T(8,128)S(1)} %block.4.own_ref, bf16[256,3072]{1,0:T(8,128)(2,1)S(1)} %collective-permute-done.14.other_ref, f32[3072,256]{1,0:T(8,128)S(1)} %bitcast.25, f32[3072,256]{1,0:T(8,128)S(1)} %bitcast.26, f32[3072,256]{1,0:T(8,128)S(1)} %get-tuple-element.33.mixed_ref), custom_call_target="tpu_custom_call" | custom-call | flops 1 | bytes 1 | tf_op jit(solution)/shard_map/adam/pallas_call | solution.py:323
  (22 shorter events, 0.0 us)
Async XLA Ops:
  0.6 47.2 %collective-permute-start.6 = (bf16[3,3072,256]{2,1,0:T(8,128)(2,1)}, bf16[3,3072,256]{2,1,0:T(8,128)(2,1)}, u32[]{:S(2)}, u32[]{:S(2)}) collective-permute-start(bf16[3,3072,256]{2,1,0:T(8,128)(2,1)} %bitcast.19), channel_id=1, source_target_pairs={{0,1},{1,0},{2,3},{3,2},{4,5},{5,4},{6,7},{7,6},{8,9},{9,8},{10,11... | collective-permute-start | bytes 14155784 | tf_op jit(solution)/shard_map/ppermute | solution.py:343
  4.9 36.9 %collective-permute-start.1 = (bf16[2,128,3072]{2,1,0:T(8,128)(2,1)}, bf16[2,128,3072]{2,1,0:T(8,128)(2,1)S(1)}, u32[]{:S(2)}, u32[]{:S(2)}) collective-permute-start(bf16[2,128,3072]{2,1,0:T(8,128)(2,1)} %norm.1.refs_0_), channel_id=1, source_target_pairs={{0,8},{1,9},{2,10},{3,11},{4,12},{5,13},{6,14},{7,15},{8,0},{9,1},... | collective-permute-start | bytes 4718600 | tf_op jit(solution)/shard_map/ppermute | solution.py:373
  6.7 35.1 %collective-permute-start.2 = (bf16[2,128,3072]{2,1,0:T(8,128)(2,1)}, bf16[2,128,3072]{2,1,0:T(8,128)(2,1)S(1)}, u32[]{:S(2)}, u32[]{:S(2)}) collective-permute-start(bf16[2,128,3072]{2,1,0:T(8,128)(2,1)} %norm.1.refs_0_), channel_id=1, source_target_pairs={{0,2},{1,7},{2,4},{3,1},{4,6},{5,3},{6,0},{7,5},{8,10},{9,15},{10,... | collective-permute-start | bytes 4718600 | tf_op jit(solution)/shard_map/ppermute | solution.py:372
  12.2 12.7 %collective-permute-start.3 = (bf16[1536,256]{1,0:T(8,128)(2,1)}, bf16[1536,256]{1,0:T(8,128)(2,1)}, u32[]{:S(2)}, u32[]{:S(2)}) collective-permute-start(bf16[1536,256]{1,0:T(8,128)(2,1)} %dynamic-slice_bitcast_fusion), channel_id=1, source_target_pairs={{0,16},{1,49},{2,18},{3,51},{4,20},{5,53},{6,22},{7,55},{8,24},{9,... | collective-permute-start | bytes 2359304 | tf_op jit(solution)/shard_map/ppermute | solution.py:375
  14.7 33.1 %collective-permute-start = (bf16[2,128,3072]{2,1,0:T(8,128)(2,1)}, bf16[2,128,3072]{2,1,0:T(8,128)(2,1)}, u32[]{:S(2)}, u32[]{:S(2)}) collective-permute-start(bf16[2,128,3072]{2,1,0:T(8,128)(2,1)} %norm.1.refs_0_), channel_id=1, source_target_pairs={{0,7},{1,2},{2,1},{3,4},{4,3},{5,6},{6,5},{7,0},{8,15},{9,10},{10,... | collective-permute-start | bytes 4718600 | tf_op jit(solution)/shard_map/ppermute | solution.py:374
  27.1 7.2 %collective-permute-start.4 = (f16[768,256]{1,0:T(8,128)(2,1)}, f16[768,256]{1,0:T(8,128)(2,1)S(1)}, u32[]{:S(2)}, u32[]{:S(2)}) collective-permute-start(f16[768,256]{1,0:T(8,128)(2,1)} %fusion.3), channel_id=1, source_target_pairs={{0,48},{1,17},{2,50},{3,19},{4,52},{5,21},{6,54},{7,23},{8,56},{9,... | collective-permute-start | bytes 1179656 | tf_op jit(solution)/shard_map/ppermute | solution.py:384
  41.7 6.0 %copy-start.1 = (bf16[2,128,3072]{2,1,0:T(8,128)(2,1)}, bf16[2,128,3072]{2,1,0:T(8,128)(2,1)S(1)}, u32[]{:S(2)}) copy-start(bf16[2,128,3072]{2,1,0:T(8,128)(2,1)S(1)} %collective-permute-done.1.refs_3_) | copy-start | bytes 4718596
  41.7 6.0 %copy-start.3 = (bf16[2,128,3072]{2,1,0:T(8,128)(2,1)}, bf16[2,128,3072]{2,1,0:T(8,128)(2,1)S(1)}, u32[]{:S(2)}) copy-start(bf16[2,128,3072]{2,1,0:T(8,128)(2,1)S(1)} %collective-permute-done.2.refs_1_) | copy-start | bytes 4718596
  41.7 20.1 %collective-permute-start.10 = (bf16[2,128,3072]{2,1,0:T(8,128)(2,1)S(1)}, bf16[2,128,3072]{2,1,0:T(8,128)(2,1)}, u32[]{:S(2)}, u32[]{:S(2)}) collective-permute-start(bf16[2,128,3072]{2,1,0:T(8,128)(2,1)S(1)} %collective-permute-done.1.refs_3_), channel_id=1, source_target_pairs={{0,2},{1,7},{2,4},{3,1},{4,6},{5,3},{6,0},{7,5},{8,10},{9,15},{10,... | collective-permute-start | bytes 4718600 | tf_op jit(solution)/shard_map/ppermute | solution.py:388
  44.5 13.0 %collective-permute-start.5 = (f16[768,256]{1,0:T(8,128)(2,1)S(1)}, f16[768,256]{1,0:T(8,128)(2,1)S(1)}, u32[]{:S(2)}, u32[]{:S(2)}) collective-permute-start(f16[768,256]{1,0:T(8,128)(2,1)S(1)} %fusion.7), channel_id=1, source_target_pairs={{0,64},{16,80},{32,96},{48,112},{64,0},{80,16},{96,32},{112,48},{1... | collective-permute-start | bytes 1179656 | tf_op jit(solution)/shard_map/ppermute | solution.py:387
  57.6 8.4 %collective-permute-start.7 = (f16[768,256]{1,0:T(8,128)(2,1)S(1)}, f16[768,256]{1,0:T(8,128)(2,1)S(1)}, u32[]{:S(2)}, u32[]{:S(2)}) collective-permute-start(f16[768,256]{1,0:T(8,128)(2,1)S(1)} %add_convert_fusion), channel_id=1, source_target_pairs={{0,48},{1,17},{2,50},{3,19},{4,52},{5,21},{6,54},{7,23},{8,56},{9,... | collective-permute-start | bytes 1179656 | tf_op jit(solution)/shard_map/ppermute | solution.py:396
  58.9 18.9 %collective-permute-start.8 = (f16[768,256]{1,0:T(8,128)(2,1)S(1)}, f16[768,256]{1,0:T(8,128)(2,1)S(1)}, u32[]{:S(2)}, u32[]{:S(2)}) collective-permute-start(f16[768,256]{1,0:T(8,128)(2,1)S(1)} %add_convert_fusion), channel_id=1, source_target_pairs={{0,16},{1,49},{2,18},{3,51},{4,20},{5,53},{6,22},{7,55},{8,24},{9,... | collective-permute-start | bytes 1179656 | tf_op jit(solution)/shard_map/ppermute | solution.py:396
  60.7 18.0 %collective-permute-start.9 = (f16[768,256]{1,0:T(8,128)(2,1)S(1)}, f16[768,256]{1,0:T(8,128)(2,1)S(1)}, u32[]{:S(2)}, u32[]{:S(2)}) collective-permute-start(f16[768,256]{1,0:T(8,128)(2,1)S(1)} %add_convert_fusion), channel_id=1, source_target_pairs={{0,32},{16,48},{32,0},{48,16},{64,96},{80,112},{96,64},{112,80},{1... | collective-permute-start | bytes 1179656 | tf_op jit(solution)/shard_map/ppermute | solution.py:397
  61.4 23.7 %collective-permute-start.12 = (bf16[2,128,3072]{2,1,0:T(8,128)(2,1)}, bf16[2,128,3072]{2,1,0:T(8,128)(2,1)}, u32[]{:S(2)}, u32[]{:S(2)}) collective-permute-start(bf16[2,128,3072]{2,1,0:T(8,128)(2,1)} %copy-done.3), channel_id=1, source_target_pairs={{0,2},{1,7},{2,4},{3,1},{4,6},{5,3},{6,0},{7,5},{8,10},{9,15},{10,... | collective-permute-start | bytes 4718600 | tf_op jit(solution)/shard_map/ppermute | solution.py:389
  61.9 34.0 %collective-permute-start.13 = (bf16[2,128,3072]{2,1,0:T(8,128)(2,1)}, bf16[2,128,3072]{2,1,0:T(8,128)(2,1)}, u32[]{:S(2)}, u32[]{:S(2)}) collective-permute-start(bf16[2,128,3072]{2,1,0:T(8,128)(2,1)} %collective-permute-done.refs_2_), channel_id=1, source_target_pairs={{0,8},{1,9},{2,10},{3,11},{4,12},{5,13},{6,14},{7,15},{8,0},{9,1},... | collective-permute-start | bytes 4718600 | tf_op jit(solution)/shard_map/ppermute | solution.py:395
  66.0 35.2 %collective-permute-start.11 = (bf16[2,128,3072]{2,1,0:T(8,128)(2,1)}, bf16[2,128,3072]{2,1,0:T(8,128)(2,1)S(1)}, u32[]{:S(2)}, u32[]{:S(2)}) collective-permute-start(bf16[2,128,3072]{2,1,0:T(8,128)(2,1)} %collective-permute-done.10.refs_0_.refs_4_), channel_id=1, source_target_pairs={{0,2},{1,7},{2,4},{3,1},{4,6},{5,3},{6,0},{7,5},{8,10},{9,15},{10,... | collective-permute-start | bytes 4718600 | tf_op jit(solution)/shard_map/ppermute | solution.py:399
  72.3 6.8 %copy-start.9 = (f32[3072,256]{1,0:T(8,128)S(1)}, f32[3072,256]{1,0:T(8,128)}, u32[]{:S(2)}) copy-start(f32[3072,256]{1,0:T(8,128)} %param.16) | copy-start | bytes 9437188
  78.7 6.3 %slice-start = ((s8[4718592]{0:T(1024)(128)(4,1)}), s8[4194304]{0:T(1024)(128)(4,1)S(1)}, s32[]{:S(2)}) async-start(s8[4718592]{0:T(1024)(128)(4,1)} %bitcast.22), calls=%async_computation | async-start | bytes 8388608
  79.1 6.0 %slice-start.1 = ((s8[4718592]{0:T(1024)(128)(4,1)}), s8[524288]{0:T(1024)(128)(4,1)S(1)}, s32[]{:S(2)}) async-start(s8[4718592]{0:T(1024)(128)(4,1)} %bitcast.22), calls=%async_computation.1 | async-start | bytes 1048576
  79.1 5.9 %copy-start = (bf16[2,128,3072]{2,1,0:T(8,128)(2,1)S(1)}, bf16[2,128,3072]{2,1,0:T(8,128)(2,1)}, u32[]{:S(2)}) copy-start(bf16[2,128,3072]{2,1,0:T(8,128)(2,1)} %norm.1.refs_0_) | copy-start | bytes 4718596
  79.1 5.9 %copy-start.2 = (bf16[2,128,3072]{2,1,0:T(8,128)(2,1)S(1)}, bf16[2,128,3072]{2,1,0:T(8,128)(2,1)}, u32[]{:S(2)}) copy-start(bf16[2,128,3072]{2,1,0:T(8,128)(2,1)} %copy-done.1) | copy-start | bytes 4718596
  79.1 7.1 %copy-start.4 = (bf16[2,128,3072]{2,1,0:T(8,128)(2,1)S(1)}, bf16[2,128,3072]{2,1,0:T(8,128)(2,1)}, u32[]{:S(2)}) copy-start(bf16[2,128,3072]{2,1,0:T(8,128)(2,1)} %copy-done.3) | copy-start | bytes 4718596
  79.1 7.1 %copy-start.7 = (bf16[512,512]{1,0:T(8,128)(2,1)S(1)}, bf16[512,512]{1,0:T(8,128)(2,1)}, u32[]{:S(2)}) copy-start(bf16[512,512]{1,0:T(8,128)(2,1)} %forward.2.refs_5_) | copy-start | bytes 1572868
  79.2 7.1 %copy-start.8 = (bf16[128,512]{1,0:T(8,128)(2,1)S(1)}, bf16[128,512]{1,0:T(8,128)(2,1)}, u32[]{:S(2)}) copy-start(bf16[128,512]{1,0:T(8,128)(2,1)} %forward.3.refs_6_) | copy-start | bytes 393220
  103.4 8.3 %collective-permute-start.14 = (bf16[256,3072]{1,0:T(8,128)(2,1)S(1)}, bf16[256,3072]{1,0:T(8,128)(2,1)S(1)}, u32[]{:S(2)}, u32[]{:S(2)}) collective-permute-start(bf16[256,3072]{1,0:T(8,128)(2,1)S(1)} %block.5), channel_id=1, source_target_pairs={{0,1},{1,0},{2,3},{3,2},{4,5},{5,4},{6,7},{7,6},{8,9},{9,8},{10,11... | collective-permute-start | bytes 4718600 | tf_op jit(solution)/shard_map/ppermute | solution.py:410
  108.6 3.0 %copy-start.5 = (f32[1,3072,256]{2,1,0:T(8,128)S(1)}, f32[1,3072,256]{2,1,0:T(8,128)}, u32[]{:S(2)}) copy-start(f32[1,3072,256]{2,1,0:T(8,128)} %param.14) | copy-start | bytes 9437188
  108.7 3.0 %copy-start.6 = (f32[1,3072,256]{2,1,0:T(8,128)S(1)}, f32[1,3072,256]{2,1,0:T(8,128)}, u32[]{:S(2)}) copy-start(f32[1,3072,256]{2,1,0:T(8,128)} %param.15) | copy-start | bytes 9437188

commit v4 on v3

--- a/solution.py
+++ b/solution.py
@@ -262,43 +262,43 @@
     return out[:2], out[2:]
 
 
-def step_kernel(halves, frag_ref, block, *refs):
-    weights, totals, outs = refs[:halves], refs[halves : 2 * halves], refs[2 * halves : 3 * halves]
-    n_s, c_s, up_s, dh_s, right_s, sems = refs[3 * halves :]
+def step_kernel(count, frag_ref, *refs):
+    blocks, (weight, total, out) = refs[:count], refs[count : count + 3]
+    n_s, c_s, up_s, dh_s, right_s, sems = refs[count + 3 :]
+    rows = blocks[0].shape[1]
     frag = frag_ref[0]
-    loads = Loads(frag, sems, 2)
-    loads.add(("n", 0), block.at[0], n_s)
-    loads.add(("c", 0), block.at[1], c_s)
+    loads = Loads(frag, sems, 2 * count)
+    for kind, side, target in (("n", 0, n_s), ("c", 1, c_s)):
+        for k, block in enumerate(blocks):
+            loads.add((kind, 0), block.at[side], target.at[pl.ds(k * rows, rows)])
     loads.start()
-    for h in range(halves):
-        right_side(frag, loads, h, n_s, c_s, weights[h], up_s, dh_s, right_s)
-        right_t = right_s[...].T
-        pl.when(frag == 2)(functools.partial(add_gradient, right_t, c_s, outs[h], totals[h]))
-        pl.when(frag != 2)(functools.partial(add_gradient, right_t, n_s, outs[h], totals[h]))
-
-
-def add_block(frag, block, weights, totals, kind=jnp.float32):
-    halves, rows = len(weights), block.shape[1]
-    _, d, cols = weights[0].shape
-    aliases = {2 + halves + h: h for h in range(halves)} if kind == jnp.float32 else {}
+    right_side(frag, loads, 0, n_s, c_s, weight, up_s, dh_s, right_s)
+    right_t = right_s[...].T
+    pl.when(frag == 2)(functools.partial(add_gradient, right_t, c_s, out, total))
+    pl.when(frag != 2)(functools.partial(add_gradient, right_t, n_s, out, total))
+
+
+def add_blocks(frag, blocks, weight, total, kind=jnp.float32):
+    count, rows = len(blocks), len(blocks) * blocks[0].shape[1]
+    _, d, cols = weight.shape
     return pl.pallas_call(
-        functools.partial(step_kernel, halves),
-        out_shape=[jax.ShapeDtypeStruct((cols, d), kind)] * halves,
-        in_specs=[SMEM, ANY] + [VMEM] * (2 * halves),
-        out_specs=[VMEM] * halves,
+        functools.partial(step_kernel, count),
+        out_shape=jax.ShapeDtypeStruct((cols, d), kind),
+        in_specs=[SMEM] + [ANY] * count + [VMEM] * 2,
+        out_specs=VMEM,
         scratch_shapes=[
             pltpu.VMEM((rows, d), jnp.bfloat16),
             pltpu.VMEM((rows, d), jnp.bfloat16),
             pltpu.VMEM((rows, cols), jnp.float32),
             pltpu.VMEM((rows, cols), jnp.float32),
             pltpu.VMEM((rows, cols), jnp.bfloat16),
-            pltpu.SemaphoreType.DMA((2,)),
+            pltpu.SemaphoreType.DMA((2 * count,)),
         ],
-        input_output_aliases=aliases,
+        input_output_aliases={count + 2: 0} if kind == jnp.float32 else {},
         compiler_params=pltpu.CompilerParams(vmem_limit_bytes=12 * MIB),
         cost_estimate=CHEAP,
-        name="block",
-    )(frag, block, *weights, *totals)
+        name="blocks",
+    )(frag, *blocks, weight, total)
 
 
 def adam_kernel(tokens, tile, own_ref, other_ref, m_ref, v_ref, mixed_ref, out_ref, out_s, sems):
@@ -395,9 +395,8 @@
     z_cross = other_z(cross)
     beside, across = lax.ppermute(mine, everyone, QUARTER_PAIR), lax.ppermute(mine, everyone, HALF_PAIR)
     opposite = lax.ppermute(mine, "replica", OPPOSITE)
-    z_near = after(z_near, beside)
-    z_far = straight(z_near)
     rights = [right, forward(frag, [z_near], w_both)]
+    z_far = straight(after(z_near, beside, rights[1]))
 
     delta = ordered(h, ordered(q, mine, beside), ordered(q, across, opposite)).astype(jnp.float32) * (1 / WIRE_SCALE)
     momentum_new = nesterov_mu * outer_mom + delta
@@ -405,10 +404,10 @@
     mixed = mix_alpha * w_rows(0, d).astype(jnp.float32) + (1.0 - mix_alpha) * global_new
 
     held, totals = gradients(frag, after(far, mixed), w_both, [*first, z_near], rights)
-    totals = add_block(frag, z_cross, held, totals)
-    (grad_sib,) = add_block(frag, z_far, held[:1], totals[:1], jnp.bfloat16)
+    sib_total = add_blocks(frag, [z_cross], held[0], totals[0])
+    grad_sib = add_blocks(frag, [z_far], held[0], sib_total, jnp.bfloat16)
     grad_sib = lax.ppermute(grad_sib, "fsdp", SIBLING)
-    (grad_own,) = add_block(frag, z_far, held[1:], totals[1:])
+    grad_own = add_blocks(frag, [z_cross, z_far], held[1], totals[1])
     tokens_total = hidden_in.shape[1] * lax.axis_size("fsdp")
     merged = adam(tokens_total, grad_own, grad_sib, adam_m[0], adam_v[0], mixed)
     return (global_new, momentum_new, merged[None])

time: 114 us -> 112 us (0.982); the launches traced: 115 us -> 111 us
  Pallas kernels: 39.7 us -> 34.8 us
  starting transfers between devices: 25.9 us -> 27.2 us
    ppermute x1, starting transfers between devices: 0.57 us -> 3.66 us  [per_device(): z_far = straight(after(z_near, beside, rights[1]))]
    ppermute x1, waiting for transfers between devices: 2.85 us -> 0.01 us  [per_device(): lax.ppermute(mine, everyone, QUARTER_PAIR)]
    pallas_call x2, Pallas kernels: 15.4 us -> 12.9 us  [forward(): pl.pallas_call(functools.partial(forward_kernel, count), out_shape=jax.Sh...]
    ppermute x1, waiting for transfers between devices: 0.92 us -> 3.02 us  [per_device(): z_cross = other_z(cross)]
    ppermute x1, starting transfers between devices: 5.29 us -> 3.41 us  [per_device(): grad_sib = lax.ppermute(grad_sib, 'fsdp', SIBLING)]
    pallas_call x3, Pallas kernels: 9.68 us -> 8.16 us  [add_blocks(): pl.pallas_call(functools.partial(step_kernel, count), out_shape=jax.Shape...]
  transfers between devices with their start and end apart: 15 -> 15, of which waited for: 8 -> 8; matrix products, arithmetic and copies ran while one was open for 11% -> 11% of each run, Pallas kernels for 30% -> 26%
where the time goes in v4:
time: 112 us; the launch traced here: 111 us
  Pallas kernels  34.8 us (31%)
  waiting for transfers between devices  33.2 us (30%)
  starting transfers between devices  27.2 us (24%)
  other arithmetic  10.6 us (9%)
  local copies, waits for them, and re-layouts  3.34 us (3%)
  between operations  1.74 us (2%)
    pallas_call x2, Pallas kernels, forward(): pl.pallas_call(functools.partial(forward_kernel, count), out_shape=jax.Sh...  12.9 us
    ppermute x1, waiting for transfers between devices, per_device(): lax.ppermute(after(w_rows((1 - h) * half, half), own), everyone, HALF_PAIR)  10.2 us
    pallas_call x3, Pallas kernels, add_blocks(): pl.pallas_call(functools.partial(step_kernel, count), out_shape=jax.Shape...  8.16 us
    pallas_call x1, Pallas kernels, gradients(): pl.pallas_call(functools.partial(gradient_kernel, past, tuple(spans)), ou...  7.76 us
    ppermute x1, waiting for transfers between devices, per_device(): got = lax.ppermute(sent, everyone, QUARTER_PAIR)  7.23 us
    add x1, other arithmetic, per_device(): mix_alpha * w_rows(0, d).astype(jnp.float32)  5.88 us
    ppermute x1, waiting for transfers between devices, per_device(): z_own = other_z(own)  5.73 us
    ppermute x1, waiting for transfers between devices, per_device(): lax.ppermute(mine, everyone, HALF_PAIR)  5.2 us
  transfers between devices with their start and end apart: 15, of which 8 were waited for; matrix products, arithmetic and copies ran while one was open for 11% of the time, Pallas kernels for 26%

profile of v4, /device:TPU:1, one launch (start us, length us, event | category | flops | bytes accessed | tf_op | source)
XLA Modules:
  0.0 110.9 jit_solution(947070529976562411)
XLA Ops:
  0.6 1.5 %collective-permute-start.6 = (bf16[3,3072,256]{2,1,0:T(8,128)(2,1)}, bf16[3,3072,256]{2,1,0:T(8,128)(2,1)}, u32[]{:S(2)}, u32[]{:S(2)}) collective-permute-start(bf16[3,3072,256]{2,1,0:T(8,128)(2,1)} %bitcast.19), channel_id=1, source_target_pairs={{0,1},{1,0},{2,3},{3,2},{4,5},{5,4},{6,7},{7,6},{8,9},{9,8},{10,11... | collective-permute-start | bytes 14155784 | tf_op jit(solution)/shard_map/ppermute | solution.py:343
  2.1 2.7 %norm.1.refs_0_ = bf16[2,128,3072]{2,1,0:T(8,128)(2,1)} custom-call(bf16[128,3072]{1,0:T(8,128)(2,1)} %bitcast.28, bf16[128,3072]{1,0:T(8,128)(2,1)} %bitcast.29, bf16[3072]{0:T(1024)(128)(2,1)} %g_ref.1), custom_call_target="tpu_custom_call" | custom-call | flops 1 | bytes 1 | tf_op jit(solution)/shard_map/norm/pallas_call | solution.py:73
  4.9 1.8 %collective-permute-start.1 = (bf16[2,128,3072]{2,1,0:T(8,128)(2,1)}, bf16[2,128,3072]{2,1,0:T(8,128)(2,1)S(1)}, u32[]{:S(2)}, u32[]{:S(2)}) collective-permute-start(bf16[2,128,3072]{2,1,0:T(8,128)(2,1)} %norm.1.refs_0_), channel_id=1, source_target_pairs={{0,8},{1,9},{2,10},{3,11},{4,12},{5,13},{6,14},{7,15},{8,0},{9,1},... | collective-permute-start | bytes 4718600 | tf_op jit(solution)/shard_map/ppermute | solution.py:373
  6.7 2.7 %collective-permute-start.2 = (bf16[2,128,3072]{2,1,0:T(8,128)(2,1)}, bf16[2,128,3072]{2,1,0:T(8,128)(2,1)S(1)}, u32[]{:S(2)}, u32[]{:S(2)}) collective-permute-start(bf16[2,128,3072]{2,1,0:T(8,128)(2,1)} %norm.1.refs_0_), channel_id=1, source_target_pairs={{0,2},{1,7},{2,4},{3,1},{4,6},{5,3},{6,0},{7,5},{8,10},{9,15},{10,... | collective-permute-start | bytes 4718600 | tf_op jit(solution)/shard_map/ppermute | solution.py:372
  10.1 2.1 %dynamic-slice_bitcast_fusion = bf16[1536,256]{1,0:T(8,128)(2,1)} fusion(bf16[1,3,3072,256]{3,2,1,0:T(8,128)(2,1)} %param.13, s32[]{:T(128)S(6)} %select_n.71, s32[]{:T(128)S(6)} %select_n.72), kind=kLoop, calls=%fused_computation.18 | loop fusion | bytes 1572872 | tf_op jit(solution)/shard_map/squeeze | solution.py:361
  12.2 2.5 %collective-permute-start.3 = (bf16[1536,256]{1,0:T(8,128)(2,1)}, bf16[1536,256]{1,0:T(8,128)(2,1)}, u32[]{:S(2)}, u32[]{:S(2)}) collective-permute-start(bf16[1536,256]{1,0:T(8,128)(2,1)} %dynamic-slice_bitcast_fusion), channel_id=1, source_target_pairs={{0,16},{1,49},{2,18},{3,51},{4,20},{5,53},{6,22},{7,55},{8,24},{9,... | collective-permute-start | bytes 2359304 | tf_op jit(solution)/shard_map/ppermute | solution.py:375
  14.7 0.0 collective-permute-start
  14.7 10.2 %collective-permute-done.3 = bf16[1536,256]{1,0:T(8,128)(2,1)} collective-permute-done((bf16[1536,256]{1,0:T(8,128)(2,1)}, bf16[1536,256]{1,0:T(8,128)(2,1)}, u32[]{:S(2)}, u32[]{:S(2)}) %collective-permute-start.3) | collective-permute-done | bytes 786464 | tf_op jit(solution)/shard_map/ppermute | solution.py:375
  24.9 2.3 %fusion.3 = f16[768,256]{1,0:T(8,128)(2,1)} fusion(f32[3072,256]{1,0:T(8,128)} %param.16, s32[]{:T(128)S(6)} %select_n.74, bf16[1536,256]{1,0:T(8,128)(2,1)} %collective-permute-done.3, s32[]{:T(128)S(6)} %select_n.75, bf16[1,3,3072,256]{3,2,1,0:T(8,128)(2,1)} %param.13, s32[]{:T(128)S(6)} %select_n.71), kind=kLoop, calls=%fused_computation.11 | loop fusion | flops 1376256 | bytes 1966092 | tf_op jit(solution)/shard_map/convert_element_type | solution.py:370
  27.1 0.0 collective-permute-start.4
  27.1 7.2 %collective-permute-done.4 = f16[768,256]{1,0:T(8,128)(2,1)S(1)} collective-permute-done((f16[768,256]{1,0:T(8,128)(2,1)}, f16[768,256]{1,0:T(8,128)(2,1)S(1)}, u32[]{:S(2)}, u32[]{:S(2)}) %collective-permute-start.4) | collective-permute-done | bytes 393248 | tf_op jit(solution)/shard_map/ppermute | solution.py:384
  34.4 1.6 %fusion.7 = f16[768,256]{1,0:T(8,128)(2,1)S(1)} fusion(f16[768,256]{1,0:T(8,128)(2,1)S(1)} %collective-permute-done.4, f32[3072,256]{1,0:T(8,128)} %param.16, s32[]{:T(128)S(6)} %select_n.69, bf16[1536,256]{1,0:T(8,128)(2,1)} %collective-permute-done.3, s32[]{:T(128)S(6)} %select_n.73, bf16[1,3,3072,256]{3,2,1,0:T(8,128)(2,1)} %param.13, s32[]{:T(128)S(6)} %select_n.71), kind=kLoop, calls=%fused_computation.16 | loop fusion | flops 1966080 | bytes 2359308 | tf_op jit(solution)/shard_map/convert_element_type | solution.py:370
  36.0 5.7 %collective-permute-done.1.refs_3_ = bf16[2,128,3072]{2,1,0:T(8,128)(2,1)S(1)} collective-permute-done((bf16[2,128,3072]{2,1,0:T(8,128)(2,1)}, bf16[2,128,3072]{2,1,0:T(8,128)(2,1)S(1)}, u32[]{:S(2)}, u32[]{:S(2)}) %collective-permute-start.1) | collective-permute-done | bytes 1572896 | tf_op jit(solution)/shard_map/ppermute | solution.py:373
  41.7 0.0 collective-permute-done.2.refs_1_
  41.7 2.7 %collective-permute-start.11 = (bf16[2,128,3072]{2,1,0:T(8,128)(2,1)S(1)}, bf16[2,128,3072]{2,1,0:T(8,128)(2,1)}, u32[]{:S(2)}, u32[]{:S(2)}) collective-permute-start(bf16[2,128,3072]{2,1,0:T(8,128)(2,1)S(1)} %collective-permute-done.1.refs_3_), channel_id=1, source_target_pairs={{0,2},{1,7},{2,4},{3,1},{4,6},{5,3},{6,0},{7,5},{8,10},{9,15},{10,... | collective-permute-start | bytes 4718600 | tf_op jit(solution)/shard_map/ppermute | solution.py:388
  44.5 3.3 %collective-permute-start.5 = (f16[768,256]{1,0:T(8,128)(2,1)S(1)}, f16[768,256]{1,0:T(8,128)(2,1)S(1)}, u32[]{:S(2)}, u32[]{:S(2)}) collective-permute-start(f16[768,256]{1,0:T(8,128)(2,1)S(1)} %fusion.7), channel_id=1, source_target_pairs={{0,64},{16,80},{32,96},{48,112},{64,0},{80,16},{96,32},{112,48},{1... | collective-permute-start | bytes 1179656 | tf_op jit(solution)/shard_map/ppermute | solution.py:387
  47.8 0.0 collective-permute-done.refs_2_
  47.8 0.0 collective-permute-done.6.refs_4_.refs_1_.refs_7_
  47.8 8.1 %forward.2.refs_5_ = bf16[512,512]{1,0:T(8,128)(2,1)} custom-call(s32[1]{0:T(128)} %bitcast.6.frag_ref, bf16[2,128,3072]{2,1,0:T(8,128)(2,1)} %norm.1.refs_0_, bf16[2,128,3072]{2,1,0:T(8,128)(2,1)} %copy-done.3, bf16[2,128,3072]{2,1,0:T(8,128)(2,1)} %collective-permute-done.refs_2_, bf16[2,128,3072]{2,1,0:T(8,128)(2,1)} %copy-done.1, ...), custom_call_target="tpu_custom_call" | custom-call | flops 1 | bytes 1 | tf_op jit(solution)/shard_map/forward/pallas_call | solution.py:178
  55.9 0.9 collective-permute-done.5
  56.9 0.1 add_convert_fusion
  57.0 1.3 %collective-permute-start.7 = (f16[768,256]{1,0:T(8,128)(2,1)S(1)}, f16[768,256]{1,0:T(8,128)(2,1)S(1)}, u32[]{:S(2)}, u32[]{:S(2)}) collective-permute-start(f16[768,256]{1,0:T(8,128)(2,1)S(1)} %add_convert_fusion), channel_id=1, source_target_pairs={{0,48},{1,17},{2,50},{3,19},{4,52},{5,21},{6,54},{7,23},{8,56},{9,... | collective-permute-start | bytes 1179656 | tf_op jit(solution)/shard_map/ppermute | solution.py:396
  58.3 1.8 %collective-permute-start.8 = (f16[768,256]{1,0:T(8,128)(2,1)S(1)}, f16[768,256]{1,0:T(8,128)(2,1)S(1)}, u32[]{:S(2)}, u32[]{:S(2)}) collective-permute-start(f16[768,256]{1,0:T(8,128)(2,1)S(1)} %add_convert_fusion), channel_id=1, source_target_pairs={{0,16},{1,49},{2,18},{3,51},{4,20},{5,53},{6,22},{7,55},{8,24},{9,... | collective-permute-start | bytes 1179656 | tf_op jit(solution)/shard_map/ppermute | solution.py:396
  60.1 0.6 collective-permute-start.9
  60.7 0.4 collective-permute-start.13
  61.2 0.6 collective-permute-done.11.refs_0_.refs_4_
  61.8 1.4 %collective-permute-start.10 = (bf16[2,128,3072]{2,1,0:T(8,128)(2,1)}, bf16[2,128,3072]{2,1,0:T(8,128)(2,1)S(1)}, u32[]{:S(2)}, u32[]{:S(2)}) collective-permute-start(bf16[2,128,3072]{2,1,0:T(8,128)(2,1)} %collective-permute-done.refs_2_), channel_id=1, source_target_pairs={{0,8},{1,9},{2,10},{3,11},{4,12},{5,13},{6,14},{7,15},{8,0},{9,1},... | collective-permute-start | bytes 4718600 | tf_op jit(solution)/shard_map/ppermute | solution.py:395
  63.2 4.8 %forward.3.refs_6_ = bf16[128,512]{1,0:T(8,128)(2,1)} custom-call(s32[1]{0:T(128)} %bitcast.6.frag_ref, bf16[2,128,3072]{2,1,0:T(8,128)(2,1)} %collective-permute-done.11.refs_0_.refs_4_, bf16[3,3072,256]{2,1,0:T(8,128)(2,1)} %collective-permute-done.6.refs_4_.refs_1_.refs_7_, bf16[3,3072,256]{2,1,0:T(8,128)(2,1)} %bitcast.21), custom_call_target="tpu_custom_call" | custom-call | flops 1 | bytes 1 | tf_op jit(solution)/shard_map/forward/pallas_call | solution.py:178
  68.0 0.0 collective-permute-done.7
  68.0 3.7 %collective-permute-start.12 = (bf16[2,128,3072]{2,1,0:T(8,128)(2,1)}, bf16[2,128,3072]{2,1,0:T(8,128)(2,1)}, u32[]{:S(2)}, u32[]{:S(2)}) collective-permute-start(bf16[2,128,3072]{2,1,0:T(8,128)(2,1)} %collective-permute-done.11.refs_0_.refs_4_), channel_id=1, source_target_pairs={{0,2},{1,7},{2,4},{3,1},{4,6},{5,3},{6,0},{7,5},{8,10},{9,15},{10,... | collective-permute-start | bytes 4718600 | tf_op jit(solution)/shard_map/ppermute | solution.py:399
  71.6 0.3 maximum_select_fusion.1
  72.0 5.2 %collective-permute-done.8 = f16[768,256]{1,0:T(8,128)(2,1)S(1)} collective-permute-done((f16[768,256]{1,0:T(8,128)(2,1)S(1)}, f16[768,256]{1,0:T(8,128)(2,1)S(1)}, u32[]{:S(2)}, u32[]{:S(2)}) %collective-permute-start.8) | collective-permute-done | bytes 393248 | tf_op jit(solution)/shard_map/ppermute | solution.py:396
  77.2 0.3 collective-permute-done.9
  77.5 0.3 maximum_select_fusion.2
  77.8 0.0 slice-start.1
  77.8 0.0 copy-start
  77.9 5.9 %fusion = (f32[3072,256]{1,0:T(8,128)S(1)}, f32[3072,256]{1,0:T(8,128)}, f32[3072,256]{1,0:T(8,128)}) fusion(bf16[1,3,3072,256]{3,2,1,0:T(8,128)(2,1)} %param.13, s32[]{:T(128)S(6)} %select_n.71, f32[3072,256]{1,0:T(8,128)S(1)} %copy-done.9, f16[1536,256]{1,0:T(8,128)(2,1)S(1)} %maximum_select_fusion.1, f16[1536,256]{1,0:T(8,128)(2,1)S(1)} %maximum_select_fusion.2, ...), kind=kLoop, calls=%fused_computation.1 | loop fusion | flops 11010048 | bytes 18874372 | tf_op jit(solution)/shard_map/add | solution.py:404
  83.8 1.1 %copy-done.4 = bf16[2,128,3072]{2,1,0:T(8,128)(2,1)S(1)} copy-done((bf16[2,128,3072]{2,1,0:T(8,128)(2,1)S(1)}, bf16[2,128,3072]{2,1,0:T(8,128)(2,1)}, u32[]{:S(2)}) %copy-start.4) | copy-done | bytes 1572888
  84.9 0.1 copy-done.7
  85.0 0.0 copy-done.8
  85.0 7.8 %gradients.1 = (bf16[3,3072,256]{2,1,0:T(8,128)(2,1)S(1)}, bf16[3,3072,256]{2,1,0:T(8,128)(2,1)S(1)}, f32[256,3072]{1,0:T(8,128)S(1)}, f32[256,3072]{1,0:T(8,128)S(1)}) custom-call(s32[1]{0:T(128)} %bitcast.6.frag_ref, bf16[2,128,3072]{2,1,0:T(8,128)(2,1)} %collective-permute-done.13.block, bf16[2,128,3072]{2,1,0:T(8,128)(2,1)S(1)} %copy-done, ...), custom_call_target="tpu_custom_call" | custom-call | flops 1 | bytes 1 | tf_op jit(solution)/shard_map/gradients/pallas_call | solution.py:244
  92.8 3.0 %collective-permute-done.10.refs_0_ = bf16[2,128,3072]{2,1,0:T(8,128)(2,1)S(1)} collective-permute-done((bf16[2,128,3072]{2,1,0:T(8,128)(2,1)}, bf16[2,128,3072]{2,1,0:T(8,128)(2,1)S(1)}, u32[]{:S(2)}, u32[]{:S(2)}) %collective-permute-start.10) | collective-permute-done | bytes 1572896 | tf_op jit(solution)/shard_map/ppermute | solution.py:395
  95.8 1.8 %blocks.4.refs_2_ = f32[256,3072]{1,0:T(8,128)S(1)} custom-call(s32[1]{0:T(128)} %bitcast.6.frag_ref, bf16[2,128,3072]{2,1,0:T(8,128)(2,1)S(1)} %collective-permute-done.10.refs_0_, bf16[3,3072,256]{2,1,0:T(8,128)(2,1)S(1)} %get-tuple-element.27.refs_1_, f32[256,3072]{1,0:T(8,128)S(1)} %get-tuple-element.28.refs_2_), custom_call_target="tpu_custom_call", output_to_operand_aliasing={{}: (3, {})} | custom-call | flops 1 | bytes 1 | tf_op jit(solution)/shard_map/blocks/pallas_call | solution.py:284
  97.6 0.0 collective-permute-done.12.refs_1_.refs_0_
  97.6 2.6 %blocks.5 = bf16[256,3072]{1,0:T(8,128)(2,1)S(1)} custom-call(s32[1]{0:T(128)} %bitcast.6.frag_ref, bf16[2,128,3072]{2,1,0:T(8,128)(2,1)} %collective-permute-done.12.refs_1_.refs_0_, bf16[3,3072,256]{2,1,0:T(8,128)(2,1)S(1)} %get-tuple-element.27.refs_1_, f32[256,3072]{1,0:T(8,128)S(1)} %blocks.4.refs_2_), custom_call_target="tpu_custom_call" | custom-call | flops 1 | bytes 1 | tf_op jit(solution)/shard_map/blocks/pallas_call | solution.py:284
  100.2 3.4 %collective-permute-start.14 = (bf16[256,3072]{1,0:T(8,128)(2,1)S(1)}, bf16[256,3072]{1,0:T(8,128)(2,1)S(1)}, u32[]{:S(2)}, u32[]{:S(2)}) collective-permute-start(bf16[256,3072]{1,0:T(8,128)(2,1)S(1)} %blocks.5), channel_id=1, source_target_pairs={{0,1},{1,0},{2,3},{3,2},{4,5},{5,4},{6,7},{7,6},{8,9},{9,8},{10,11... | collective-permute-start | bytes 4718600 | tf_op jit(solution)/shard_map/ppermute | solution.py:409
  103.7 3.7 %blocks.3.own_ref = f32[256,3072]{1,0:T(8,128)S(1)} custom-call(s32[1]{0:T(128)} %bitcast.6.frag_ref, bf16[2,128,3072]{2,1,0:T(8,128)(2,1)S(1)} %collective-permute-done.10.refs_0_, bf16[2,128,3072]{2,1,0:T(8,128)(2,1)} %collective-permute-done.12.refs_1_.refs_0_, ...), custom_call_target="tpu_custom_call", output_to_operand_aliasing={{}: (4, {})} | custom-call | flops 1 | bytes 1 | tf_op jit(solution)/shard_map/blocks/pallas_call | solution.py:284
  107.4 3.2 %adam.1 = bf16[3072,256]{1,0:T(8,128)(2,1)} custom-call(f32[256,3072]{1,0:T(8,128)S(1)} %blocks.3.own_ref, bf16[256,3072]{1,0:T(8,128)(2,1)S(1)} %collective-permute-done.14.other_ref, f32[3072,256]{1,0:T(8,128)S(1)} %bitcast.25, f32[3072,256]{1,0:T(8,128)S(1)} %bitcast.26, f32[3072,256]{1,0:T(8,128)S(1)} %get-tuple-element.29.mixed_ref), custom_call_target="tpu_custom_call" | custom-call | flops 1 | bytes 1 | tf_op jit(solution)/shard_map/adam/pallas_call | solution.py:323
  (22 shorter events, 0.0 us)
Async XLA Ops:
  0.6 47.2 %collective-permute-start.6 = (bf16[3,3072,256]{2,1,0:T(8,128)(2,1)}, bf16[3,3072,256]{2,1,0:T(8,128)(2,1)}, u32[]{:S(2)}, u32[]{:S(2)}) collective-permute-start(bf16[3,3072,256]{2,1,0:T(8,128)(2,1)} %bitcast.19), channel_id=1, source_target_pairs={{0,1},{1,0},{2,3},{3,2},{4,5},{5,4},{6,7},{7,6},{8,9},{9,8},{10,11... | collective-permute-start | bytes 14155784 | tf_op jit(solution)/shard_map/ppermute | solution.py:343
  4.9 36.9 %collective-permute-start.1 = (bf16[2,128,3072]{2,1,0:T(8,128)(2,1)}, bf16[2,128,3072]{2,1,0:T(8,128)(2,1)S(1)}, u32[]{:S(2)}, u32[]{:S(2)}) collective-permute-start(bf16[2,128,3072]{2,1,0:T(8,128)(2,1)} %norm.1.refs_0_), channel_id=1, source_target_pairs={{0,8},{1,9},{2,10},{3,11},{4,12},{5,13},{6,14},{7,15},{8,0},{9,1},... | collective-permute-start | bytes 4718600 | tf_op jit(solution)/shard_map/ppermute | solution.py:373
  6.7 35.1 %collective-permute-start.2 = (bf16[2,128,3072]{2,1,0:T(8,128)(2,1)}, bf16[2,128,3072]{2,1,0:T(8,128)(2,1)S(1)}, u32[]{:S(2)}, u32[]{:S(2)}) collective-permute-start(bf16[2,128,3072]{2,1,0:T(8,128)(2,1)} %norm.1.refs_0_), channel_id=1, source_target_pairs={{0,2},{1,7},{2,4},{3,1},{4,6},{5,3},{6,0},{7,5},{8,10},{9,15},{10,... | collective-permute-start | bytes 4718600 | tf_op jit(solution)/shard_map/ppermute | solution.py:372
  12.2 12.7 %collective-permute-start.3 = (bf16[1536,256]{1,0:T(8,128)(2,1)}, bf16[1536,256]{1,0:T(8,128)(2,1)}, u32[]{:S(2)}, u32[]{:S(2)}) collective-permute-start(bf16[1536,256]{1,0:T(8,128)(2,1)} %dynamic-slice_bitcast_fusion), channel_id=1, source_target_pairs={{0,16},{1,49},{2,18},{3,51},{4,20},{5,53},{6,22},{7,55},{8,24},{9,... | collective-permute-start | bytes 2359304 | tf_op jit(solution)/shard_map/ppermute | solution.py:375
  14.7 33.1 %collective-permute-start = (bf16[2,128,3072]{2,1,0:T(8,128)(2,1)}, bf16[2,128,3072]{2,1,0:T(8,128)(2,1)}, u32[]{:S(2)}, u32[]{:S(2)}) collective-permute-start(bf16[2,128,3072]{2,1,0:T(8,128)(2,1)} %norm.1.refs_0_), channel_id=1, source_target_pairs={{0,7},{1,2},{2,1},{3,4},{4,3},{5,6},{6,5},{7,0},{8,15},{9,10},{10,... | collective-permute-start | bytes 4718600 | tf_op jit(solution)/shard_map/ppermute | solution.py:374
  27.1 7.2 %collective-permute-start.4 = (f16[768,256]{1,0:T(8,128)(2,1)}, f16[768,256]{1,0:T(8,128)(2,1)S(1)}, u32[]{:S(2)}, u32[]{:S(2)}) collective-permute-start(f16[768,256]{1,0:T(8,128)(2,1)} %fusion.3), channel_id=1, source_target_pairs={{0,48},{1,17},{2,50},{3,19},{4,52},{5,21},{6,54},{7,23},{8,56},{9,... | collective-permute-start | bytes 1179656 | tf_op jit(solution)/shard_map/ppermute | solution.py:384
  41.7 6.0 %copy-start.1 = (bf16[2,128,3072]{2,1,0:T(8,128)(2,1)}, bf16[2,128,3072]{2,1,0:T(8,128)(2,1)S(1)}, u32[]{:S(2)}) copy-start(bf16[2,128,3072]{2,1,0:T(8,128)(2,1)S(1)} %collective-permute-done.1.refs_3_) | copy-start | bytes 4718596
  41.7 6.0 %copy-start.3 = (bf16[2,128,3072]{2,1,0:T(8,128)(2,1)}, bf16[2,128,3072]{2,1,0:T(8,128)(2,1)S(1)}, u32[]{:S(2)}) copy-start(bf16[2,128,3072]{2,1,0:T(8,128)(2,1)S(1)} %collective-permute-done.2.refs_1_) | copy-start | bytes 4718596
  41.7 20.1 %collective-permute-start.11 = (bf16[2,128,3072]{2,1,0:T(8,128)(2,1)S(1)}, bf16[2,128,3072]{2,1,0:T(8,128)(2,1)}, u32[]{:S(2)}, u32[]{:S(2)}) collective-permute-start(bf16[2,128,3072]{2,1,0:T(8,128)(2,1)S(1)} %collective-permute-done.1.refs_3_), channel_id=1, source_target_pairs={{0,2},{1,7},{2,4},{3,1},{4,6},{5,3},{6,0},{7,5},{8,10},{9,15},{10,... | collective-permute-start | bytes 4718600 | tf_op jit(solution)/shard_map/ppermute | solution.py:388
  44.5 12.4 %collective-permute-start.5 = (f16[768,256]{1,0:T(8,128)(2,1)S(1)}, f16[768,256]{1,0:T(8,128)(2,1)S(1)}, u32[]{:S(2)}, u32[]{:S(2)}) collective-permute-start(f16[768,256]{1,0:T(8,128)(2,1)S(1)} %fusion.7), channel_id=1, source_target_pairs={{0,64},{16,80},{32,96},{48,112},{64,0},{80,16},{96,32},{112,48},{1... | collective-permute-start | bytes 1179656 | tf_op jit(solution)/shard_map/ppermute | solution.py:387
  57.0 11.0 %collective-permute-start.7 = (f16[768,256]{1,0:T(8,128)(2,1)S(1)}, f16[768,256]{1,0:T(8,128)(2,1)S(1)}, u32[]{:S(2)}, u32[]{:S(2)}) collective-permute-start(f16[768,256]{1,0:T(8,128)(2,1)S(1)} %add_convert_fusion), channel_id=1, source_target_pairs={{0,48},{1,17},{2,50},{3,19},{4,52},{5,21},{6,54},{7,23},{8,56},{9,... | collective-permute-start | bytes 1179656 | tf_op jit(solution)/shard_map/ppermute | solution.py:396
  58.3 18.9 %collective-permute-start.8 = (f16[768,256]{1,0:T(8,128)(2,1)S(1)}, f16[768,256]{1,0:T(8,128)(2,1)S(1)}, u32[]{:S(2)}, u32[]{:S(2)}) collective-permute-start(f16[768,256]{1,0:T(8,128)(2,1)S(1)} %add_convert_fusion), channel_id=1, source_target_pairs={{0,16},{1,49},{2,18},{3,51},{4,20},{5,53},{6,22},{7,55},{8,24},{9,... | collective-permute-start | bytes 1179656 | tf_op jit(solution)/shard_map/ppermute | solution.py:396
  60.1 17.3 %collective-permute-start.9 = (f16[768,256]{1,0:T(8,128)(2,1)S(1)}, f16[768,256]{1,0:T(8,128)(2,1)S(1)}, u32[]{:S(2)}, u32[]{:S(2)}) collective-permute-start(f16[768,256]{1,0:T(8,128)(2,1)S(1)} %add_convert_fusion), channel_id=1, source_target_pairs={{0,32},{16,48},{32,0},{48,16},{64,96},{80,112},{96,64},{112,80},{1... | collective-permute-start | bytes 1179656 | tf_op jit(solution)/shard_map/ppermute | solution.py:397
  60.7 23.0 %collective-permute-start.13 = (bf16[2,128,3072]{2,1,0:T(8,128)(2,1)}, bf16[2,128,3072]{2,1,0:T(8,128)(2,1)}, u32[]{:S(2)}, u32[]{:S(2)}) collective-permute-start(bf16[2,128,3072]{2,1,0:T(8,128)(2,1)} %copy-done.3), channel_id=1, source_target_pairs={{0,2},{1,7},{2,4},{3,1},{4,6},{5,3},{6,0},{7,5},{8,10},{9,15},{10,... | collective-permute-start | bytes 4718600 | tf_op jit(solution)/shard_map/ppermute | solution.py:389
  61.8 34.0 %collective-permute-start.10 = (bf16[2,128,3072]{2,1,0:T(8,128)(2,1)}, bf16[2,128,3072]{2,1,0:T(8,128)(2,1)S(1)}, u32[]{:S(2)}, u32[]{:S(2)}) collective-permute-start(bf16[2,128,3072]{2,1,0:T(8,128)(2,1)} %collective-permute-done.refs_2_), channel_id=1, source_target_pairs={{0,8},{1,9},{2,10},{3,11},{4,12},{5,13},{6,14},{7,15},{8,0},{9,1},... | collective-permute-start | bytes 4718600 | tf_op jit(solution)/shard_map/ppermute | solution.py:395
  68.0 29.7 %collective-permute-start.12 = (bf16[2,128,3072]{2,1,0:T(8,128)(2,1)}, bf16[2,128,3072]{2,1,0:T(8,128)(2,1)}, u32[]{:S(2)}, u32[]{:S(2)}) collective-permute-start(bf16[2,128,3072]{2,1,0:T(8,128)(2,1)} %collective-permute-done.11.refs_0_.refs_4_), channel_id=1, source_target_pairs={{0,2},{1,7},{2,4},{3,1},{4,6},{5,3},{6,0},{7,5},{8,10},{9,15},{10,... | collective-permute-start | bytes 4718600 | tf_op jit(solution)/shard_map/ppermute | solution.py:399
  71.6 6.2 %copy-start.9 = (f32[3072,256]{1,0:T(8,128)S(1)}, f32[3072,256]{1,0:T(8,128)}, u32[]{:S(2)}) copy-start(f32[3072,256]{1,0:T(8,128)} %param.16) | copy-start | bytes 9437188
  77.5 6.3 %slice-start = ((s8[4718592]{0:T(1024)(128)(4,1)}), s8[4194304]{0:T(1024)(128)(4,1)S(1)}, s32[]{:S(2)}) async-start(s8[4718592]{0:T(1024)(128)(4,1)} %bitcast.22), calls=%async_computation | async-start | bytes 8388608
  77.8 6.0 %slice-start.1 = ((s8[4718592]{0:T(1024)(128)(4,1)}), s8[524288]{0:T(1024)(128)(4,1)S(1)}, s32[]{:S(2)}) async-start(s8[4718592]{0:T(1024)(128)(4,1)} %bitcast.22), calls=%async_computation.1 | async-start | bytes 1048576
  77.8 5.9 %copy-start = (bf16[2,128,3072]{2,1,0:T(8,128)(2,1)S(1)}, bf16[2,128,3072]{2,1,0:T(8,128)(2,1)}, u32[]{:S(2)}) copy-start(bf16[2,128,3072]{2,1,0:T(8,128)(2,1)} %norm.1.refs_0_) | copy-start | bytes 4718596
  77.8 5.9 %copy-start.2 = (bf16[2,128,3072]{2,1,0:T(8,128)(2,1)S(1)}, bf16[2,128,3072]{2,1,0:T(8,128)(2,1)}, u32[]{:S(2)}) copy-start(bf16[2,128,3072]{2,1,0:T(8,128)(2,1)} %copy-done.1) | copy-start | bytes 4718596
  77.8 7.1 %copy-start.4 = (bf16[2,128,3072]{2,1,0:T(8,128)(2,1)S(1)}, bf16[2,128,3072]{2,1,0:T(8,128)(2,1)}, u32[]{:S(2)}) copy-start(bf16[2,128,3072]{2,1,0:T(8,128)(2,1)} %copy-done.3) | copy-start | bytes 4718596
  77.9 7.1 %copy-start.7 = (bf16[512,512]{1,0:T(8,128)(2,1)S(1)}, bf16[512,512]{1,0:T(8,128)(2,1)}, u32[]{:S(2)}) copy-start(bf16[512,512]{1,0:T(8,128)(2,1)} %forward.2.refs_5_) | copy-start | bytes 1572868
  77.9 7.1 %copy-start.8 = (bf16[128,512]{1,0:T(8,128)(2,1)S(1)}, bf16[128,512]{1,0:T(8,128)(2,1)}, u32[]{:S(2)}) copy-start(bf16[128,512]{1,0:T(8,128)(2,1)} %forward.3.refs_6_) | copy-start | bytes 393220
  100.2 7.2 %collective-permute-start.14 = (bf16[256,3072]{1,0:T(8,128)(2,1)S(1)}, bf16[256,3072]{1,0:T(8,128)(2,1)S(1)}, u32[]{:S(2)}, u32[]{:S(2)}) collective-permute-start(bf16[256,3072]{1,0:T(8,128)(2,1)S(1)} %blocks.5), channel_id=1, source_target_pairs={{0,1},{1,0},{2,3},{3,2},{4,5},{5,4},{6,7},{7,6},{8,9},{9,8},{10,11... | collective-permute-start | bytes 4718600 | tf_op jit(solution)/shard_map/ppermute | solution.py:409
  103.7 3.8 %copy-start.5 = (f32[1,3072,256]{2,1,0:T(8,128)S(1)}, f32[1,3072,256]{2,1,0:T(8,128)}, u32[]{:S(2)}) copy-start(f32[1,3072,256]{2,1,0:T(8,128)} %param.14) | copy-start | bytes 9437188
  103.7 3.8 %copy-start.6 = (f32[1,3072,256]{2,1,0:T(8,128)S(1)}, f32[1,3072,256]{2,1,0:T(8,128)}, u32[]{:S(2)}) copy-start(f32[1,3072,256]{2,1,0:T(8,128)} %param.15) | copy-start | bytes 9437188

commit v5 on v4

--- a/solution.py
+++ b/solution.py
@@ -56,16 +56,19 @@
 
 def norm_kernel(x_ref, c_ref, g_ref, u_ref, x_s, g_s, sems):
     g_in = pltpu.make_async_copy(g_ref, g_s, sems.at[0])
-    x_in = pltpu.make_async_copy(x_ref, x_s, sems.at[1])
-    c_in = pltpu.make_async_copy(c_ref, u_ref.at[1], sems.at[2])
-    for copy in (g_in, x_in, c_in):
+    c_in = pltpu.make_async_copy(c_ref, u_ref.at[1], sems.at[1])
+    tile = x_ref.shape[0] // 2
+    spans = [pl.ds(0, tile), pl.ds(tile, tile)]
+    x_in = [pltpu.make_async_copy(x_ref.at[span], x_s.at[span], sems.at[2 + i]) for i, span in enumerate(spans)]
+    for copy in (g_in, *x_in, c_in):
         copy.start()
     g_in.wait()
     gain = g_s[...].astype(jnp.float32).reshape(1, -1)
-    x_in.wait()
-    x = x_s[...].astype(jnp.float32)
-    scale = lax.rsqrt(jnp.mean(x * x, axis=1, keepdims=True) + norm_eps)
-    u_ref[0] = (x * scale * gain).astype(jnp.bfloat16)
+    for span, copy in zip(spans, x_in):
+        copy.wait()
+        x = x_s[span].astype(jnp.float32)
+        scale = lax.rsqrt(jnp.mean(x * x, axis=1, keepdims=True) + norm_eps)
+        u_ref[0, span] = (x * scale * gain).astype(jnp.bfloat16)
     c_in.wait()
 
 
@@ -78,7 +81,7 @@
         scratch_shapes=[
             pltpu.VMEM(x.shape, jnp.bfloat16),
             pltpu.VMEM(gain.shape, jnp.bfloat16),
-            pltpu.SemaphoreType.DMA((3,)),
+            pltpu.SemaphoreType.DMA((4,)),
         ],
         compiler_params=pltpu.CompilerParams(vmem_limit_bytes=60 * MIB),
         cost_estimate=CHEAP,
@@ -278,7 +281,7 @@
     pl.when(frag != 2)(functools.partial(add_gradient, right_t, n_s, out, total))
 
 
-def add_blocks(frag, blocks, weight, total, kind=jnp.float32):
+def add_blocks(frag, blocks, weight, total, kind=jnp.float32, cost=CHEAP):
     count, rows = len(blocks), len(blocks) * blocks[0].shape[1]
     _, d, cols = weight.shape
     return pl.pallas_call(
@@ -296,7 +299,7 @@
         ],
         input_output_aliases={count + 2: 0} if kind == jnp.float32 else {},
         compiler_params=pltpu.CompilerParams(vmem_limit_bytes=12 * MIB),
-        cost_estimate=CHEAP,
+        cost_estimate=cost,
         name="blocks",
     )(frag, *blocks, weight, total)
 
@@ -308,7 +311,8 @@
         grad = (own_ref[:, span] + other_ref[:, span].astype(jnp.float32)).T * (1.0 / tokens)
         moment_one = beta_one * m_ref[span, :] + (1.0 - beta_one) * grad
         moment_two = beta_two * v_ref[span, :] + (1.0 - beta_two) * grad * grad
-        step_inner = inner_lr * moment_one / (jnp.sqrt(moment_two) + adam_eps)
+        root = moment_two * lax.rsqrt(moment_two)
+        step_inner = inner_lr * moment_one / (root + adam_eps)
         out_s[span, :] = (mixed_ref[span, :] - mix_alpha * step_inner).astype(jnp.bfloat16)
         copy = pltpu.make_async_copy(out_s.at[span, :], out_ref.at[span, :], sems.at[i])
         copy.start()
@@ -404,7 +408,8 @@
     mixed = mix_alpha * w_rows(0, d).astype(jnp.float32) + (1.0 - mix_alpha) * global_new
 
     held, totals = gradients(frag, after(far, mixed), w_both, [*first, z_near], rights)
-    sib_total = add_blocks(frag, [z_cross], held[0], totals[0])
+    cost = pl.CostEstimate(flops=8 * z_cross.size * cols, bytes_accessed=3 * totals[0].size * 4, transcendentals=0)
+    sib_total = add_blocks(frag, [z_cross], held[0], totals[0], cost=cost)
     grad_sib = add_blocks(frag, [z_far], held[0], sib_total, jnp.bfloat16)
     grad_sib = lax.ppermute(grad_sib, "fsdp", SIBLING)
     grad_own = add_blocks(frag, [z_cross, z_far], held[1], totals[1])

time: 112 us -> 110 us (0.982)
  Pallas kernels: 34.8 us -> 31.3 us
  other arithmetic: 10.6 us -> 13.7 us
  local copies, waits for them, and re-layouts: 3.34 us -> 2.13 us
    select_n x2, other arithmetic: 0.67 us -> 3.32 us  [ordered(): jnp.where(second == 0, jnp.concatenate([first, other]), jnp.concatenate([...]
    pallas_call x3, Pallas kernels: 8.16 us -> 5.88 us  [add_blocks(): pl.pallas_call(functools.partial(step_kernel, count), out_shape=jax.Shape...]
    unnamed x24, local copies, waits for them, and re-layouts: 1.27 us -> 0.06 us
  transfers between devices with their start and end apart: 15 -> 15, of which waited for: 8 -> 8; matrix products, arithmetic and copies ran while one was open for 11% -> 14% of each run, Pallas kernels for 26% -> 25%
where the time goes in v5:
time: 110 us; the launch traced here: 109 us
  waiting for transfers between devices  33.5 us (30%)
  Pallas kernels  31.3 us (28%)
  starting transfers between devices  27 us (25%)
  other arithmetic  13.7 us (12%)
  local copies, waits for them, and re-layouts  2.13 us (2%)
  between operations  1.74 us (2%)
    pallas_call x2, Pallas kernels, forward(): pl.pallas_call(functools.partial(forward_kernel, count), out_shape=jax.Sh...  12 us
    ppermute x1, waiting for transfers between devices, per_device(): lax.ppermute(after(w_rows((1 - h) * half, half), own), everyone, HALF_PAIR)  10.2 us
    pallas_call x1, Pallas kernels, gradients(): pl.pallas_call(functools.partial(gradient_kernel, past, tuple(spans)), ou...  8.17 us
    ppermute x1, waiting for transfers between devices, per_device(): got = lax.ppermute(sent, everyone, QUARTER_PAIR)  7.23 us
    pallas_call x3, Pallas kernels, add_blocks(): pl.pallas_call(functools.partial(step_kernel, count), out_shape=jax.Shape...  5.88 us
    ppermute x1, waiting for transfers between devices, per_device(): z_own = other_z(own)  5.73 us
    ppermute x1, waiting for transfers between devices, per_device(): lax.ppermute(mine, everyone, HALF_PAIR)  5.41 us
    add x1, other arithmetic, per_device(): mix_alpha * w_rows(0, d).astype(jnp.float32)  5.36 us
  transfers between devices with their start and end apart: 15, of which 8 were waited for; matrix products, arithmetic and copies ran while one was open for 14% of the time, Pallas kernels for 25%

profile of v5, /device:TPU:1, one launch (start us, length us, event | category | flops | bytes accessed | tf_op | source)
XLA Modules:
  0.0 109.4 jit_solution(5430710044235691753)
XLA Ops:
  0.6 1.5 %collective-permute-start.6 = (bf16[3,3072,256]{2,1,0:T(8,128)(2,1)}, bf16[3,3072,256]{2,1,0:T(8,128)(2,1)}, u32[]{:S(2)}, u32[]{:S(2)}) collective-permute-start(bf16[3,3072,256]{2,1,0:T(8,128)(2,1)} %bitcast.19), channel_id=1, source_target_pairs={{0,1},{1,0},{2,3},{3,2},{4,5},{5,4},{6,7},{7,6},{8,9},{9,8},{10,11... | collective-permute-start | bytes 14155784 | tf_op jit(solution)/shard_map/ppermute | solution.py:347
  2.1 2.6 %norm.1.refs_0_ = bf16[2,128,3072]{2,1,0:T(8,128)(2,1)} custom-call(bf16[128,3072]{1,0:T(8,128)(2,1)} %bitcast.28, bf16[128,3072]{1,0:T(8,128)(2,1)} %bitcast.29, bf16[3072]{0:T(1024)(128)(2,1)} %g_ref.1), custom_call_target="tpu_custom_call" | custom-call | flops 1 | bytes 1 | tf_op jit(solution)/shard_map/norm/pallas_call | solution.py:76
  4.7 1.8 %collective-permute-start.1 = (bf16[2,128,3072]{2,1,0:T(8,128)(2,1)}, bf16[2,128,3072]{2,1,0:T(8,128)(2,1)S(1)}, u32[]{:S(2)}, u32[]{:S(2)}) collective-permute-start(bf16[2,128,3072]{2,1,0:T(8,128)(2,1)} %norm.1.refs_0_), channel_id=1, source_target_pairs={{0,8},{1,9},{2,10},{3,11},{4,12},{5,13},{6,14},{7,15},{8,0},{9,1},... | collective-permute-start | bytes 4718600 | tf_op jit(solution)/shard_map/ppermute | solution.py:377
  6.5 2.7 %collective-permute-start.2 = (bf16[2,128,3072]{2,1,0:T(8,128)(2,1)}, bf16[2,128,3072]{2,1,0:T(8,128)(2,1)S(1)}, u32[]{:S(2)}, u32[]{:S(2)}) collective-permute-start(bf16[2,128,3072]{2,1,0:T(8,128)(2,1)} %norm.1.refs_0_), channel_id=1, source_target_pairs={{0,2},{1,7},{2,4},{3,1},{4,6},{5,3},{6,0},{7,5},{8,10},{9,15},{10,... | collective-permute-start | bytes 4718600 | tf_op jit(solution)/shard_map/ppermute | solution.py:376
  9.9 2.1 %dynamic-slice_bitcast_fusion = bf16[1536,256]{1,0:T(8,128)(2,1)} fusion(bf16[1,3,3072,256]{3,2,1,0:T(8,128)(2,1)} %param.13, s32[]{:T(128)S(6)} %select_n.71, s32[]{:T(128)S(6)} %select_n.72), kind=kLoop, calls=%fused_computation.18 | loop fusion | bytes 1572872 | tf_op jit(solution)/shard_map/squeeze | solution.py:365
  12.0 2.5 %collective-permute-start.3 = (bf16[1536,256]{1,0:T(8,128)(2,1)}, bf16[1536,256]{1,0:T(8,128)(2,1)}, u32[]{:S(2)}, u32[]{:S(2)}) collective-permute-start(bf16[1536,256]{1,0:T(8,128)(2,1)} %dynamic-slice_bitcast_fusion), channel_id=1, source_target_pairs={{0,16},{1,49},{2,18},{3,51},{4,20},{5,53},{6,22},{7,55},{8,24},{9,... | collective-permute-start | bytes 2359304 | tf_op jit(solution)/shard_map/ppermute | solution.py:379
  14.5 0.0 collective-permute-start
  14.5 10.2 %collective-permute-done.3 = bf16[1536,256]{1,0:T(8,128)(2,1)} collective-permute-done((bf16[1536,256]{1,0:T(8,128)(2,1)}, bf16[1536,256]{1,0:T(8,128)(2,1)}, u32[]{:S(2)}, u32[]{:S(2)}) %collective-permute-start.3) | collective-permute-done | bytes 786464 | tf_op jit(solution)/shard_map/ppermute | solution.py:379
  24.7 2.3 %fusion.3 = f16[768,256]{1,0:T(8,128)(2,1)} fusion(f32[3072,256]{1,0:T(8,128)} %param.16, s32[]{:T(128)S(6)} %select_n.74, bf16[1536,256]{1,0:T(8,128)(2,1)} %collective-permute-done.3, s32[]{:T(128)S(6)} %select_n.75, bf16[1,3,3072,256]{3,2,1,0:T(8,128)(2,1)} %param.13, s32[]{:T(128)S(6)} %select_n.71), kind=kLoop, calls=%fused_computation.11 | loop fusion | flops 1376256 | bytes 1966092 | tf_op jit(solution)/shard_map/convert_element_type | solution.py:374
  27.0 0.0 collective-permute-start.4
  27.0 7.2 %collective-permute-done.4 = f16[768,256]{1,0:T(8,128)(2,1)S(1)} collective-permute-done((f16[768,256]{1,0:T(8,128)(2,1)}, f16[768,256]{1,0:T(8,128)(2,1)S(1)}, u32[]{:S(2)}, u32[]{:S(2)}) %collective-permute-start.4) | collective-permute-done | bytes 393248 | tf_op jit(solution)/shard_map/ppermute | solution.py:388
  34.2 1.6 %fusion.7 = f16[768,256]{1,0:T(8,128)(2,1)S(1)} fusion(f16[768,256]{1,0:T(8,128)(2,1)S(1)} %collective-permute-done.4, f32[3072,256]{1,0:T(8,128)} %param.16, s32[]{:T(128)S(6)} %select_n.69, bf16[1536,256]{1,0:T(8,128)(2,1)} %collective-permute-done.3, s32[]{:T(128)S(6)} %select_n.73, bf16[1,3,3072,256]{3,2,1,0:T(8,128)(2,1)} %param.13, s32[]{:T(128)S(6)} %select_n.71), kind=kLoop, calls=%fused_computation.16 | loop fusion | flops 1966080 | bytes 2359308 | tf_op jit(solution)/shard_map/convert_element_type | solution.py:374
  35.8 5.7 %collective-permute-done.1.refs_3_ = bf16[2,128,3072]{2,1,0:T(8,128)(2,1)S(1)} collective-permute-done((bf16[2,128,3072]{2,1,0:T(8,128)(2,1)}, bf16[2,128,3072]{2,1,0:T(8,128)(2,1)S(1)}, u32[]{:S(2)}, u32[]{:S(2)}) %collective-permute-start.1) | collective-permute-done | bytes 1572896 | tf_op jit(solution)/shard_map/ppermute | solution.py:377
  41.6 0.0 collective-permute-done.2.refs_1_
  41.6 2.7 %collective-permute-start.11 = (bf16[2,128,3072]{2,1,0:T(8,128)(2,1)S(1)}, bf16[2,128,3072]{2,1,0:T(8,128)(2,1)}, u32[]{:S(2)}, u32[]{:S(2)}) collective-permute-start(bf16[2,128,3072]{2,1,0:T(8,128)(2,1)S(1)} %collective-permute-done.1.refs_3_), channel_id=1, source_target_pairs={{0,2},{1,7},{2,4},{3,1},{4,6},{5,3},{6,0},{7,5},{8,10},{9,15},{10,... | collective-permute-start | bytes 4718600 | tf_op jit(solution)/shard_map/ppermute | solution.py:392
  44.3 3.3 %collective-permute-start.5 = (f16[768,256]{1,0:T(8,128)(2,1)S(1)}, f16[768,256]{1,0:T(8,128)(2,1)}, u32[]{:S(2)}, u32[]{:S(2)}) collective-permute-start(f16[768,256]{1,0:T(8,128)(2,1)S(1)} %fusion.7), channel_id=1, source_target_pairs={{0,64},{16,80},{32,96},{48,112},{64,0},{80,16},{96,32},{112,48},{1... | collective-permute-start | bytes 1179656 | tf_op jit(solution)/shard_map/ppermute | solution.py:391
  47.6 0.0 collective-permute-done.refs_2_
  47.6 0.0 collective-permute-done.6.refs_4_.refs_1_.refs_7_
  47.6 7.6 %forward.2.refs_5_ = bf16[512,512]{1,0:T(8,128)(2,1)} custom-call(s32[1]{0:T(128)} %bitcast.6.frag_ref, bf16[2,128,3072]{2,1,0:T(8,128)(2,1)} %norm.1.refs_0_, bf16[2,128,3072]{2,1,0:T(8,128)(2,1)} %copy-done.3, bf16[2,128,3072]{2,1,0:T(8,128)(2,1)} %collective-permute-done.refs_2_, bf16[2,128,3072]{2,1,0:T(8,128)(2,1)} %copy-done.1, ...), custom_call_target="tpu_custom_call" | custom-call | flops 1 | bytes 1 | tf_op jit(solution)/shard_map/forward/pallas_call | solution.py:181
  55.2 1.6 %collective-permute-done.5 = f16[768,256]{1,0:T(8,128)(2,1)} collective-permute-done((f16[768,256]{1,0:T(8,128)(2,1)S(1)}, f16[768,256]{1,0:T(8,128)(2,1)}, u32[]{:S(2)}, u32[]{:S(2)}) %collective-permute-start.5) | collective-permute-done | bytes 393248 | tf_op jit(solution)/shard_map/ppermute | solution.py:391
  56.8 1.1 %add_convert_fusion = f16[768,256]{1,0:T(8,128)(2,1)S(1)} fusion(f16[768,256]{1,0:T(8,128)(2,1)} %collective-permute-done.5, f16[768,256]{1,0:T(8,128)(2,1)S(1)} %fusion.7), kind=kLoop, calls=%fused_computation.17 | loop fusion | flops 786432 | bytes 1179648 | tf_op jit(solution)/shard_map/convert_element_type | solution.py:397
  57.9 1.3 %collective-permute-start.7 = (f16[768,256]{1,0:T(8,128)(2,1)S(1)}, f16[768,256]{1,0:T(8,128)(2,1)}, u32[]{:S(2)}, u32[]{:S(2)}) collective-permute-start(f16[768,256]{1,0:T(8,128)(2,1)S(1)} %add_convert_fusion), channel_id=1, source_target_pairs={{0,48},{1,17},{2,50},{3,19},{4,52},{5,21},{6,54},{7,23},{8,56},{9,... | collective-permute-start | bytes 1179656 | tf_op jit(solution)/shard_map/ppermute | solution.py:400
  59.2 1.8 %collective-permute-start.8 = (f16[768,256]{1,0:T(8,128)(2,1)S(1)}, f16[768,256]{1,0:T(8,128)(2,1)}, u32[]{:S(2)}, u32[]{:S(2)}) collective-permute-start(f16[768,256]{1,0:T(8,128)(2,1)S(1)} %add_convert_fusion), channel_id=1, source_target_pairs={{0,16},{1,49},{2,18},{3,51},{4,20},{5,53},{6,22},{7,55},{8,24},{9,... | collective-permute-start | bytes 1179656 | tf_op jit(solution)/shard_map/ppermute | solution.py:400
  61.0 0.6 collective-permute-start.9
  61.7 0.4 collective-permute-start.13
  62.1 0.0 collective-permute-done.11.refs_0_.refs_4_
  62.1 1.1 %collective-permute-start.10 = (bf16[2,128,3072]{2,1,0:T(8,128)(2,1)}, bf16[2,128,3072]{2,1,0:T(8,128)(2,1)S(1)}, u32[]{:S(2)}, u32[]{:S(2)}) collective-permute-start(bf16[2,128,3072]{2,1,0:T(8,128)(2,1)} %collective-permute-done.refs_2_), channel_id=1, source_target_pairs={{0,8},{1,9},{2,10},{3,11},{4,12},{5,13},{6,14},{7,15},{8,0},{9,1},... | collective-permute-start | bytes 4718600 | tf_op jit(solution)/shard_map/ppermute | solution.py:399
  63.2 4.4 %forward.3.refs_6_ = bf16[128,512]{1,0:T(8,128)(2,1)} custom-call(s32[1]{0:T(128)} %bitcast.6.frag_ref, bf16[2,128,3072]{2,1,0:T(8,128)(2,1)} %collective-permute-done.11.refs_0_.refs_4_, bf16[3,3072,256]{2,1,0:T(8,128)(2,1)} %collective-permute-done.6.refs_4_.refs_1_.refs_7_, bf16[3,3072,256]{2,1,0:T(8,128)(2,1)} %bitcast.21), custom_call_target="tpu_custom_call" | custom-call | flops 1 | bytes 1 | tf_op jit(solution)/shard_map/forward/pallas_call | solution.py:181
  67.6 0.0 copy-start.9
  67.7 0.0 collective-permute-done.7
  67.7 3.5 %collective-permute-start.12 = (bf16[2,128,3072]{2,1,0:T(8,128)(2,1)}, bf16[2,128,3072]{2,1,0:T(8,128)(2,1)S(1)}, u32[]{:S(2)}, u32[]{:S(2)}) collective-permute-start(bf16[2,128,3072]{2,1,0:T(8,128)(2,1)} %collective-permute-done.11.refs_0_.refs_4_), channel_id=1, source_target_pairs={{0,2},{1,7},{2,4},{3,1},{4,6},{5,3},{6,0},{7,5},{8,10},{9,15},{10,... | collective-permute-start | bytes 4718600 | tf_op jit(solution)/shard_map/ppermute | solution.py:403
  71.2 1.5 %maximum_select_fusion.1 = f16[1536,256]{1,0:T(8,128)(2,1)S(1)} fusion(f16[768,256]{1,0:T(8,128)(2,1)} %collective-permute-done.7, f16[768,256]{1,0:T(8,128)(2,1)S(1)} %add_convert_fusion, pred[]{:T(512)S(6)} %eq.14), kind=kLoop, calls=%fused_computation.6 | loop fusion | flops 1179648 | bytes 1572865 | tf_op jit(solution)/shard_map/jit(_where)/select_n | solution.py:371
  72.7 5.4 %collective-permute-done.8 = f16[768,256]{1,0:T(8,128)(2,1)} collective-permute-done((f16[768,256]{1,0:T(8,128)(2,1)S(1)}, f16[768,256]{1,0:T(8,128)(2,1)}, u32[]{:S(2)}, u32[]{:S(2)}) %collective-permute-start.8) | collective-permute-done | bytes 393248 | tf_op jit(solution)/shard_map/ppermute | solution.py:400
  78.1 0.4 collective-permute-done.9
  78.5 1.8 %maximum_select_fusion.2 = f16[1536,256]{1,0:T(8,128)(2,1)S(1)} fusion(f16[768,256]{1,0:T(8,128)(2,1)} %collective-permute-done.9, f16[768,256]{1,0:T(8,128)(2,1)} %collective-permute-done.8, pred[]{:T(512)S(6)} %eq.14), kind=kLoop, calls=%fused_computation.7 | loop fusion | flops 1179648 | bytes 1572865 | tf_op jit(solution)/shard_map/jit(_where)/select_n | solution.py:371
  80.3 0.0 slice-start.1
  80.3 0.0 copy-start
  80.4 5.4 %fusion = (f32[3072,256]{1,0:T(8,128)S(1)}, f32[3072,256]{1,0:T(8,128)}, f32[3072,256]{1,0:T(8,128)}) fusion(bf16[1,3,3072,256]{3,2,1,0:T(8,128)(2,1)} %param.13, s32[]{:T(128)S(6)} %select_n.71, f32[3072,256]{1,0:T(8,128)S(1)} %copy-done.9, f16[1536,256]{1,0:T(8,128)(2,1)S(1)} %maximum_select_fusion.1, f16[1536,256]{1,0:T(8,128)(2,1)S(1)} %maximum_select_fusion.2, ...), kind=kLoop, calls=%fused_computation.1 | loop fusion | flops 11010048 | bytes 18874372 | tf_op jit(solution)/shard_map/add | solution.py:408
  85.8 0.0 collective-permute-done.13.block
  85.8 8.2 %gradients.1 = (bf16[3,3072,256]{2,1,0:T(8,128)(2,1)S(1)}, bf16[3,3072,256]{2,1,0:T(8,128)(2,1)S(1)}, f32[256,3072]{1,0:T(8,128)S(1)}, f32[256,3072]{1,0:T(8,128)S(1)}) custom-call(s32[1]{0:T(128)} %bitcast.6.frag_ref, bf16[2,128,3072]{2,1,0:T(8,128)(2,1)} %collective-permute-done.13.block, bf16[2,128,3072]{2,1,0:T(8,128)(2,1)S(1)} %copy-done, ...), custom_call_target="tpu_custom_call" | custom-call | flops 1 | bytes 1 | tf_op jit(solution)/shard_map/gradients/pallas_call | solution.py:247
  94.0 2.5 %collective-permute-done.10.refs_0_ = bf16[2,128,3072]{2,1,0:T(8,128)(2,1)S(1)} collective-permute-done((bf16[2,128,3072]{2,1,0:T(8,128)(2,1)}, bf16[2,128,3072]{2,1,0:T(8,128)(2,1)S(1)}, u32[]{:S(2)}, u32[]{:S(2)}) %collective-permute-start.10) | collective-permute-done | bytes 1572896 | tf_op jit(solution)/shard_map/ppermute | solution.py:399
  96.5 1.8 %blocks.4.refs_2_ = f32[256,3072]{1,0:T(8,128)S(1)} custom-call(s32[1]{0:T(128)} %bitcast.6.frag_ref, bf16[2,128,3072]{2,1,0:T(8,128)(2,1)S(1)} %collective-permute-done.10.refs_0_, bf16[3,3072,256]{2,1,0:T(8,128)(2,1)S(1)} %get-tuple-element.27.refs_1_, f32[256,3072]{1,0:T(8,128)S(1)} %get-tuple-element.28.refs_2_), custom_call_target="tpu_custom_call", output_to_operand_aliasing={{}: (3, {})} | custom-call | flops 1610612736 | bytes 9437184 | tf_op jit(solution)/shard_map/blocks/pallas_call | solution.py:287
  98.3 0.0 collective-permute-done.12.refs_1_.refs_0_
  98.3 1.5 %blocks.5 = bf16[256,3072]{1,0:T(8,128)(2,1)S(1)} custom-call(s32[1]{0:T(128)} %bitcast.6.frag_ref, bf16[2,128,3072]{2,1,0:T(8,128)(2,1)S(1)} %collective-permute-done.12.refs_1_.refs_0_, bf16[3,3072,256]{2,1,0:T(8,128)(2,1)S(1)} %get-tuple-element.27.refs_1_, f32[256,3072]{1,0:T(8,128)S(1)} %blocks.4.refs_2_), custom_call_target="tpu_custom_call" | custom-call | flops 1 | bytes 1 | tf_op jit(solution)/shard_map/blocks/pallas_call | solution.py:287
  99.8 3.6 %collective-permute-start.14 = (bf16[256,3072]{1,0:T(8,128)(2,1)S(1)}, bf16[256,3072]{1,0:T(8,128)(2,1)S(1)}, u32[]{:S(2)}, u32[]{:S(2)}) collective-permute-start(bf16[256,3072]{1,0:T(8,128)(2,1)S(1)} %blocks.5), channel_id=1, source_target_pairs={{0,1},{1,0},{2,3},{3,2},{4,5},{5,4},{6,7},{7,6},{8,9},{9,8},{10,11... | collective-permute-start | bytes 4718600 | tf_op jit(solution)/shard_map/ppermute | solution.py:414
  103.4 2.6 %blocks.3.own_ref = f32[256,3072]{1,0:T(8,128)S(1)} custom-call(s32[1]{0:T(128)} %bitcast.6.frag_ref, bf16[2,128,3072]{2,1,0:T(8,128)(2,1)S(1)} %collective-permute-done.10.refs_0_, bf16[2,128,3072]{2,1,0:T(8,128)(2,1)S(1)} %collective-permute-done.12.refs_1_.refs_0_, ...), custom_call_target="tpu_custom_call", output_to_operand_aliasing={{}: (4, {})} | custom-call | flops 1 | bytes 1 | tf_op jit(solution)/shard_map/blocks/pallas_call | solution.py:287
  106.0 0.5 collective-permute-done.14.other_ref
  106.4 2.8 %adam.1 = bf16[3072,256]{1,0:T(8,128)(2,1)} custom-call(f32[256,3072]{1,0:T(8,128)S(1)} %blocks.3.own_ref, bf16[256,3072]{1,0:T(8,128)(2,1)S(1)} %collective-permute-done.14.other_ref, f32[3072,256]{1,0:T(8,128)S(1)} %bitcast.25, f32[3072,256]{1,0:T(8,128)S(1)} %bitcast.26, f32[3072,256]{1,0:T(8,128)S(1)} %get-tuple-element.29.mixed_ref), custom_call_target="tpu_custom_call" | custom-call | flops 1 | bytes 1 | tf_op jit(solution)/shard_map/adam/pallas_call | solution.py:327
  (22 shorter events, 0.0 us)
Async XLA Ops:
  0.6 47.0 %collective-permute-start.6 = (bf16[3,3072,256]{2,1,0:T(8,128)(2,1)}, bf16[3,3072,256]{2,1,0:T(8,128)(2,1)}, u32[]{:S(2)}, u32[]{:S(2)}) collective-permute-start(bf16[3,3072,256]{2,1,0:T(8,128)(2,1)} %bitcast.19), channel_id=1, source_target_pairs={{0,1},{1,0},{2,3},{3,2},{4,5},{5,4},{6,7},{7,6},{8,9},{9,8},{10,11... | collective-permute-start | bytes 14155784 | tf_op jit(solution)/shard_map/ppermute | solution.py:347
  4.7 36.9 %collective-permute-start.1 = (bf16[2,128,3072]{2,1,0:T(8,128)(2,1)}, bf16[2,128,3072]{2,1,0:T(8,128)(2,1)S(1)}, u32[]{:S(2)}, u32[]{:S(2)}) collective-permute-start(bf16[2,128,3072]{2,1,0:T(8,128)(2,1)} %norm.1.refs_0_), channel_id=1, source_target_pairs={{0,8},{1,9},{2,10},{3,11},{4,12},{5,13},{6,14},{7,15},{8,0},{9,1},... | collective-permute-start | bytes 4718600 | tf_op jit(solution)/shard_map/ppermute | solution.py:377
  6.5 35.1 %collective-permute-start.2 = (bf16[2,128,3072]{2,1,0:T(8,128)(2,1)}, bf16[2,128,3072]{2,1,0:T(8,128)(2,1)S(1)}, u32[]{:S(2)}, u32[]{:S(2)}) collective-permute-start(bf16[2,128,3072]{2,1,0:T(8,128)(2,1)} %norm.1.refs_0_), channel_id=1, source_target_pairs={{0,2},{1,7},{2,4},{3,1},{4,6},{5,3},{6,0},{7,5},{8,10},{9,15},{10,... | collective-permute-start | bytes 4718600 | tf_op jit(solution)/shard_map/ppermute | solution.py:376
  12.0 12.7 %collective-permute-start.3 = (bf16[1536,256]{1,0:T(8,128)(2,1)}, bf16[1536,256]{1,0:T(8,128)(2,1)}, u32[]{:S(2)}, u32[]{:S(2)}) collective-permute-start(bf16[1536,256]{1,0:T(8,128)(2,1)} %dynamic-slice_bitcast_fusion), channel_id=1, source_target_pairs={{0,16},{1,49},{2,18},{3,51},{4,20},{5,53},{6,22},{7,55},{8,24},{9,... | collective-permute-start | bytes 2359304 | tf_op jit(solution)/shard_map/ppermute | solution.py:379
  14.5 33.1 %collective-permute-start = (bf16[2,128,3072]{2,1,0:T(8,128)(2,1)}, bf16[2,128,3072]{2,1,0:T(8,128)(2,1)}, u32[]{:S(2)}, u32[]{:S(2)}) collective-permute-start(bf16[2,128,3072]{2,1,0:T(8,128)(2,1)} %norm.1.refs_0_), channel_id=1, source_target_pairs={{0,7},{1,2},{2,1},{3,4},{4,3},{5,6},{6,5},{7,0},{8,15},{9,10},{10,... | collective-permute-start | bytes 4718600 | tf_op jit(solution)/shard_map/ppermute | solution.py:378
  27.0 7.2 %collective-permute-start.4 = (f16[768,256]{1,0:T(8,128)(2,1)}, f16[768,256]{1,0:T(8,128)(2,1)S(1)}, u32[]{:S(2)}, u32[]{:S(2)}) collective-permute-start(f16[768,256]{1,0:T(8,128)(2,1)} %fusion.3), channel_id=1, source_target_pairs={{0,48},{1,17},{2,50},{3,19},{4,52},{5,21},{6,54},{7,23},{8,56},{9,... | collective-permute-start | bytes 1179656 | tf_op jit(solution)/shard_map/ppermute | solution.py:388
  41.6 6.0 %copy-start.1 = (bf16[2,128,3072]{2,1,0:T(8,128)(2,1)}, bf16[2,128,3072]{2,1,0:T(8,128)(2,1)S(1)}, u32[]{:S(2)}) copy-start(bf16[2,128,3072]{2,1,0:T(8,128)(2,1)S(1)} %collective-permute-done.1.refs_3_) | copy-start | bytes 4718596
  41.6 6.0 %copy-start.3 = (bf16[2,128,3072]{2,1,0:T(8,128)(2,1)}, bf16[2,128,3072]{2,1,0:T(8,128)(2,1)S(1)}, u32[]{:S(2)}) copy-start(bf16[2,128,3072]{2,1,0:T(8,128)(2,1)S(1)} %collective-permute-done.2.refs_1_) | copy-start | bytes 4718596
  41.6 20.6 %collective-permute-start.11 = (bf16[2,128,3072]{2,1,0:T(8,128)(2,1)S(1)}, bf16[2,128,3072]{2,1,0:T(8,128)(2,1)}, u32[]{:S(2)}, u32[]{:S(2)}) collective-permute-start(bf16[2,128,3072]{2,1,0:T(8,128)(2,1)S(1)} %collective-permute-done.1.refs_3_), channel_id=1, source_target_pairs={{0,2},{1,7},{2,4},{3,1},{4,6},{5,3},{6,0},{7,5},{8,10},{9,15},{10,... | collective-permute-start | bytes 4718600 | tf_op jit(solution)/shard_map/ppermute | solution.py:392
  44.3 12.5 %collective-permute-start.5 = (f16[768,256]{1,0:T(8,128)(2,1)S(1)}, f16[768,256]{1,0:T(8,128)(2,1)}, u32[]{:S(2)}, u32[]{:S(2)}) collective-permute-start(f16[768,256]{1,0:T(8,128)(2,1)S(1)} %fusion.7), channel_id=1, source_target_pairs={{0,64},{16,80},{32,96},{48,112},{64,0},{80,16},{96,32},{112,48},{1... | collective-permute-start | bytes 1179656 | tf_op jit(solution)/shard_map/ppermute | solution.py:391
  57.9 9.7 %collective-permute-start.7 = (f16[768,256]{1,0:T(8,128)(2,1)S(1)}, f16[768,256]{1,0:T(8,128)(2,1)}, u32[]{:S(2)}, u32[]{:S(2)}) collective-permute-start(f16[768,256]{1,0:T(8,128)(2,1)S(1)} %add_convert_fusion), channel_id=1, source_target_pairs={{0,48},{1,17},{2,50},{3,19},{4,52},{5,21},{6,54},{7,23},{8,56},{9,... | collective-permute-start | bytes 1179656 | tf_op jit(solution)/shard_map/ppermute | solution.py:400
  59.2 18.9 %collective-permute-start.8 = (f16[768,256]{1,0:T(8,128)(2,1)S(1)}, f16[768,256]{1,0:T(8,128)(2,1)}, u32[]{:S(2)}, u32[]{:S(2)}) collective-permute-start(f16[768,256]{1,0:T(8,128)(2,1)S(1)} %add_convert_fusion), channel_id=1, source_target_pairs={{0,16},{1,49},{2,18},{3,51},{4,20},{5,53},{6,22},{7,55},{8,24},{9,... | collective-permute-start | bytes 1179656 | tf_op jit(solution)/shard_map/ppermute | solution.py:400
  61.0 17.5 %collective-permute-start.9 = (f16[768,256]{1,0:T(8,128)(2,1)S(1)}, f16[768,256]{1,0:T(8,128)(2,1)}, u32[]{:S(2)}, u32[]{:S(2)}) collective-permute-start(f16[768,256]{1,0:T(8,128)(2,1)S(1)} %add_convert_fusion), channel_id=1, source_target_pairs={{0,32},{16,48},{32,0},{48,16},{64,96},{80,112},{96,64},{112,80},{1... | collective-permute-start | bytes 1179656 | tf_op jit(solution)/shard_map/ppermute | solution.py:401
  61.7 24.1 %collective-permute-start.13 = (bf16[2,128,3072]{2,1,0:T(8,128)(2,1)}, bf16[2,128,3072]{2,1,0:T(8,128)(2,1)}, u32[]{:S(2)}, u32[]{:S(2)}) collective-permute-start(bf16[2,128,3072]{2,1,0:T(8,128)(2,1)} %copy-done.3), channel_id=1, source_target_pairs={{0,2},{1,7},{2,4},{3,1},{4,6},{5,3},{6,0},{7,5},{8,10},{9,15},{10,... | collective-permute-start | bytes 4718600 | tf_op jit(solution)/shard_map/ppermute | solution.py:393
  62.1 34.3 %collective-permute-start.10 = (bf16[2,128,3072]{2,1,0:T(8,128)(2,1)}, bf16[2,128,3072]{2,1,0:T(8,128)(2,1)S(1)}, u32[]{:S(2)}, u32[]{:S(2)}) collective-permute-start(bf16[2,128,3072]{2,1,0:T(8,128)(2,1)} %collective-permute-done.refs_2_), channel_id=1, source_target_pairs={{0,8},{1,9},{2,10},{3,11},{4,12},{5,13},{6,14},{7,15},{8,0},{9,1},... | collective-permute-start | bytes 4718600 | tf_op jit(solution)/shard_map/ppermute | solution.py:399
  67.6 12.7 %copy-start.9 = (f32[3072,256]{1,0:T(8,128)S(1)}, f32[3072,256]{1,0:T(8,128)}, u32[]{:S(2)}) copy-start(f32[3072,256]{1,0:T(8,128)} %param.16) | copy-start | bytes 9437188
  67.7 30.6 %collective-permute-start.12 = (bf16[2,128,3072]{2,1,0:T(8,128)(2,1)}, bf16[2,128,3072]{2,1,0:T(8,128)(2,1)S(1)}, u32[]{:S(2)}, u32[]{:S(2)}) collective-permute-start(bf16[2,128,3072]{2,1,0:T(8,128)(2,1)} %collective-permute-done.11.refs_0_.refs_4_), channel_id=1, source_target_pairs={{0,2},{1,7},{2,4},{3,1},{4,6},{5,3},{6,0},{7,5},{8,10},{9,15},{10,... | collective-permute-start | bytes 4718600 | tf_op jit(solution)/shard_map/ppermute | solution.py:403
  78.5 7.3 %slice-start = ((s8[4718592]{0:T(1024)(128)(4,1)}), s8[4194304]{0:T(1024)(128)(4,1)S(1)}, s32[]{:S(2)}) async-start(s8[4718592]{0:T(1024)(128)(4,1)} %bitcast.22), calls=%async_computation | async-start | bytes 8388608
  80.3 5.4 %slice-start.1 = ((s8[4718592]{0:T(1024)(128)(4,1)}), s8[524288]{0:T(1024)(128)(4,1)S(1)}, s32[]{:S(2)}) async-start(s8[4718592]{0:T(1024)(128)(4,1)} %bitcast.22), calls=%async_computation.1 | async-start | bytes 1048576
  80.3 5.4 %copy-start = (bf16[2,128,3072]{2,1,0:T(8,128)(2,1)S(1)}, bf16[2,128,3072]{2,1,0:T(8,128)(2,1)}, u32[]{:S(2)}) copy-start(bf16[2,128,3072]{2,1,0:T(8,128)(2,1)} %norm.1.refs_0_) | copy-start | bytes 4718596
  80.4 5.4 %copy-start.2 = (bf16[2,128,3072]{2,1,0:T(8,128)(2,1)S(1)}, bf16[2,128,3072]{2,1,0:T(8,128)(2,1)}, u32[]{:S(2)}) copy-start(bf16[2,128,3072]{2,1,0:T(8,128)(2,1)} %copy-done.1) | copy-start | bytes 4718596
  80.4 5.4 %copy-start.4 = (bf16[2,128,3072]{2,1,0:T(8,128)(2,1)S(1)}, bf16[2,128,3072]{2,1,0:T(8,128)(2,1)}, u32[]{:S(2)}) copy-start(bf16[2,128,3072]{2,1,0:T(8,128)(2,1)} %copy-done.3) | copy-start | bytes 4718596
  80.4 5.4 %copy-start.7 = (bf16[512,512]{1,0:T(8,128)(2,1)S(1)}, bf16[512,512]{1,0:T(8,128)(2,1)}, u32[]{:S(2)}) copy-start(bf16[512,512]{1,0:T(8,128)(2,1)} %forward.2.refs_5_) | copy-start | bytes 1572868
  80.4 5.4 %copy-start.8 = (bf16[128,512]{1,0:T(8,128)(2,1)S(1)}, bf16[128,512]{1,0:T(8,128)(2,1)}, u32[]{:S(2)}) copy-start(bf16[128,512]{1,0:T(8,128)(2,1)} %forward.3.refs_6_) | copy-start | bytes 393220
  99.8 6.6 %collective-permute-start.14 = (bf16[256,3072]{1,0:T(8,128)(2,1)S(1)}, bf16[256,3072]{1,0:T(8,128)(2,1)S(1)}, u32[]{:S(2)}, u32[]{:S(2)}) collective-permute-start(bf16[256,3072]{1,0:T(8,128)(2,1)S(1)} %blocks.5), channel_id=1, source_target_pairs={{0,1},{1,0},{2,3},{3,2},{4,5},{5,4},{6,7},{7,6},{8,9},{9,8},{10,11... | collective-permute-start | bytes 4718600 | tf_op jit(solution)/shard_map/ppermute | solution.py:414
  103.4 3.0 %copy-start.5 = (f32[1,3072,256]{2,1,0:T(8,128)S(1)}, f32[1,3072,256]{2,1,0:T(8,128)}, u32[]{:S(2)}) copy-start(f32[1,3072,256]{2,1,0:T(8,128)} %param.14) | copy-start | bytes 9437188
  103.4 3.0 %copy-start.6 = (f32[1,3072,256]{2,1,0:T(8,128)S(1)}, f32[1,3072,256]{2,1,0:T(8,128)}, u32[]{:S(2)}) copy-start(f32[1,3072,256]{2,1,0:T(8,128)} %param.15) | copy-start | bytes 9437188

commit v6 on v5

--- a/solution.py
+++ b/solution.py
@@ -267,15 +267,16 @@
 
 def step_kernel(count, frag_ref, *refs):
     blocks, (weight, total, out) = refs[:count], refs[count : count + 3]
-    n_s, c_s, up_s, dh_s, right_s, sems = refs[count + 3 :]
+    n_s, c_s, up_s, dh_s, right_s = refs[count + 3 :]
     rows = blocks[0].shape[1]
     frag = frag_ref[0]
-    loads = Loads(frag, sems, 2 * count)
-    for kind, side, target in (("n", 0, n_s), ("c", 1, c_s)):
+    if count == 1:
+        n_s, c_s = blocks[0].at[0], blocks[0].at[1]
+    else:
         for k, block in enumerate(blocks):
-            loads.add((kind, 0), block.at[side], target.at[pl.ds(k * rows, rows)])
-    loads.start()
-    right_side(frag, loads, 0, n_s, c_s, weight, up_s, dh_s, right_s)
+            n_s[k * rows : (k + 1) * rows, :] = block[0]
+            c_s[k * rows : (k + 1) * rows, :] = block[1]
+    right_side(frag, Loads(frag, None, 0), 0, n_s, c_s, weight, up_s, dh_s, right_s)
     right_t = right_s[...].T
     pl.when(frag == 2)(functools.partial(add_gradient, right_t, c_s, out, total))
     pl.when(frag != 2)(functools.partial(add_gradient, right_t, n_s, out, total))
@@ -287,15 +288,14 @@
     return pl.pallas_call(
         functools.partial(step_kernel, count),
         out_shape=jax.ShapeDtypeStruct((cols, d), kind),
-        in_specs=[SMEM] + [ANY] * count + [VMEM] * 2,
+        in_specs=[SMEM] + [VMEM] * (count + 2),
         out_specs=VMEM,
         scratch_shapes=[
-            pltpu.VMEM((rows, d), jnp.bfloat16),
-            pltpu.VMEM((rows, d), jnp.bfloat16),
+            pltpu.VMEM((rows if count > 1 else 16, d), jnp.bfloat16),
+            pltpu.VMEM((rows if count > 1 else 16, d), jnp.bfloat16),
             pltpu.VMEM((rows, cols), jnp.float32),
             pltpu.VMEM((rows, cols), jnp.float32),
             pltpu.VMEM((rows, cols), jnp.bfloat16),
-            pltpu.SemaphoreType.DMA((2 * count,)),
         ],
         input_output_aliases={count + 2: 0} if kind == jnp.float32 else {},
         compiler_params=pltpu.CompilerParams(vmem_limit_bytes=12 * MIB),
@@ -407,7 +407,7 @@
     global_new = global_frag - outer_lr * (delta + nesterov_mu * momentum_new)
     mixed = mix_alpha * w_rows(0, d).astype(jnp.float32) + (1.0 - mix_alpha) * global_new
 
-    held, totals = gradients(frag, after(far, mixed), w_both, [*first, z_near], rights)
+    held, totals = gradients(frag, far, w_both, [*first, z_near], [rights[0], after(rights[1], mixed)])
     cost = pl.CostEstimate(flops=8 * z_cross.size * cols, bytes_accessed=3 * totals[0].size * 4, transcendentals=0)
     sib_total = add_blocks(frag, [z_cross], held[0], totals[0], cost=cost)
     grad_sib = add_blocks(frag, [z_far], held[0], sib_total, jnp.bfloat16)

time: 110 us -> 110 us (level)
  Pallas kernels: 31.3 us -> 36.2 us
  waiting for transfers between devices: 33.5 us -> 30.2 us
  starting transfers between devices: 27 us -> 25.8 us
    pallas_call x2, Pallas kernels: 12 us -> 15.3 us  [forward(): pl.pallas_call(functools.partial(forward_kernel, count), out_shape=jax.Sh...]
    ppermute x1, waiting for transfers between devices: 1.62 us -> 0.01 us  [per_device(): other = lax.ppermute(part, 'replica', OTHER_H)]
    ppermute x1, waiting for transfers between devices: 2.46 us -> 1.12 us  [per_device(): z_cross = other_z(cross)]
  transfers between devices with their start and end apart: 15 -> 15, of which waited for: 8 -> 6; matrix products, arithmetic and copies ran while one was open for 14% -> 14% of each run, Pallas kernels for 25% -> 29%
where the time goes in v6:
time: 110 us
  Pallas kernels  36.2 us (33%)
  waiting for transfers between devices  30.2 us (27%)
  starting transfers between devices  25.8 us (23%)
  other arithmetic  13.7 us (12%)
  local copies, waits for them, and re-layouts  2.13 us (2%)
  between operations  1.78 us (2%)
    pallas_call x2, Pallas kernels, forward(): pl.pallas_call(functools.partial(forward_kernel, count), out_shape=jax.Sh...  15.3 us
    ppermute x1, waiting for transfers between devices, per_device(): lax.ppermute(after(w_rows((1 - h) * half, half), own), everyone, HALF_PAIR)  10.2 us
    pallas_call x1, Pallas kernels, gradients(): pl.pallas_call(functools.partial(gradient_kernel, past, tuple(spans)), ou...  8.64 us
    ppermute x1, waiting for transfers between devices, per_device(): got = lax.ppermute(sent, everyone, QUARTER_PAIR)  7.23 us
    pallas_call x3, Pallas kernels, add_blocks(): pl.pallas_call(functools.partial(step_kernel, count), out_shape=jax.Shape...  6.98 us
    ppermute x1, waiting for transfers between devices, per_device(): z_own = other_z(own)  5.73 us
    add x1, other arithmetic, per_device(): mix_alpha * w_rows(0, d).astype(jnp.float32)  5.36 us
    ppermute x1, waiting for transfers between devices, per_device(): lax.ppermute(mine, everyone, HALF_PAIR)  4.91 us
  transfers between devices with their start and end apart: 15, of which 6 were waited for; matrix products, arithmetic and copies ran while one was open for 14% of the time, Pallas kernels for 29%

profile of v6, /device:TPU:1, one launch (start us, length us, event | category | flops | bytes accessed | tf_op | source)
XLA Modules:
  0.0 109.8 jit_solution(12821500781188761183)
XLA Ops:
  0.6 1.5 %collective-permute-start.6 = (bf16[3,3072,256]{2,1,0:T(8,128)(2,1)}, bf16[3,3072,256]{2,1,0:T(8,128)(2,1)}, u32[]{:S(2)}, u32[]{:S(2)}) collective-permute-start(bf16[3,3072,256]{2,1,0:T(8,128)(2,1)} %bitcast.19), channel_id=1, source_target_pairs={{0,1},{1,0},{2,3},{3,2},{4,5},{5,4},{6,7},{7,6},{8,9},{9,8},{10,11... | collective-permute-start | bytes 14155784 | tf_op jit(solution)/shard_map/ppermute | solution.py:347
  2.1 2.6 %norm.1.refs_0_ = bf16[2,128,3072]{2,1,0:T(8,128)(2,1)} custom-call(bf16[128,3072]{1,0:T(8,128)(2,1)} %bitcast.28, bf16[128,3072]{1,0:T(8,128)(2,1)} %bitcast.29, bf16[3072]{0:T(1024)(128)(2,1)} %g_ref.1), custom_call_target="tpu_custom_call" | custom-call | flops 1 | bytes 1 | tf_op jit(solution)/shard_map/norm/pallas_call | solution.py:76
  4.7 1.8 %collective-permute-start.1 = (bf16[2,128,3072]{2,1,0:T(8,128)(2,1)}, bf16[2,128,3072]{2,1,0:T(8,128)(2,1)S(1)}, u32[]{:S(2)}, u32[]{:S(2)}) collective-permute-start(bf16[2,128,3072]{2,1,0:T(8,128)(2,1)} %norm.1.refs_0_), channel_id=1, source_target_pairs={{0,8},{1,9},{2,10},{3,11},{4,12},{5,13},{6,14},{7,15},{8,0},{9,1},... | collective-permute-start | bytes 4718600 | tf_op jit(solution)/shard_map/ppermute | solution.py:377
  6.5 2.7 %collective-permute-start.2 = (bf16[2,128,3072]{2,1,0:T(8,128)(2,1)}, bf16[2,128,3072]{2,1,0:T(8,128)(2,1)S(1)}, u32[]{:S(2)}, u32[]{:S(2)}) collective-permute-start(bf16[2,128,3072]{2,1,0:T(8,128)(2,1)} %norm.1.refs_0_), channel_id=1, source_target_pairs={{0,2},{1,7},{2,4},{3,1},{4,6},{5,3},{6,0},{7,5},{8,10},{9,15},{10,... | collective-permute-start | bytes 4718600 | tf_op jit(solution)/shard_map/ppermute | solution.py:376
  9.9 2.1 %dynamic-slice_bitcast_fusion = bf16[1536,256]{1,0:T(8,128)(2,1)} fusion(bf16[1,3,3072,256]{3,2,1,0:T(8,128)(2,1)} %param.13, s32[]{:T(128)S(6)} %select_n.71, s32[]{:T(128)S(6)} %select_n.72), kind=kLoop, calls=%fused_computation.18 | loop fusion | bytes 1572872 | tf_op jit(solution)/shard_map/squeeze | solution.py:365
  12.0 2.5 %collective-permute-start.3 = (bf16[1536,256]{1,0:T(8,128)(2,1)}, bf16[1536,256]{1,0:T(8,128)(2,1)}, u32[]{:S(2)}, u32[]{:S(2)}) collective-permute-start(bf16[1536,256]{1,0:T(8,128)(2,1)} %dynamic-slice_bitcast_fusion), channel_id=1, source_target_pairs={{0,16},{1,49},{2,18},{3,51},{4,20},{5,53},{6,22},{7,55},{8,24},{9,... | collective-permute-start | bytes 2359304 | tf_op jit(solution)/shard_map/ppermute | solution.py:379
  14.5 0.0 collective-permute-start
  14.5 10.2 %collective-permute-done.3 = bf16[1536,256]{1,0:T(8,128)(2,1)} collective-permute-done((bf16[1536,256]{1,0:T(8,128)(2,1)}, bf16[1536,256]{1,0:T(8,128)(2,1)}, u32[]{:S(2)}, u32[]{:S(2)}) %collective-permute-start.3) | collective-permute-done | bytes 786464 | tf_op jit(solution)/shard_map/ppermute | solution.py:379
  24.7 2.3 %fusion.3 = f16[768,256]{1,0:T(8,128)(2,1)} fusion(f32[3072,256]{1,0:T(8,128)} %param.16, s32[]{:T(128)S(6)} %select_n.74, bf16[1536,256]{1,0:T(8,128)(2,1)} %collective-permute-done.3, s32[]{:T(128)S(6)} %select_n.75, bf16[1,3,3072,256]{3,2,1,0:T(8,128)(2,1)} %param.13, s32[]{:T(128)S(6)} %select_n.71), kind=kLoop, calls=%fused_computation.11 | loop fusion | flops 1376256 | bytes 1966092 | tf_op jit(solution)/shard_map/convert_element_type | solution.py:374
  27.0 0.0 collective-permute-start.4
  27.0 7.2 %collective-permute-done.4 = f16[768,256]{1,0:T(8,128)(2,1)S(1)} collective-permute-done((f16[768,256]{1,0:T(8,128)(2,1)}, f16[768,256]{1,0:T(8,128)(2,1)S(1)}, u32[]{:S(2)}, u32[]{:S(2)}) %collective-permute-start.4) | collective-permute-done | bytes 393248 | tf_op jit(solution)/shard_map/ppermute | solution.py:388
  34.2 1.6 %fusion.7 = f16[768,256]{1,0:T(8,128)(2,1)S(1)} fusion(f16[768,256]{1,0:T(8,128)(2,1)S(1)} %collective-permute-done.4, f32[3072,256]{1,0:T(8,128)} %param.16, s32[]{:T(128)S(6)} %select_n.69, bf16[1536,256]{1,0:T(8,128)(2,1)} %collective-permute-done.3, s32[]{:T(128)S(6)} %select_n.73, bf16[1,3,3072,256]{3,2,1,0:T(8,128)(2,1)} %param.13, s32[]{:T(128)S(6)} %select_n.71), kind=kLoop, calls=%fused_computation.16 | loop fusion | flops 1966080 | bytes 2359308 | tf_op jit(solution)/shard_map/convert_element_type | solution.py:374
  35.8 5.7 %collective-permute-done.1.refs_3_ = bf16[2,128,3072]{2,1,0:T(8,128)(2,1)S(1)} collective-permute-done((bf16[2,128,3072]{2,1,0:T(8,128)(2,1)}, bf16[2,128,3072]{2,1,0:T(8,128)(2,1)S(1)}, u32[]{:S(2)}, u32[]{:S(2)}) %collective-permute-start.1) | collective-permute-done | bytes 1572896 | tf_op jit(solution)/shard_map/ppermute | solution.py:377
  41.6 0.0 collective-permute-done.2.refs_1_
  41.6 2.7 %collective-permute-start.11 = (bf16[2,128,3072]{2,1,0:T(8,128)(2,1)S(1)}, bf16[2,128,3072]{2,1,0:T(8,128)(2,1)}, u32[]{:S(2)}, u32[]{:S(2)}) collective-permute-start(bf16[2,128,3072]{2,1,0:T(8,128)(2,1)S(1)} %collective-permute-done.1.refs_3_), channel_id=1, source_target_pairs={{0,2},{1,7},{2,4},{3,1},{4,6},{5,3},{6,0},{7,5},{8,10},{9,15},{10,... | collective-permute-start | bytes 4718600 | tf_op jit(solution)/shard_map/ppermute | solution.py:392
  44.3 3.3 %collective-permute-start.5 = (f16[768,256]{1,0:T(8,128)(2,1)S(1)}, f16[768,256]{1,0:T(8,128)(2,1)}, u32[]{:S(2)}, u32[]{:S(2)}) collective-permute-start(f16[768,256]{1,0:T(8,128)(2,1)S(1)} %fusion.7), channel_id=1, source_target_pairs={{0,64},{16,80},{32,96},{48,112},{64,0},{80,16},{96,32},{112,48},{1... | collective-permute-start | bytes 1179656 | tf_op jit(solution)/shard_map/ppermute | solution.py:391
  47.6 0.0 collective-permute-done.refs_2_
  47.6 0.0 collective-permute-done.6.refs_4_.refs_1_.refs_7_
  47.6 9.7 %forward.2.refs_5_ = bf16[512,512]{1,0:T(8,128)(2,1)} custom-call(s32[1]{0:T(128)} %bitcast.6.frag_ref, bf16[2,128,3072]{2,1,0:T(8,128)(2,1)} %norm.1.refs_0_, bf16[2,128,3072]{2,1,0:T(8,128)(2,1)} %copy-done.3, bf16[2,128,3072]{2,1,0:T(8,128)(2,1)} %collective-permute-done.refs_2_, bf16[2,128,3072]{2,1,0:T(8,128)(2,1)} %copy-done.1, ...), custom_call_target="tpu_custom_call" | custom-call | flops 1 | bytes 1 | tf_op jit(solution)/shard_map/forward/pallas_call | solution.py:181
  57.4 0.0 collective-permute-done.5
  57.4 1.1 %add_convert_fusion = f16[768,256]{1,0:T(8,128)(2,1)S(1)} fusion(f16[768,256]{1,0:T(8,128)(2,1)} %collective-permute-done.5, f16[768,256]{1,0:T(8,128)(2,1)S(1)} %fusion.7), kind=kLoop, calls=%fused_computation.17 | loop fusion | flops 786432 | bytes 1179648 | tf_op jit(solution)/shard_map/convert_element_type | solution.py:397
  58.5 1.3 %collective-permute-start.7 = (f16[768,256]{1,0:T(8,128)(2,1)S(1)}, f16[768,256]{1,0:T(8,128)(2,1)}, u32[]{:S(2)}, u32[]{:S(2)}) collective-permute-start(f16[768,256]{1,0:T(8,128)(2,1)S(1)} %add_convert_fusion), channel_id=1, source_target_pairs={{0,48},{1,17},{2,50},{3,19},{4,52},{5,21},{6,54},{7,23},{8,56},{9,... | collective-permute-start | bytes 1179656 | tf_op jit(solution)/shard_map/ppermute | solution.py:400
  59.8 1.8 %collective-permute-start.8 = (f16[768,256]{1,0:T(8,128)(2,1)S(1)}, f16[768,256]{1,0:T(8,128)(2,1)}, u32[]{:S(2)}, u32[]{:S(2)}) collective-permute-start(f16[768,256]{1,0:T(8,128)(2,1)S(1)} %add_convert_fusion), channel_id=1, source_target_pairs={{0,16},{1,49},{2,18},{3,51},{4,20},{5,53},{6,22},{7,55},{8,24},{9,... | collective-permute-start | bytes 1179656 | tf_op jit(solution)/shard_map/ppermute | solution.py:400
  61.6 0.6 collective-permute-start.9
  62.2 0.5 collective-permute-start.13
  62.7 0.0 collective-permute-done.11.refs_0_.refs_4_
  62.7 0.7 collective-permute-start.10
  63.4 5.5 %forward.3.refs_6_ = bf16[128,512]{1,0:T(8,128)(2,1)} custom-call(s32[1]{0:T(128)} %bitcast.6.frag_ref, bf16[2,128,3072]{2,1,0:T(8,128)(2,1)} %collective-permute-done.11.refs_0_.refs_4_, bf16[3,3072,256]{2,1,0:T(8,128)(2,1)} %collective-permute-done.6.refs_4_.refs_1_.refs_7_, bf16[3,3072,256]{2,1,0:T(8,128)(2,1)} %bitcast.21), custom_call_target="tpu_custom_call" | custom-call | flops 1 | bytes 1 | tf_op jit(solution)/shard_map/forward/pallas_call | solution.py:181
  69.0 0.0 copy-start.9
  69.0 0.0 collective-permute-done.7
  69.0 3.3 %collective-permute-start.12 = (bf16[2,128,3072]{2,1,0:T(8,128)(2,1)}, bf16[2,128,3072]{2,1,0:T(8,128)(2,1)S(1)}, u32[]{:S(2)}, u32[]{:S(2)}) collective-permute-start(bf16[2,128,3072]{2,1,0:T(8,128)(2,1)} %collective-permute-done.11.refs_0_.refs_4_), channel_id=1, source_target_pairs={{0,2},{1,7},{2,4},{3,1},{4,6},{5,3},{6,0},{7,5},{8,10},{9,15},{10,... | collective-permute-start | bytes 4718600 | tf_op jit(solution)/shard_map/ppermute | solution.py:403
  72.3 1.5 %maximum_select_fusion.1 = f16[1536,256]{1,0:T(8,128)(2,1)S(1)} fusion(f16[768,256]{1,0:T(8,128)(2,1)} %collective-permute-done.7, f16[768,256]{1,0:T(8,128)(2,1)S(1)} %add_convert_fusion, pred[]{:T(512)S(6)} %eq.14), kind=kLoop, calls=%fused_computation.6 | loop fusion | flops 1179648 | bytes 1572865 | tf_op jit(solution)/shard_map/jit(_where)/select_n | solution.py:371
  73.8 4.9 %collective-permute-done.8 = f16[768,256]{1,0:T(8,128)(2,1)} collective-permute-done((f16[768,256]{1,0:T(8,128)(2,1)S(1)}, f16[768,256]{1,0:T(8,128)(2,1)}, u32[]{:S(2)}, u32[]{:S(2)}) %collective-permute-start.8) | collective-permute-done | bytes 393248 | tf_op jit(solution)/shard_map/ppermute | solution.py:400
  78.7 1.0 collective-permute-done.9
  79.7 1.8 %maximum_select_fusion.2 = f16[1536,256]{1,0:T(8,128)(2,1)S(1)} fusion(f16[768,256]{1,0:T(8,128)(2,1)} %collective-permute-done.9, f16[768,256]{1,0:T(8,128)(2,1)} %collective-permute-done.8, pred[]{:T(512)S(6)} %eq.14), kind=kLoop, calls=%fused_computation.7 | loop fusion | flops 1179648 | bytes 1572865 | tf_op jit(solution)/shard_map/jit(_where)/select_n | solution.py:371
  81.6 0.0 slice-start.1
  81.6 0.0 copy-start
  81.6 5.4 %fusion = (f32[3072,256]{1,0:T(8,128)S(1)}, f32[3072,256]{1,0:T(8,128)}, f32[3072,256]{1,0:T(8,128)}) fusion(bf16[1,3,3072,256]{3,2,1,0:T(8,128)(2,1)} %param.13, s32[]{:T(128)S(6)} %select_n.71, f32[3072,256]{1,0:T(8,128)S(1)} %copy-done.9, f16[1536,256]{1,0:T(8,128)(2,1)S(1)} %maximum_select_fusion.1, f16[1536,256]{1,0:T(8,128)(2,1)S(1)} %maximum_select_fusion.2, ...), kind=kLoop, calls=%fused_computation.1 | loop fusion | flops 11010048 | bytes 18874372 | tf_op jit(solution)/shard_map/add | solution.py:408
  87.0 0.0 collective-permute-done.13.block
  87.1 8.6 %gradients.1 = (bf16[3,3072,256]{2,1,0:T(8,128)(2,1)S(1)}, bf16[3,3072,256]{2,1,0:T(8,128)(2,1)S(1)}, f32[256,3072]{1,0:T(8,128)S(1)}, f32[256,3072]{1,0:T(8,128)S(1)}) custom-call(s32[1]{0:T(128)} %bitcast.6.frag_ref, bf16[2,128,3072]{2,1,0:T(8,128)(2,1)} %collective-permute-done.13.block, bf16[2,128,3072]{2,1,0:T(8,128)(2,1)S(1)} %copy-done, ...), custom_call_target="tpu_custom_call" | custom-call | flops 1 | bytes 1 | tf_op jit(solution)/shard_map/gradients/pallas_call | solution.py:247
  95.7 1.1 %collective-permute-done.10.refs_0_ = bf16[2,128,3072]{2,1,0:T(8,128)(2,1)S(1)} collective-permute-done((bf16[2,128,3072]{2,1,0:T(8,128)(2,1)}, bf16[2,128,3072]{2,1,0:T(8,128)(2,1)S(1)}, u32[]{:S(2)}, u32[]{:S(2)}) %collective-permute-start.10) | collective-permute-done | bytes 1572896 | tf_op jit(solution)/shard_map/ppermute | solution.py:399
  96.8 2.1 %blocks.4.refs_2_ = f32[256,3072]{1,0:T(8,128)S(1)} custom-call(s32[1]{0:T(128)} %bitcast.6.frag_ref, bf16[2,128,3072]{2,1,0:T(8,128)(2,1)S(1)} %collective-permute-done.10.refs_0_, bf16[3,3072,256]{2,1,0:T(8,128)(2,1)S(1)} %get-tuple-element.27.refs_1_, f32[256,3072]{1,0:T(8,128)S(1)} %get-tuple-element.28.refs_2_), custom_call_target="tpu_custom_call", output_to_operand_aliasing={{}: (3, {})} | custom-call | flops 1610612736 | bytes 9437184 | tf_op jit(solution)/shard_map/blocks/pallas_call | solution.py:288
  98.9 0.0 collective-permute-done.12.refs_1_.refs_0_
  99.0 1.8 %blocks.5 = bf16[256,3072]{1,0:T(8,128)(2,1)S(1)} custom-call(s32[1]{0:T(128)} %bitcast.6.frag_ref, bf16[2,128,3072]{2,1,0:T(8,128)(2,1)S(1)} %collective-permute-done.12.refs_1_.refs_0_, bf16[3,3072,256]{2,1,0:T(8,128)(2,1)S(1)} %get-tuple-element.27.refs_1_, f32[256,3072]{1,0:T(8,128)S(1)} %blocks.4.refs_2_), custom_call_target="tpu_custom_call" | custom-call | flops 1 | bytes 1 | tf_op jit(solution)/shard_map/blocks/pallas_call | solution.py:288
  100.8 3.0 %collective-permute-start.14 = (bf16[256,3072]{1,0:T(8,128)(2,1)S(1)}, bf16[256,3072]{1,0:T(8,128)(2,1)S(1)}, u32[]{:S(2)}, u32[]{:S(2)}) collective-permute-start(bf16[256,3072]{1,0:T(8,128)(2,1)S(1)} %blocks.5), channel_id=1, source_target_pairs={{0,1},{1,0},{2,3},{3,2},{4,5},{5,4},{6,7},{7,6},{8,9},{9,8},{10,11... | collective-permute-start | bytes 4718600 | tf_op jit(solution)/shard_map/ppermute | solution.py:414
  103.8 3.0 %blocks.3.own_ref = f32[256,3072]{1,0:T(8,128)S(1)} custom-call(s32[1]{0:T(128)} %bitcast.6.frag_ref, bf16[2,128,3072]{2,1,0:T(8,128)(2,1)S(1)} %collective-permute-done.10.refs_0_, bf16[2,128,3072]{2,1,0:T(8,128)(2,1)S(1)} %collective-permute-done.12.refs_1_.refs_0_, ...), custom_call_target="tpu_custom_call", output_to_operand_aliasing={{}: (4, {})} | custom-call | flops 1 | bytes 1 | tf_op jit(solution)/shard_map/blocks/pallas_call | solution.py:288
  106.8 0.0 collective-permute-done.14.other_ref
  106.9 2.8 %adam.1 = bf16[3072,256]{1,0:T(8,128)(2,1)} custom-call(f32[256,3072]{1,0:T(8,128)S(1)} %blocks.3.own_ref, bf16[256,3072]{1,0:T(8,128)(2,1)S(1)} %collective-permute-done.14.other_ref, f32[3072,256]{1,0:T(8,128)S(1)} %bitcast.25, f32[3072,256]{1,0:T(8,128)S(1)} %bitcast.26, f32[3072,256]{1,0:T(8,128)S(1)} %get-tuple-element.29.mixed_ref), custom_call_target="tpu_custom_call" | custom-call | flops 1 | bytes 1 | tf_op jit(solution)/shard_map/adam/pallas_call | solution.py:327
  (22 shorter events, 0.0 us)
Async XLA Ops:
  0.6 47.0 %collective-permute-start.6 = (bf16[3,3072,256]{2,1,0:T(8,128)(2,1)}, bf16[3,3072,256]{2,1,0:T(8,128)(2,1)}, u32[]{:S(2)}, u32[]{:S(2)}) collective-permute-start(bf16[3,3072,256]{2,1,0:T(8,128)(2,1)} %bitcast.19), channel_id=1, source_target_pairs={{0,1},{1,0},{2,3},{3,2},{4,5},{5,4},{6,7},{7,6},{8,9},{9,8},{10,11... | collective-permute-start | bytes 14155784 | tf_op jit(solution)/shard_map/ppermute | solution.py:347
  4.7 36.9 %collective-permute-start.1 = (bf16[2,128,3072]{2,1,0:T(8,128)(2,1)}, bf16[2,128,3072]{2,1,0:T(8,128)(2,1)S(1)}, u32[]{:S(2)}, u32[]{:S(2)}) collective-permute-start(bf16[2,128,3072]{2,1,0:T(8,128)(2,1)} %norm.1.refs_0_), channel_id=1, source_target_pairs={{0,8},{1,9},{2,10},{3,11},{4,12},{5,13},{6,14},{7,15},{8,0},{9,1},... | collective-permute-start | bytes 4718600 | tf_op jit(solution)/shard_map/ppermute | solution.py:377
  6.5 35.1 %collective-permute-start.2 = (bf16[2,128,3072]{2,1,0:T(8,128)(2,1)}, bf16[2,128,3072]{2,1,0:T(8,128)(2,1)S(1)}, u32[]{:S(2)}, u32[]{:S(2)}) collective-permute-start(bf16[2,128,3072]{2,1,0:T(8,128)(2,1)} %norm.1.refs_0_), channel_id=1, source_target_pairs={{0,2},{1,7},{2,4},{3,1},{4,6},{5,3},{6,0},{7,5},{8,10},{9,15},{10,... | collective-permute-start | bytes 4718600 | tf_op jit(solution)/shard_map/ppermute | solution.py:376
  12.0 12.7 %collective-permute-start.3 = (bf16[1536,256]{1,0:T(8,128)(2,1)}, bf16[1536,256]{1,0:T(8,128)(2,1)}, u32[]{:S(2)}, u32[]{:S(2)}) collective-permute-start(bf16[1536,256]{1,0:T(8,128)(2,1)} %dynamic-slice_bitcast_fusion), channel_id=1, source_target_pairs={{0,16},{1,49},{2,18},{3,51},{4,20},{5,53},{6,22},{7,55},{8,24},{9,... | collective-permute-start | bytes 2359304 | tf_op jit(solution)/shard_map/ppermute | solution.py:379
  14.5 33.1 %collective-permute-start = (bf16[2,128,3072]{2,1,0:T(8,128)(2,1)}, bf16[2,128,3072]{2,1,0:T(8,128)(2,1)}, u32[]{:S(2)}, u32[]{:S(2)}) collective-permute-start(bf16[2,128,3072]{2,1,0:T(8,128)(2,1)} %norm.1.refs_0_), channel_id=1, source_target_pairs={{0,7},{1,2},{2,1},{3,4},{4,3},{5,6},{6,5},{7,0},{8,15},{9,10},{10,... | collective-permute-start | bytes 4718600 | tf_op jit(solution)/shard_map/ppermute | solution.py:378
  27.0 7.2 %collective-permute-start.4 = (f16[768,256]{1,0:T(8,128)(2,1)}, f16[768,256]{1,0:T(8,128)(2,1)S(1)}, u32[]{:S(2)}, u32[]{:S(2)}) collective-permute-start(f16[768,256]{1,0:T(8,128)(2,1)} %fusion.3), channel_id=1, source_target_pairs={{0,48},{1,17},{2,50},{3,19},{4,52},{5,21},{6,54},{7,23},{8,56},{9,... | collective-permute-start | bytes 1179656 | tf_op jit(solution)/shard_map/ppermute | solution.py:388
  41.6 6.0 %copy-start.1 = (bf16[2,128,3072]{2,1,0:T(8,128)(2,1)}, bf16[2,128,3072]{2,1,0:T(8,128)(2,1)S(1)}, u32[]{:S(2)}) copy-start(bf16[2,128,3072]{2,1,0:T(8,128)(2,1)S(1)} %collective-permute-done.1.refs_3_) | copy-start | bytes 4718596
  41.6 6.0 %copy-start.3 = (bf16[2,128,3072]{2,1,0:T(8,128)(2,1)}, bf16[2,128,3072]{2,1,0:T(8,128)(2,1)S(1)}, u32[]{:S(2)}) copy-start(bf16[2,128,3072]{2,1,0:T(8,128)(2,1)S(1)} %collective-permute-done.2.refs_1_) | copy-start | bytes 4718596
  41.6 21.1 %collective-permute-start.11 = (bf16[2,128,3072]{2,1,0:T(8,128)(2,1)S(1)}, bf16[2,128,3072]{2,1,0:T(8,128)(2,1)}, u32[]{:S(2)}, u32[]{:S(2)}) collective-permute-start(bf16[2,128,3072]{2,1,0:T(8,128)(2,1)S(1)} %collective-permute-done.1.refs_3_), channel_id=1, source_target_pairs={{0,2},{1,7},{2,4},{3,1},{4,6},{5,3},{6,0},{7,5},{8,10},{9,15},{10,... | collective-permute-start | bytes 4718600 | tf_op jit(solution)/shard_map/ppermute | solution.py:392
  44.3 13.1 %collective-permute-start.5 = (f16[768,256]{1,0:T(8,128)(2,1)S(1)}, f16[768,256]{1,0:T(8,128)(2,1)}, u32[]{:S(2)}, u32[]{:S(2)}) collective-permute-start(f16[768,256]{1,0:T(8,128)(2,1)S(1)} %fusion.7), channel_id=1, source_target_pairs={{0,64},{16,80},{32,96},{48,112},{64,0},{80,16},{96,32},{112,48},{1... | collective-permute-start | bytes 1179656 | tf_op jit(solution)/shard_map/ppermute | solution.py:391
  58.5 10.5 %collective-permute-start.7 = (f16[768,256]{1,0:T(8,128)(2,1)S(1)}, f16[768,256]{1,0:T(8,128)(2,1)}, u32[]{:S(2)}, u32[]{:S(2)}) collective-permute-start(f16[768,256]{1,0:T(8,128)(2,1)S(1)} %add_convert_fusion), channel_id=1, source_target_pairs={{0,48},{1,17},{2,50},{3,19},{4,52},{5,21},{6,54},{7,23},{8,56},{9,... | collective-permute-start | bytes 1179656 | tf_op jit(solution)/shard_map/ppermute | solution.py:400
  59.8 18.9 %collective-permute-start.8 = (f16[768,256]{1,0:T(8,128)(2,1)S(1)}, f16[768,256]{1,0:T(8,128)(2,1)}, u32[]{:S(2)}, u32[]{:S(2)}) collective-permute-start(f16[768,256]{1,0:T(8,128)(2,1)S(1)} %add_convert_fusion), channel_id=1, source_target_pairs={{0,16},{1,49},{2,18},{3,51},{4,20},{5,53},{6,22},{7,55},{8,24},{9,... | collective-permute-start | bytes 1179656 | tf_op jit(solution)/shard_map/ppermute | solution.py:400
  61.6 18.1 %collective-permute-start.9 = (f16[768,256]{1,0:T(8,128)(2,1)S(1)}, f16[768,256]{1,0:T(8,128)(2,1)}, u32[]{:S(2)}, u32[]{:S(2)}) collective-permute-start(f16[768,256]{1,0:T(8,128)(2,1)S(1)} %add_convert_fusion), channel_id=1, source_target_pairs={{0,32},{16,48},{32,0},{48,16},{64,96},{80,112},{96,64},{112,80},{1... | collective-permute-start | bytes 1179656 | tf_op jit(solution)/shard_map/ppermute | solution.py:401
  62.2 24.8 %collective-permute-start.13 = (bf16[2,128,3072]{2,1,0:T(8,128)(2,1)}, bf16[2,128,3072]{2,1,0:T(8,128)(2,1)}, u32[]{:S(2)}, u32[]{:S(2)}) collective-permute-start(bf16[2,128,3072]{2,1,0:T(8,128)(2,1)} %copy-done.3), channel_id=1, source_target_pairs={{0,2},{1,7},{2,4},{3,1},{4,6},{5,3},{6,0},{7,5},{8,10},{9,15},{10,... | collective-permute-start | bytes 4718600 | tf_op jit(solution)/shard_map/ppermute | solution.py:393
  62.7 34.1 %collective-permute-start.10 = (bf16[2,128,3072]{2,1,0:T(8,128)(2,1)}, bf16[2,128,3072]{2,1,0:T(8,128)(2,1)S(1)}, u32[]{:S(2)}, u32[]{:S(2)}) collective-permute-start(bf16[2,128,3072]{2,1,0:T(8,128)(2,1)} %collective-permute-done.refs_2_), channel_id=1, source_target_pairs={{0,8},{1,9},{2,10},{3,11},{4,12},{5,13},{6,14},{7,15},{8,0},{9,1},... | collective-permute-start | bytes 4718600 | tf_op jit(solution)/shard_map/ppermute | solution.py:399
  69.0 12.6 %copy-start.9 = (f32[3072,256]{1,0:T(8,128)S(1)}, f32[3072,256]{1,0:T(8,128)}, u32[]{:S(2)}) copy-start(f32[3072,256]{1,0:T(8,128)} %param.16) | copy-start | bytes 9437188
  69.0 30.0 %collective-permute-start.12 = (bf16[2,128,3072]{2,1,0:T(8,128)(2,1)}, bf16[2,128,3072]{2,1,0:T(8,128)(2,1)S(1)}, u32[]{:S(2)}, u32[]{:S(2)}) collective-permute-start(bf16[2,128,3072]{2,1,0:T(8,128)(2,1)} %collective-permute-done.11.refs_0_.refs_4_), channel_id=1, source_target_pairs={{0,2},{1,7},{2,4},{3,1},{4,6},{5,3},{6,0},{7,5},{8,10},{9,15},{10,... | collective-permute-start | bytes 4718600 | tf_op jit(solution)/shard_map/ppermute | solution.py:403
  79.7 7.3 %slice-start = ((s8[4718592]{0:T(1024)(128)(4,1)}), s8[4194304]{0:T(1024)(128)(4,1)S(1)}, s32[]{:S(2)}) async-start(s8[4718592]{0:T(1024)(128)(4,1)} %bitcast.22), calls=%async_computation | async-start | bytes 8388608
  81.6 5.4 %slice-start.1 = ((s8[4718592]{0:T(1024)(128)(4,1)}), s8[524288]{0:T(1024)(128)(4,1)S(1)}, s32[]{:S(2)}) async-start(s8[4718592]{0:T(1024)(128)(4,1)} %bitcast.22), calls=%async_computation.1 | async-start | bytes 1048576
  81.6 5.4 %copy-start = (bf16[2,128,3072]{2,1,0:T(8,128)(2,1)S(1)}, bf16[2,128,3072]{2,1,0:T(8,128)(2,1)}, u32[]{:S(2)}) copy-start(bf16[2,128,3072]{2,1,0:T(8,128)(2,1)} %norm.1.refs_0_) | copy-start | bytes 4718596
  81.6 5.4 %copy-start.2 = (bf16[2,128,3072]{2,1,0:T(8,128)(2,1)S(1)}, bf16[2,128,3072]{2,1,0:T(8,128)(2,1)}, u32[]{:S(2)}) copy-start(bf16[2,128,3072]{2,1,0:T(8,128)(2,1)} %copy-done.1) | copy-start | bytes 4718596
  81.6 5.4 %copy-start.4 = (bf16[2,128,3072]{2,1,0:T(8,128)(2,1)S(1)}, bf16[2,128,3072]{2,1,0:T(8,128)(2,1)}, u32[]{:S(2)}) copy-start(bf16[2,128,3072]{2,1,0:T(8,128)(2,1)} %copy-done.3) | copy-start | bytes 4718596
  81.6 5.4 %copy-start.7 = (bf16[512,512]{1,0:T(8,128)(2,1)S(1)}, bf16[512,512]{1,0:T(8,128)(2,1)}, u32[]{:S(2)}) copy-start(bf16[512,512]{1,0:T(8,128)(2,1)} %forward.2.refs_5_) | copy-start | bytes 1572868
  81.6 5.4 %copy-start.8 = (bf16[128,512]{1,0:T(8,128)(2,1)S(1)}, bf16[128,512]{1,0:T(8,128)(2,1)}, u32[]{:S(2)}) copy-start(bf16[128,512]{1,0:T(8,128)(2,1)} %forward.3.refs_6_) | copy-start | bytes 393220
  100.8 6.0 %collective-permute-start.14 = (bf16[256,3072]{1,0:T(8,128)(2,1)S(1)}, bf16[256,3072]{1,0:T(8,128)(2,1)S(1)}, u32[]{:S(2)}, u32[]{:S(2)}) collective-permute-start(bf16[256,3072]{1,0:T(8,128)(2,1)S(1)} %blocks.5), channel_id=1, source_target_pairs={{0,1},{1,0},{2,3},{3,2},{4,5},{5,4},{6,7},{7,6},{8,9},{9,8},{10,11... | collective-permute-start | bytes 4718600 | tf_op jit(solution)/shard_map/ppermute | solution.py:414
  103.8 3.1 %copy-start.5 = (f32[1,3072,256]{2,1,0:T(8,128)S(1)}, f32[1,3072,256]{2,1,0:T(8,128)}, u32[]{:S(2)}) copy-start(f32[1,3072,256]{2,1,0:T(8,128)} %param.14) | copy-start | bytes 9437188
  103.8 3.1 %copy-start.6 = (f32[1,3072,256]{2,1,0:T(8,128)S(1)}, f32[1,3072,256]{2,1,0:T(8,128)}, u32[]{:S(2)}) copy-start(f32[1,3072,256]{2,1,0:T(8,128)} %param.15) | copy-start | bytes 9437188

commit v7 on v6

--- a/solution.py
+++ b/solution.py
@@ -304,6 +304,59 @@
     )(frag, *blocks, weight, total)
 
 
+def right_kernel(frag_ref, block, weight, out_ref, up_s, dh_s):
+    frag = frag_ref[0]
+    right_side(frag, Loads(frag, None, 0), 0, block.at[0], block.at[1], weight, up_s, dh_s, out_ref)
+
+
+def right_of(frag, block, weight, cost):
+    rows, cols = block.shape[1], weight.shape[2]
+    return pl.pallas_call(
+        right_kernel,
+        out_shape=jax.ShapeDtypeStruct((rows, cols), jnp.bfloat16),
+        in_specs=[SMEM, VMEM, VMEM],
+        out_specs=VMEM,
+        scratch_shapes=[pltpu.VMEM((rows, cols), jnp.float32)] * 2,
+        compiler_params=pltpu.CompilerParams(vmem_limit_bytes=12 * MIB),
+        cost_estimate=cost,
+        name="right",
+    )(frag, block, weight)
+
+
+def last_kernel(frag_ref, block, past, past_right, weight, total, out, up_s, dh_s, right_s):
+    rows = block.shape[1]
+    frag = frag_ref[0]
+    right_s[:rows, :] = past_right[...]
+    right_side(frag, Loads(frag, None, 0), 0, block.at[0], block.at[1], weight, up_s, dh_s, right_s.at[rows:, :])
+    right_t = right_s[...].T
+
+    def add(side):
+        step = 768
+        for at in range(0, out.shape[1], step):
+            span = slice(at, at + step)
+            left = jnp.concatenate([past[side, :, span], block[side, :, span]], axis=0)
+            term = total[:, span] + jnp.dot(right_t, left, preferred_element_type=jnp.float32)
+            out[:, span] = term.astype(out.dtype)
+
+    pl.when(frag == 2)(lambda: add(1))
+    pl.when(frag != 2)(lambda: add(0))
+
+
+def last_gradient(frag, block, past, past_right, weight, total):
+    rows = block.shape[1]
+    _, d, cols = weight.shape
+    return pl.pallas_call(
+        last_kernel,
+        out_shape=jax.ShapeDtypeStruct((cols, d), jnp.bfloat16),
+        in_specs=[SMEM] + [VMEM] * 5,
+        out_specs=VMEM,
+        scratch_shapes=[pltpu.VMEM((rows, cols), jnp.float32)] * 2 + [pltpu.VMEM((2 * rows, cols), jnp.bfloat16)],
+        compiler_params=pltpu.CompilerParams(vmem_limit_bytes=12 * MIB),
+        cost_estimate=CHEAP,
+        name="last",
+    )(frag, block, past, past_right, weight, total)
+
+
 def adam_kernel(tokens, tile, own_ref, other_ref, m_ref, v_ref, mixed_ref, out_ref, out_s, sems):
     copies = []
     for i in range(m_ref.shape[0] // tile):
@@ -409,8 +462,8 @@
 
     held, totals = gradients(frag, far, w_both, [*first, z_near], [rights[0], after(rights[1], mixed)])
     cost = pl.CostEstimate(flops=8 * z_cross.size * cols, bytes_accessed=3 * totals[0].size * 4, transcendentals=0)
-    sib_total = add_blocks(frag, [z_cross], held[0], totals[0], cost=cost)
-    grad_sib = add_blocks(frag, [z_far], held[0], sib_total, jnp.bfloat16)
+    right_cross = right_of(frag, z_cross, held[0], cost)
+    grad_sib = last_gradient(frag, z_far, z_cross, right_cross, held[0], totals[0])
     grad_sib = lax.ppermute(grad_sib, "fsdp", SIBLING)
     grad_own = add_blocks(frag, [z_cross, z_far], held[1], totals[1])
     tokens_total = hidden_in.shape[1] * lax.axis_size("fsdp")

time: 110 us -> 110 us (level)
  Pallas kernels: 36.2 us -> 34.7 us
  waiting for transfers between devices: 30.2 us -> 31.6 us
    pallas_call x3 -> x1, Pallas kernels: 6.98 us -> 2.92 us  [add_blocks(): pl.pallas_call(functools.partial(step_kernel, count), out_shape=jax.Shape...]
    pallas_call x0 -> x2, Pallas kernels: none -> 3.09 us  [the longest x1 1.91 us: last_gradient(): pl.pallas_call(last_kernel, out_shape=jax.ShapeDtypeStruct((cols, d), jnp...]
  transfers between devices with their start and end apart: 15 -> 15, of which waited for: 6 -> 8; matrix products, arithmetic and copies ran while one was open for 14% -> 14% of each run, Pallas kernels for 29% -> 27%
where the time goes in v7:
time: 110 us
  Pallas kernels  34.7 us (32%)
  waiting for transfers between devices  31.6 us (29%)
  starting transfers between devices  25.9 us (24%)
  other arithmetic  13.7 us (12%)
  local copies, waits for them, and re-layouts  2.13 us (2%)
  between operations  1.73 us (2%)
    pallas_call x2, Pallas kernels, forward(): pl.pallas_call(functools.partial(forward_kernel, count), out_shape=jax.Sh...  15.2 us
    ppermute x1, waiting for transfers between devices, per_device(): lax.ppermute(after(w_rows((1 - h) * half, half), own), everyone, HALF_PAIR)  10.2 us
    pallas_call x1, Pallas kernels, gradients(): pl.pallas_call(functools.partial(gradient_kernel, past, tuple(spans)), ou...  8.17 us
    ppermute x1, waiting for transfers between devices, per_device(): got = lax.ppermute(sent, everyone, QUARTER_PAIR)  7.23 us
    ppermute x1, waiting for transfers between devices, per_device(): z_own = other_z(own)  5.73 us
    add x1, other arithmetic, per_device(): mix_alpha * w_rows(0, d).astype(jnp.float32)  5.36 us
    ppermute x1, waiting for transfers between devices, per_device(): lax.ppermute(mine, everyone, HALF_PAIR)  4.94 us
    convert_element_type x2, other arithmetic, wire(): return (value * (WIRE_SCALE / 8)).astype(jnp.float16)  3.91 us
  transfers between devices with their start and end apart: 15, of which 8 were waited for; matrix products, arithmetic and copies ran while one was open for 14% of the time, Pallas kernels for 27%

profile of v7, /device:TPU:1, one launch (start us, length us, event | category | flops | bytes accessed | tf_op | source)
XLA Modules:
  0.0 109.8 jit_solution(196896967657735149)
XLA Ops:
  0.6 1.5 %collective-permute-start.6 = (bf16[3,3072,256]{2,1,0:T(8,128)(2,1)}, bf16[3,3072,256]{2,1,0:T(8,128)(2,1)}, u32[]{:S(2)}, u32[]{:S(2)}) collective-permute-start(bf16[3,3072,256]{2,1,0:T(8,128)(2,1)} %bitcast.19), channel_id=1, source_target_pairs={{0,1},{1,0},{2,3},{3,2},{4,5},{5,4},{6,7},{7,6},{8,9},{9,8},{10,11... | collective-permute-start | bytes 14155784 | tf_op jit(solution)/shard_map/ppermute | solution.py:400
  2.1 2.6 %norm.1.refs_0_ = bf16[2,128,3072]{2,1,0:T(8,128)(2,1)} custom-call(bf16[128,3072]{1,0:T(8,128)(2,1)} %bitcast.28, bf16[128,3072]{1,0:T(8,128)(2,1)} %bitcast.29, bf16[3072]{0:T(1024)(128)(2,1)} %g_ref.1), custom_call_target="tpu_custom_call" | custom-call | flops 1 | bytes 1 | tf_op jit(solution)/shard_map/norm/pallas_call | solution.py:76
  4.7 1.8 %collective-permute-start.1 = (bf16[2,128,3072]{2,1,0:T(8,128)(2,1)}, bf16[2,128,3072]{2,1,0:T(8,128)(2,1)S(1)}, u32[]{:S(2)}, u32[]{:S(2)}) collective-permute-start(bf16[2,128,3072]{2,1,0:T(8,128)(2,1)} %norm.1.refs_0_), channel_id=1, source_target_pairs={{0,8},{1,9},{2,10},{3,11},{4,12},{5,13},{6,14},{7,15},{8,0},{9,1},... | collective-permute-start | bytes 4718600 | tf_op jit(solution)/shard_map/ppermute | solution.py:430
  6.5 2.7 %collective-permute-start.2 = (bf16[2,128,3072]{2,1,0:T(8,128)(2,1)}, bf16[2,128,3072]{2,1,0:T(8,128)(2,1)S(1)}, u32[]{:S(2)}, u32[]{:S(2)}) collective-permute-start(bf16[2,128,3072]{2,1,0:T(8,128)(2,1)} %norm.1.refs_0_), channel_id=1, source_target_pairs={{0,2},{1,7},{2,4},{3,1},{4,6},{5,3},{6,0},{7,5},{8,10},{9,15},{10,... | collective-permute-start | bytes 4718600 | tf_op jit(solution)/shard_map/ppermute | solution.py:429
  9.9 2.1 %dynamic-slice_bitcast_fusion = bf16[1536,256]{1,0:T(8,128)(2,1)} fusion(bf16[1,3,3072,256]{3,2,1,0:T(8,128)(2,1)} %param.13, s32[]{:T(128)S(6)} %select_n.71, s32[]{:T(128)S(6)} %select_n.72), kind=kLoop, calls=%fused_computation.18 | loop fusion | bytes 1572872 | tf_op jit(solution)/shard_map/squeeze | solution.py:418
  12.0 2.5 %collective-permute-start.3 = (bf16[1536,256]{1,0:T(8,128)(2,1)}, bf16[1536,256]{1,0:T(8,128)(2,1)}, u32[]{:S(2)}, u32[]{:S(2)}) collective-permute-start(bf16[1536,256]{1,0:T(8,128)(2,1)} %dynamic-slice_bitcast_fusion), channel_id=1, source_target_pairs={{0,16},{1,49},{2,18},{3,51},{4,20},{5,53},{6,22},{7,55},{8,24},{9,... | collective-permute-start | bytes 2359304 | tf_op jit(solution)/shard_map/ppermute | solution.py:432
  14.5 0.0 collective-permute-start
  14.5 10.2 %collective-permute-done.3 = bf16[1536,256]{1,0:T(8,128)(2,1)} collective-permute-done((bf16[1536,256]{1,0:T(8,128)(2,1)}, bf16[1536,256]{1,0:T(8,128)(2,1)}, u32[]{:S(2)}, u32[]{:S(2)}) %collective-permute-start.3) | collective-permute-done | bytes 786464 | tf_op jit(solution)/shard_map/ppermute | solution.py:432
  24.7 2.3 %fusion.3 = f16[768,256]{1,0:T(8,128)(2,1)} fusion(f32[3072,256]{1,0:T(8,128)} %param.16, s32[]{:T(128)S(6)} %select_n.74, bf16[1536,256]{1,0:T(8,128)(2,1)} %collective-permute-done.3, s32[]{:T(128)S(6)} %select_n.75, bf16[1,3,3072,256]{3,2,1,0:T(8,128)(2,1)} %param.13, s32[]{:T(128)S(6)} %select_n.71), kind=kLoop, calls=%fused_computation.11 | loop fusion | flops 1376256 | bytes 1966092 | tf_op jit(solution)/shard_map/convert_element_type | solution.py:427
  27.0 0.0 collective-permute-start.4
  27.0 7.2 %collective-permute-done.4 = f16[768,256]{1,0:T(8,128)(2,1)S(1)} collective-permute-done((f16[768,256]{1,0:T(8,128)(2,1)}, f16[768,256]{1,0:T(8,128)(2,1)S(1)}, u32[]{:S(2)}, u32[]{:S(2)}) %collective-permute-start.4) | collective-permute-done | bytes 393248 | tf_op jit(solution)/shard_map/ppermute | solution.py:441
  34.2 1.6 %fusion.7 = f16[768,256]{1,0:T(8,128)(2,1)S(1)} fusion(f16[768,256]{1,0:T(8,128)(2,1)S(1)} %collective-permute-done.4, f32[3072,256]{1,0:T(8,128)} %param.16, s32[]{:T(128)S(6)} %select_n.69, bf16[1536,256]{1,0:T(8,128)(2,1)} %collective-permute-done.3, s32[]{:T(128)S(6)} %select_n.73, bf16[1,3,3072,256]{3,2,1,0:T(8,128)(2,1)} %param.13, s32[]{:T(128)S(6)} %select_n.71), kind=kLoop, calls=%fused_computation.16 | loop fusion | flops 1966080 | bytes 2359308 | tf_op jit(solution)/shard_map/convert_element_type | solution.py:427
  35.8 5.7 %collective-permute-done.1.refs_3_ = bf16[2,128,3072]{2,1,0:T(8,128)(2,1)S(1)} collective-permute-done((bf16[2,128,3072]{2,1,0:T(8,128)(2,1)}, bf16[2,128,3072]{2,1,0:T(8,128)(2,1)S(1)}, u32[]{:S(2)}, u32[]{:S(2)}) %collective-permute-start.1) | collective-permute-done | bytes 1572896 | tf_op jit(solution)/shard_map/ppermute | solution.py:430
  41.6 0.0 collective-permute-done.2.refs_1_
  41.6 2.7 %collective-permute-start.11 = (bf16[2,128,3072]{2,1,0:T(8,128)(2,1)S(1)}, bf16[2,128,3072]{2,1,0:T(8,128)(2,1)}, u32[]{:S(2)}, u32[]{:S(2)}) collective-permute-start(bf16[2,128,3072]{2,1,0:T(8,128)(2,1)S(1)} %collective-permute-done.1.refs_3_), channel_id=1, source_target_pairs={{0,2},{1,7},{2,4},{3,1},{4,6},{5,3},{6,0},{7,5},{8,10},{9,15},{10,... | collective-permute-start | bytes 4718600 | tf_op jit(solution)/shard_map/ppermute | solution.py:445
  44.3 3.3 %collective-permute-start.5 = (f16[768,256]{1,0:T(8,128)(2,1)S(1)}, f16[768,256]{1,0:T(8,128)(2,1)}, u32[]{:S(2)}, u32[]{:S(2)}) collective-permute-start(f16[768,256]{1,0:T(8,128)(2,1)S(1)} %fusion.7), channel_id=1, source_target_pairs={{0,64},{16,80},{32,96},{48,112},{64,0},{80,16},{96,32},{112,48},{1... | collective-permute-start | bytes 1179656 | tf_op jit(solution)/shard_map/ppermute | solution.py:444
  47.6 0.0 collective-permute-done.refs_2_
  47.6 0.0 collective-permute-done.6.refs_4_.refs_1_.refs_7_
  47.6 9.7 %forward.2.refs_5_ = bf16[512,512]{1,0:T(8,128)(2,1)} custom-call(s32[1]{0:T(128)} %bitcast.6.frag_ref, bf16[2,128,3072]{2,1,0:T(8,128)(2,1)} %norm.1.refs_0_, bf16[2,128,3072]{2,1,0:T(8,128)(2,1)} %copy-done.3, bf16[2,128,3072]{2,1,0:T(8,128)(2,1)} %collective-permute-done.refs_2_, bf16[2,128,3072]{2,1,0:T(8,128)(2,1)} %copy-done.1, ...), custom_call_target="tpu_custom_call" | custom-call | flops 1 | bytes 1 | tf_op jit(solution)/shard_map/forward/pallas_call | solution.py:181
  57.3 0.0 collective-permute-done.5
  57.3 1.1 %add_convert_fusion = f16[768,256]{1,0:T(8,128)(2,1)S(1)} fusion(f16[768,256]{1,0:T(8,128)(2,1)} %collective-permute-done.5, f16[768,256]{1,0:T(8,128)(2,1)S(1)} %fusion.7), kind=kLoop, calls=%fused_computation.17 | loop fusion | flops 786432 | bytes 1179648 | tf_op jit(solution)/shard_map/convert_element_type | solution.py:450
  58.4 1.3 %collective-permute-start.7 = (f16[768,256]{1,0:T(8,128)(2,1)S(1)}, f16[768,256]{1,0:T(8,128)(2,1)}, u32[]{:S(2)}, u32[]{:S(2)}) collective-permute-start(f16[768,256]{1,0:T(8,128)(2,1)S(1)} %add_convert_fusion), channel_id=1, source_target_pairs={{0,48},{1,17},{2,50},{3,19},{4,52},{5,21},{6,54},{7,23},{8,56},{9,... | collective-permute-start | bytes 1179656 | tf_op jit(solution)/shard_map/ppermute | solution.py:453
  59.7 1.8 %collective-permute-start.8 = (f16[768,256]{1,0:T(8,128)(2,1)S(1)}, f16[768,256]{1,0:T(8,128)(2,1)}, u32[]{:S(2)}, u32[]{:S(2)}) collective-permute-start(f16[768,256]{1,0:T(8,128)(2,1)S(1)} %add_convert_fusion), channel_id=1, source_target_pairs={{0,16},{1,49},{2,18},{3,51},{4,20},{5,53},{6,22},{7,55},{8,24},{9,... | collective-permute-start | bytes 1179656 | tf_op jit(solution)/shard_map/ppermute | solution.py:453
  61.5 0.6 collective-permute-start.9
  62.2 0.5 collective-permute-start.13
  62.6 0.0 collective-permute-done.11.refs_0_.refs_4_
  62.6 0.7 collective-permute-start.10
  63.4 5.5 %forward.3.refs_6_ = bf16[128,512]{1,0:T(8,128)(2,1)} custom-call(s32[1]{0:T(128)} %bitcast.6.frag_ref, bf16[2,128,3072]{2,1,0:T(8,128)(2,1)} %collective-permute-done.11.refs_0_.refs_4_, bf16[3,3072,256]{2,1,0:T(8,128)(2,1)} %collective-permute-done.6.refs_4_.refs_1_.refs_7_, bf16[3,3072,256]{2,1,0:T(8,128)(2,1)} %bitcast.21), custom_call_target="tpu_custom_call" | custom-call | flops 1 | bytes 1 | tf_op jit(solution)/shard_map/forward/pallas_call | solution.py:181
  68.9 0.0 copy-start.9
  68.9 0.0 collective-permute-done.7
  68.9 3.4 %collective-permute-start.12 = (bf16[2,128,3072]{2,1,0:T(8,128)(2,1)}, bf16[2,128,3072]{2,1,0:T(8,128)(2,1)S(1)}, u32[]{:S(2)}, u32[]{:S(2)}) collective-permute-start(bf16[2,128,3072]{2,1,0:T(8,128)(2,1)} %collective-permute-done.11.refs_0_.refs_4_), channel_id=1, source_target_pairs={{0,2},{1,7},{2,4},{3,1},{4,6},{5,3},{6,0},{7,5},{8,10},{9,15},{10,... | collective-permute-start | bytes 4718600 | tf_op jit(solution)/shard_map/ppermute | solution.py:456
  72.3 1.4 %maximum_select_fusion.1 = f16[1536,256]{1,0:T(8,128)(2,1)S(1)} fusion(f16[768,256]{1,0:T(8,128)(2,1)} %collective-permute-done.7, f16[768,256]{1,0:T(8,128)(2,1)S(1)} %add_convert_fusion, pred[]{:T(512)S(6)} %eq.14), kind=kLoop, calls=%fused_computation.6 | loop fusion | flops 1179648 | bytes 1572865 | tf_op jit(solution)/shard_map/jit(_where)/select_n | solution.py:424
  73.8 4.9 %collective-permute-done.8 = f16[768,256]{1,0:T(8,128)(2,1)} collective-permute-done((f16[768,256]{1,0:T(8,128)(2,1)S(1)}, f16[768,256]{1,0:T(8,128)(2,1)}, u32[]{:S(2)}, u32[]{:S(2)}) %collective-permute-start.8) | collective-permute-done | bytes 393248 | tf_op jit(solution)/shard_map/ppermute | solution.py:453
  78.7 0.9 collective-permute-done.9
  79.6 1.8 %maximum_select_fusion.2 = f16[1536,256]{1,0:T(8,128)(2,1)S(1)} fusion(f16[768,256]{1,0:T(8,128)(2,1)} %collective-permute-done.9, f16[768,256]{1,0:T(8,128)(2,1)} %collective-permute-done.8, pred[]{:T(512)S(6)} %eq.14), kind=kLoop, calls=%fused_computation.7 | loop fusion | flops 1179648 | bytes 1572865 | tf_op jit(solution)/shard_map/jit(_where)/select_n | solution.py:424
  81.4 0.0 slice-start.1
  81.4 0.0 copy-start
  81.5 5.4 %fusion = (f32[3072,256]{1,0:T(8,128)S(1)}, f32[3072,256]{1,0:T(8,128)}, f32[3072,256]{1,0:T(8,128)}) fusion(bf16[1,3,3072,256]{3,2,1,0:T(8,128)(2,1)} %param.13, s32[]{:T(128)S(6)} %select_n.71, f32[3072,256]{1,0:T(8,128)S(1)} %copy-done.9, f16[1536,256]{1,0:T(8,128)(2,1)S(1)} %maximum_select_fusion.1, f16[1536,256]{1,0:T(8,128)(2,1)S(1)} %maximum_select_fusion.2, ...), kind=kLoop, calls=%fused_computation.1 | loop fusion | flops 11010048 | bytes 18874372 | tf_op jit(solution)/shard_map/add | solution.py:461
  86.8 0.0 collective-permute-done.13.block
  86.9 8.2 %gradients.1 = (bf16[3,3072,256]{2,1,0:T(8,128)(2,1)S(1)}, bf16[3,3072,256]{2,1,0:T(8,128)(2,1)S(1)}, f32[256,3072]{1,0:T(8,128)S(1)}, f32[256,3072]{1,0:T(8,128)S(1)}) custom-call(s32[1]{0:T(128)} %bitcast.6.frag_ref, bf16[2,128,3072]{2,1,0:T(8,128)(2,1)S(1)} %collective-permute-done.13.block, bf16[2,128,3072]{2,1,0:T(8,128)(2,1)S(1)} %copy-done, ...), custom_call_target="tpu_custom_call" | custom-call | flops 1 | bytes 1 | tf_op jit(solution)/shard_map/gradients/pallas_call | solution.py:247
  95.1 1.7 %collective-permute-done.10.refs_0_.block.past = bf16[2,128,3072]{2,1,0:T(8,128)(2,1)S(1)} collective-permute-done((bf16[2,128,3072]{2,1,0:T(8,128)(2,1)}, bf16[2,128,3072]{2,1,0:T(8,128)(2,1)S(1)}, u32[]{:S(2)}, u32[]{:S(2)}) %collective-permute-start.10) | collective-permute-done | bytes 1572896 | tf_op jit(solution)/shard_map/ppermute | solution.py:452
  96.8 1.2 %right.1.past_right = bf16[128,256]{1,0:T(8,128)(2,1)S(1)} custom-call(s32[1]{0:T(128)} %bitcast.6.frag_ref, bf16[2,128,3072]{2,1,0:T(8,128)(2,1)S(1)} %collective-permute-done.10.refs_0_.block.past, bf16[3,3072,256]{2,1,0:T(8,128)(2,1)S(1)} %get-tuple-element.27.weight), custom_call_target="tpu_custom_call" | custom-call | flops 1610612736 | bytes 9437184 | tf_op jit(solution)/shard_map/right/pallas_call | solution.py:314
  98.0 0.8 collective-permute-done.12.refs_1_.block
  98.8 1.9 %last.1 = bf16[256,3072]{1,0:T(8,128)(2,1)S(1)} custom-call(s32[1]{0:T(128)} %bitcast.6.frag_ref, bf16[2,128,3072]{2,1,0:T(8,128)(2,1)S(1)} %collective-permute-done.12.refs_1_.block, bf16[2,128,3072]{2,1,0:T(8,128)(2,1)S(1)} %collective-permute-done.10.refs_0_.block.past, bf16[128,256]{1,0:T(8,128)(2,1)S(1)} %right.1.past_right, ...), custom_call_target="tpu_custom_call" | custom-call | flops 1 | bytes 1 | tf_op jit(solution)/shard_map/last/pallas_call | solution.py:348
  100.7 3.1 %collective-permute-start.14 = (bf16[256,3072]{1,0:T(8,128)(2,1)S(1)}, bf16[256,3072]{1,0:T(8,128)(2,1)S(1)}, u32[]{:S(2)}, u32[]{:S(2)}) collective-permute-start(bf16[256,3072]{1,0:T(8,128)(2,1)S(1)} %last.1), channel_id=1, source_target_pairs={{0,1},{1,0},{2,3},{3,2},{4,5},{5,4},{6,7},{7,6},{8,9},{9,8},{10,11... | collective-permute-start | bytes 4718600 | tf_op jit(solution)/shard_map/ppermute | solution.py:467
  103.8 2.9 %blocks.1.own_ref = f32[256,3072]{1,0:T(8,128)S(1)} custom-call(s32[1]{0:T(128)} %bitcast.6.frag_ref, bf16[2,128,3072]{2,1,0:T(8,128)(2,1)S(1)} %collective-permute-done.10.refs_0_.block.past, bf16[2,128,3072]{2,1,0:T(8,128)(2,1)S(1)} %collective-permute-done.12.refs_1_.block, ...), custom_call_target="tpu_custom_call", output_to_operand_aliasing={{}: (4, {})} | custom-call | flops 1 | bytes 1 | tf_op jit(solution)/shard_map/blocks/pallas_call | solution.py:288
  106.7 0.1 collective-permute-done.14.other_ref
  106.8 2.8 %adam.1 = bf16[3072,256]{1,0:T(8,128)(2,1)} custom-call(f32[256,3072]{1,0:T(8,128)S(1)} %blocks.1.own_ref, bf16[256,3072]{1,0:T(8,128)(2,1)S(1)} %collective-permute-done.14.other_ref, f32[3072,256]{1,0:T(8,128)S(1)} %bitcast.25, f32[3072,256]{1,0:T(8,128)S(1)} %bitcast.26, f32[3072,256]{1,0:T(8,128)S(1)} %get-tuple-element.29.mixed_ref), custom_call_target="tpu_custom_call" | custom-call | flops 1 | bytes 1 | tf_op jit(solution)/shard_map/adam/pallas_call | solution.py:380
  (22 shorter events, 0.0 us)
Async XLA Ops:
  0.6 47.0 %collective-permute-start.6 = (bf16[3,3072,256]{2,1,0:T(8,128)(2,1)}, bf16[3,3072,256]{2,1,0:T(8,128)(2,1)}, u32[]{:S(2)}, u32[]{:S(2)}) collective-permute-start(bf16[3,3072,256]{2,1,0:T(8,128)(2,1)} %bitcast.19), channel_id=1, source_target_pairs={{0,1},{1,0},{2,3},{3,2},{4,5},{5,4},{6,7},{7,6},{8,9},{9,8},{10,11... | collective-permute-start | bytes 14155784 | tf_op jit(solution)/shard_map/ppermute | solution.py:400
  4.7 36.9 %collective-permute-start.1 = (bf16[2,128,3072]{2,1,0:T(8,128)(2,1)}, bf16[2,128,3072]{2,1,0:T(8,128)(2,1)S(1)}, u32[]{:S(2)}, u32[]{:S(2)}) collective-permute-start(bf16[2,128,3072]{2,1,0:T(8,128)(2,1)} %norm.1.refs_0_), channel_id=1, source_target_pairs={{0,8},{1,9},{2,10},{3,11},{4,12},{5,13},{6,14},{7,15},{8,0},{9,1},... | collective-permute-start | bytes 4718600 | tf_op jit(solution)/shard_map/ppermute | solution.py:430
  6.5 35.1 %collective-permute-start.2 = (bf16[2,128,3072]{2,1,0:T(8,128)(2,1)}, bf16[2,128,3072]{2,1,0:T(8,128)(2,1)S(1)}, u32[]{:S(2)}, u32[]{:S(2)}) collective-permute-start(bf16[2,128,3072]{2,1,0:T(8,128)(2,1)} %norm.1.refs_0_), channel_id=1, source_target_pairs={{0,2},{1,7},{2,4},{3,1},{4,6},{5,3},{6,0},{7,5},{8,10},{9,15},{10,... | collective-permute-start | bytes 4718600 | tf_op jit(solution)/shard_map/ppermute | solution.py:429
  12.0 12.7 %collective-permute-start.3 = (bf16[1536,256]{1,0:T(8,128)(2,1)}, bf16[1536,256]{1,0:T(8,128)(2,1)}, u32[]{:S(2)}, u32[]{:S(2)}) collective-permute-start(bf16[1536,256]{1,0:T(8,128)(2,1)} %dynamic-slice_bitcast_fusion), channel_id=1, source_target_pairs={{0,16},{1,49},{2,18},{3,51},{4,20},{5,53},{6,22},{7,55},{8,24},{9,... | collective-permute-start | bytes 2359304 | tf_op jit(solution)/shard_map/ppermute | solution.py:432
  14.5 33.1 %collective-permute-start = (bf16[2,128,3072]{2,1,0:T(8,128)(2,1)}, bf16[2,128,3072]{2,1,0:T(8,128)(2,1)}, u32[]{:S(2)}, u32[]{:S(2)}) collective-permute-start(bf16[2,128,3072]{2,1,0:T(8,128)(2,1)} %norm.1.refs_0_), channel_id=1, source_target_pairs={{0,7},{1,2},{2,1},{3,4},{4,3},{5,6},{6,5},{7,0},{8,15},{9,10},{10,... | collective-permute-start | bytes 4718600 | tf_op jit(solution)/shard_map/ppermute | solution.py:431
  27.0 7.2 %collective-permute-start.4 = (f16[768,256]{1,0:T(8,128)(2,1)}, f16[768,256]{1,0:T(8,128)(2,1)S(1)}, u32[]{:S(2)}, u32[]{:S(2)}) collective-permute-start(f16[768,256]{1,0:T(8,128)(2,1)} %fusion.3), channel_id=1, source_target_pairs={{0,48},{1,17},{2,50},{3,19},{4,52},{5,21},{6,54},{7,23},{8,56},{9,... | collective-permute-start | bytes 1179656 | tf_op jit(solution)/shard_map/ppermute | solution.py:441
  41.6 6.0 %copy-start.1 = (bf16[2,128,3072]{2,1,0:T(8,128)(2,1)}, bf16[2,128,3072]{2,1,0:T(8,128)(2,1)S(1)}, u32[]{:S(2)}) copy-start(bf16[2,128,3072]{2,1,0:T(8,128)(2,1)S(1)} %collective-permute-done.1.refs_3_) | copy-start | bytes 4718596
  41.6 6.0 %copy-start.3 = (bf16[2,128,3072]{2,1,0:T(8,128)(2,1)}, bf16[2,128,3072]{2,1,0:T(8,128)(2,1)S(1)}, u32[]{:S(2)}) copy-start(bf16[2,128,3072]{2,1,0:T(8,128)(2,1)S(1)} %collective-permute-done.2.refs_1_) | copy-start | bytes 4718596
  41.6 21.1 %collective-permute-start.11 = (bf16[2,128,3072]{2,1,0:T(8,128)(2,1)S(1)}, bf16[2,128,3072]{2,1,0:T(8,128)(2,1)}, u32[]{:S(2)}, u32[]{:S(2)}) collective-permute-start(bf16[2,128,3072]{2,1,0:T(8,128)(2,1)S(1)} %collective-permute-done.1.refs_3_), channel_id=1, source_target_pairs={{0,2},{1,7},{2,4},{3,1},{4,6},{5,3},{6,0},{7,5},{8,10},{9,15},{10,... | collective-permute-start | bytes 4718600 | tf_op jit(solution)/shard_map/ppermute | solution.py:445
  44.3 13.0 %collective-permute-start.5 = (f16[768,256]{1,0:T(8,128)(2,1)S(1)}, f16[768,256]{1,0:T(8,128)(2,1)}, u32[]{:S(2)}, u32[]{:S(2)}) collective-permute-start(f16[768,256]{1,0:T(8,128)(2,1)S(1)} %fusion.7), channel_id=1, source_target_pairs={{0,64},{16,80},{32,96},{48,112},{64,0},{80,16},{96,32},{112,48},{1... | collective-permute-start | bytes 1179656 | tf_op jit(solution)/shard_map/ppermute | solution.py:444
  58.4 10.5 %collective-permute-start.7 = (f16[768,256]{1,0:T(8,128)(2,1)S(1)}, f16[768,256]{1,0:T(8,128)(2,1)}, u32[]{:S(2)}, u32[]{:S(2)}) collective-permute-start(f16[768,256]{1,0:T(8,128)(2,1)S(1)} %add_convert_fusion), channel_id=1, source_target_pairs={{0,48},{1,17},{2,50},{3,19},{4,52},{5,21},{6,54},{7,23},{8,56},{9,... | collective-permute-start | bytes 1179656 | tf_op jit(solution)/shard_map/ppermute | solution.py:453
  59.7 19.0 %collective-permute-start.8 = (f16[768,256]{1,0:T(8,128)(2,1)S(1)}, f16[768,256]{1,0:T(8,128)(2,1)}, u32[]{:S(2)}, u32[]{:S(2)}) collective-permute-start(f16[768,256]{1,0:T(8,128)(2,1)S(1)} %add_convert_fusion), channel_id=1, source_target_pairs={{0,16},{1,49},{2,18},{3,51},{4,20},{5,53},{6,22},{7,55},{8,24},{9,... | collective-permute-start | bytes 1179656 | tf_op jit(solution)/shard_map/ppermute | solution.py:453
  61.5 18.0 %collective-permute-start.9 = (f16[768,256]{1,0:T(8,128)(2,1)S(1)}, f16[768,256]{1,0:T(8,128)(2,1)}, u32[]{:S(2)}, u32[]{:S(2)}) collective-permute-start(f16[768,256]{1,0:T(8,128)(2,1)S(1)} %add_convert_fusion), channel_id=1, source_target_pairs={{0,32},{16,48},{32,0},{48,16},{64,96},{80,112},{96,64},{112,80},{1... | collective-permute-start | bytes 1179656 | tf_op jit(solution)/shard_map/ppermute | solution.py:454
  62.2 24.7 %collective-permute-start.13 = (bf16[2,128,3072]{2,1,0:T(8,128)(2,1)}, bf16[2,128,3072]{2,1,0:T(8,128)(2,1)S(1)}, u32[]{:S(2)}, u32[]{:S(2)}) collective-permute-start(bf16[2,128,3072]{2,1,0:T(8,128)(2,1)} %copy-done.3), channel_id=1, source_target_pairs={{0,2},{1,7},{2,4},{3,1},{4,6},{5,3},{6,0},{7,5},{8,10},{9,15},{10,... | collective-permute-start | bytes 4718600 | tf_op jit(solution)/shard_map/ppermute | solution.py:446
  62.6 34.1 %collective-permute-start.10 = (bf16[2,128,3072]{2,1,0:T(8,128)(2,1)}, bf16[2,128,3072]{2,1,0:T(8,128)(2,1)S(1)}, u32[]{:S(2)}, u32[]{:S(2)}) collective-permute-start(bf16[2,128,3072]{2,1,0:T(8,128)(2,1)} %collective-permute-done.refs_2_), channel_id=1, source_target_pairs={{0,8},{1,9},{2,10},{3,11},{4,12},{5,13},{6,14},{7,15},{8,0},{9,1},... | collective-permute-start | bytes 4718600 | tf_op jit(solution)/shard_map/ppermute | solution.py:452
  68.9 12.5 %copy-start.9 = (f32[3072,256]{1,0:T(8,128)S(1)}, f32[3072,256]{1,0:T(8,128)}, u32[]{:S(2)}) copy-start(f32[3072,256]{1,0:T(8,128)} %param.16) | copy-start | bytes 9437188
  68.9 29.9 %collective-permute-start.12 = (bf16[2,128,3072]{2,1,0:T(8,128)(2,1)}, bf16[2,128,3072]{2,1,0:T(8,128)(2,1)S(1)}, u32[]{:S(2)}, u32[]{:S(2)}) collective-permute-start(bf16[2,128,3072]{2,1,0:T(8,128)(2,1)} %collective-permute-done.11.refs_0_.refs_4_), channel_id=1, source_target_pairs={{0,2},{1,7},{2,4},{3,1},{4,6},{5,3},{6,0},{7,5},{8,10},{9,15},{10,... | collective-permute-start | bytes 4718600 | tf_op jit(solution)/shard_map/ppermute | solution.py:456
  79.6 7.3 %slice-start = ((s8[4718592]{0:T(1024)(128)(4,1)}), s8[4194304]{0:T(1024)(128)(4,1)S(1)}, s32[]{:S(2)}) async-start(s8[4718592]{0:T(1024)(128)(4,1)} %bitcast.22), calls=%async_computation | async-start | bytes 8388608
  81.4 5.4 %slice-start.1 = ((s8[4718592]{0:T(1024)(128)(4,1)}), s8[524288]{0:T(1024)(128)(4,1)S(1)}, s32[]{:S(2)}) async-start(s8[4718592]{0:T(1024)(128)(4,1)} %bitcast.22), calls=%async_computation.1 | async-start | bytes 1048576
  81.4 5.4 %copy-start = (bf16[2,128,3072]{2,1,0:T(8,128)(2,1)S(1)}, bf16[2,128,3072]{2,1,0:T(8,128)(2,1)}, u32[]{:S(2)}) copy-start(bf16[2,128,3072]{2,1,0:T(8,128)(2,1)} %norm.1.refs_0_) | copy-start | bytes 4718596
  81.4 5.4 %copy-start.2 = (bf16[2,128,3072]{2,1,0:T(8,128)(2,1)S(1)}, bf16[2,128,3072]{2,1,0:T(8,128)(2,1)}, u32[]{:S(2)}) copy-start(bf16[2,128,3072]{2,1,0:T(8,128)(2,1)} %copy-done.1) | copy-start | bytes 4718596
  81.5 5.4 %copy-start.4 = (bf16[2,128,3072]{2,1,0:T(8,128)(2,1)S(1)}, bf16[2,128,3072]{2,1,0:T(8,128)(2,1)}, u32[]{:S(2)}) copy-start(bf16[2,128,3072]{2,1,0:T(8,128)(2,1)} %copy-done.3) | copy-start | bytes 4718596
  81.5 5.4 %copy-start.7 = (bf16[512,512]{1,0:T(8,128)(2,1)S(1)}, bf16[512,512]{1,0:T(8,128)(2,1)}, u32[]{:S(2)}) copy-start(bf16[512,512]{1,0:T(8,128)(2,1)} %forward.2.refs_5_) | copy-start | bytes 1572868
  81.5 5.4 %copy-start.8 = (bf16[128,512]{1,0:T(8,128)(2,1)S(1)}, bf16[128,512]{1,0:T(8,128)(2,1)}, u32[]{:S(2)}) copy-start(bf16[128,512]{1,0:T(8,128)(2,1)} %forward.3.refs_6_) | copy-start | bytes 393220
  100.7 6.1 %collective-permute-start.14 = (bf16[256,3072]{1,0:T(8,128)(2,1)S(1)}, bf16[256,3072]{1,0:T(8,128)(2,1)S(1)}, u32[]{:S(2)}, u32[]{:S(2)}) collective-permute-start(bf16[256,3072]{1,0:T(8,128)(2,1)S(1)} %last.1), channel_id=1, source_target_pairs={{0,1},{1,0},{2,3},{3,2},{4,5},{5,4},{6,7},{7,6},{8,9},{9,8},{10,11... | collective-permute-start | bytes 4718600 | tf_op jit(solution)/shard_map/ppermute | solution.py:467
  103.8 3.0 %copy-start.5 = (f32[1,3072,256]{2,1,0:T(8,128)S(1)}, f32[1,3072,256]{2,1,0:T(8,128)}, u32[]{:S(2)}) copy-start(f32[1,3072,256]{2,1,0:T(8,128)} %param.14) | copy-start | bytes 9437188
  103.8 3.0 %copy-start.6 = (f32[1,3072,256]{2,1,0:T(8,128)S(1)}, f32[1,3072,256]{2,1,0:T(8,128)}, u32[]{:S(2)}) copy-start(f32[1,3072,256]{2,1,0:T(8,128)} %param.15) | copy-start | bytes 9437188
